TPU v7x, 32 devices: a whole 2x2x4 slice. The times are simulated.
32 devices in a mesh: seq: 8 (over z, y), fsdp: 4 (over x, core).
Axes of the slice: x: 2, y: 2, z: 4, core: 2. Of those that a mesh axis runs over, the one named last changes fastest.
Arguments:
- self_query: bfloat16 [4, 2048, 2048], P('fsdp', 'seq'), may hold values from -8 to 8, as said below
- self_key: bfloat16 [4, 2048, 2048], P('fsdp', 'seq'), may hold values from -8 to 8, as said below
- self_value: bfloat16 [4, 2048, 2048], P('fsdp', 'seq'), may hold values from -6 to 6
- cross_query: bfloat16 [4, 2048, 2048], P('fsdp', 'seq'), may hold values from -6 to 6
- neighbours: bfloat16 [4, 32, 256, 768], P('fsdp', 'seq'), may hold values from -6 to 6
- neighbour_count: int32 [4, 32], P('fsdp', 'seq'), may hold values from 1 to 2
- kv_weight: bfloat16 [768, 4096], P('fsdp'), may hold values from -0.21875 to 0.21875
- out_grad: bfloat16 [4, 2048, 2048], P('fsdp', 'seq'), may hold values from -6 to 6
Outputs:
- block_out: bfloat16 [4, 2048, 2048], P('fsdp', 'seq')
- query_grad: bfloat16 [4, 2048, 2048], P('fsdp', 'seq')
- key_grad: bfloat16 [4, 2048, 2048], P('fsdp', 'seq')
- value_grad: bfloat16 [4, 2048, 2048], P('fsdp', 'seq')
- cross_grad: bfloat16 [4, 2048, 2048], P('fsdp', 'seq')
- weight_grad: float32 [768, 4096], P(('seq', 'fsdp'))
Inputs may be any that keep to these rules, and one draw needn't show every extreme that they name: `self_query`: entries of order one. `self_key`: entries of order one.
All inputs are finite; a program needn't handle non-finite values.
Results may differ from a plain program's by a relative error of at most 0.014.
Values may be sent and summed in bfloat16 or wider, within the bound.
No kernel may reach another device: no remote copies, remote signals or barrier semaphores. Data moves between devices by JAX's collectives and lax.ppermute only.
A program may use at most 192 MiB of HBM per device.

v0:
```python
import jax
import jax.numpy as jnp
from jax import lax
from jax.sharding import PartitionSpec as P

HEADS = 16
HD = 128
GROUP = 64
RLEN = 128


neg_fill = -1e30


def from_behind(value, axis, steps):
    count = lax.axis_size(axis)
    first, last = (max(0, -steps), min(count, count - steps))
    return lax.ppermute(value, axis, [(source, source + steps) for source in range(first, last)])


def attend(queries, keys_in, values_in, grads, allowed, scaling):
    scores = (
        jnp.einsum("...qhd,...khd->...hqk", queries, keys_in, preferred_element_type=jnp.float32)
        * scaling
    )
    scores = jnp.where(allowed, scores, neg_fill)
    peaks = jnp.max(scores, axis=-1, keepdims=True)
    weights = jnp.exp(scores - peaks)
    probs = weights / jnp.sum(weights, axis=-1, keepdims=True)
    probs_low = probs.astype(jnp.bfloat16)
    output = jnp.einsum(
        "...hqk,...khd->...qhd", probs_low, values_in, preferred_element_type=jnp.float32
    )
    prob_grad = jnp.einsum(
        "...qhd,...khd->...hqk", grads, values_in, preferred_element_type=jnp.float32
    )
    row_delta = jnp.sum(probs * prob_grad, axis=-1, keepdims=True)
    score_grad = (probs * (prob_grad - row_delta) * scaling).astype(jnp.bfloat16)
    query_grad = jnp.einsum(
        "...hqk,...khd->...qhd", score_grad, keys_in, preferred_element_type=jnp.float32
    )
    key_grad = jnp.einsum(
        "...hqk,...qhd->...khd", score_grad, queries, preferred_element_type=jnp.float32
    )
    value_grad = jnp.einsum(
        "...hqk,...qhd->...khd", probs_low, grads, preferred_element_type=jnp.float32
    )
    return (output, query_grad, key_grad, value_grad)


def on_device(
    self_query, self_key, self_value, cross_query, neighbours, neighbour_count, kv_weight, out_grad
):
    tok_rows = self_query.shape[1]
    feature_width = self_query.shape[2]
    scaling = HD ** (-0.5)
    is_first = lax.axis_index("seq") == 0

    def head_view(array):
        return array.reshape(array.shape[:-1] + (HEADS, HD))

    prev_key, prev_value = from_behind((self_key, self_value), "seq", 1)
    all_keys = jnp.concatenate([prev_key[0], self_key[0]], 0)
    all_values = jnp.concatenate([prev_value[0], self_value[0]], 0)
    row_index = jnp.arange(tok_rows, dtype=jnp.int32)[:, None]
    col_index = jnp.arange(2 * tok_rows, dtype=jnp.int32)[None, :]
    self_allowed = (
        (col_index > row_index)
        & (col_index <= row_index + tok_rows)
        & ((col_index >= tok_rows) | jnp.logical_not(is_first))
    )
    self_out, self_qgrad, self_kterms, self_vterms = attend(
        head_view(self_query[0]),
        head_view(all_keys),
        head_view(all_values),
        head_view(out_grad[0]),
        self_allowed[None],
        scaling,
    )
    self_kterms = self_kterms.reshape(2 * tok_rows, feature_width)
    self_vterms = self_vterms.reshape(2 * tok_rows, feature_width)
    returned_key, returned_value = (
        from_behind(self_kterms[:tok_rows].astype(jnp.bfloat16), "seq", -1).astype(jnp.float32),
        from_behind(self_vterms[:tok_rows].astype(jnp.bfloat16), "seq", -1).astype(jnp.float32),
    )
    key_grad = (self_kterms[tok_rows:] + returned_key).astype(jnp.bfloat16)
    value_grad = (self_vterms[tok_rows:] + returned_value).astype(jnp.bfloat16)
    groups = tok_rows // GROUP
    encodings = neighbours[0]
    neigh_rows = encodings.shape[1]
    enc_width = encodings.shape[2]
    counts = neighbour_count[0].astype(jnp.bfloat16)
    rows_in = encodings.reshape(groups * neigh_rows, enc_width)
    columns = rows_in
    own_proj = (
        jnp.dot(
            columns,
            lax.all_gather(kv_weight, "fsdp", axis=0, tiled=True),
            preferred_element_type=jnp.float32,
        )
        .astype(jnp.bfloat16)
        .reshape(groups, neigh_rows, 2 * feature_width)
    )
    last_proj, last_count = from_behind((own_proj[groups - 1], counts[groups - 1 :]), "seq", 1)
    kv_proj = jnp.concatenate([last_proj[None], own_proj[: groups - 1]], 0)
    used_count = jnp.concatenate([last_count, counts[: groups - 1]], 0).astype(jnp.float32)
    neighbour_of = (jnp.arange(neigh_rows, dtype=jnp.int32) // RLEN).astype(jnp.float32)
    cross_allowed = (neighbour_of[None, :] < used_count[:, None])[:, None, None, :]
    group_keys = kv_proj[..., :feature_width].reshape(groups, neigh_rows, HEADS, HD)
    group_values = kv_proj[..., feature_width:].reshape(groups, neigh_rows, HEADS, HD)
    group_view = (groups, GROUP, HEADS, HD)
    cross_out, cross_qgrad, cross_kgrad, cross_vgrad = attend(
        cross_query[0].reshape(group_view),
        group_keys,
        group_values,
        out_grad[0].reshape(group_view),
        cross_allowed,
        scaling,
    )
    group_live = (jnp.arange(groups, dtype=jnp.int32) > 0) | jnp.logical_not(is_first)
    live_rows = group_live[:, None, None, None]
    cross_out = jnp.where(live_rows, cross_out, 0.0)
    cross_qgrad = jnp.where(live_rows, cross_qgrad, 0.0)
    kv_grad = jnp.concatenate(
        [
            cross_kgrad.reshape(groups, neigh_rows, feature_width),
            cross_vgrad.reshape(groups, neigh_rows, feature_width),
        ],
        -1,
    )
    kv_grad = jnp.where(group_live[:, None, None], kv_grad, 0.0).astype(jnp.bfloat16)
    returned_kv = from_behind(kv_grad[0], "seq", -1)
    grad_rows = encodings.reshape(groups * neigh_rows, enc_width)
    grad_kv = jnp.concatenate([kv_grad[1:], returned_kv[None]], 0).reshape(
        groups * neigh_rows, 2 * feature_width
    )
    columns = grad_rows
    weight_grad = lax.psum_scatter(
        jnp.einsum("re,rc->ec", columns, grad_kv, preferred_element_type=jnp.float32),
        ("seq", "fsdp"),
        scatter_dimension=0,
        tiled=True,
    )
    block_out = (
        self_out.reshape(tok_rows, feature_width) + cross_out.reshape(tok_rows, feature_width)
    ).astype(jnp.bfloat16)
    query_grad = self_qgrad.reshape(tok_rows, feature_width).astype(jnp.bfloat16)
    cross_grad = cross_qgrad.reshape(tok_rows, feature_width).astype(jnp.bfloat16)
    return (
        block_out[None],
        query_grad[None],
        key_grad[None],
        value_grad[None],
        cross_grad[None],
        weight_grad,
    )


def solution(mesh):
    in_specs = (
        P("fsdp", "seq", None),
        P("fsdp", "seq", None),
        P("fsdp", "seq", None),
        P("fsdp", "seq", None),
        P("fsdp", "seq", None, None),
        P("fsdp", "seq"),
        P("fsdp", None),
        P("fsdp", "seq", None),
    )
    out_specs = (
        P("fsdp", "seq", None),
        P("fsdp", "seq", None),
        P("fsdp", "seq", None),
        P("fsdp", "seq", None),
        P("fsdp", "seq", None),
        P(("seq", "fsdp"), None),
    )
    return jax.shard_map(
        on_device, mesh=mesh, in_specs=in_specs, out_specs=out_specs, check_vma=False
    )
```

profile of v0, /device:TPU:0, one launch (start us, length us, event | category | flops | bytes accessed | tf_op | source)
XLA Modules:
  0.0 493.9 jit_solution(13976105789968973370)
XLA Ops:
  8.0 50.7 %all-gather.2.cloned.1.call-done = bf16[768,4096]{1,0:T(8,128)(2,1)} async-done(((bf16[192,4096]{1,0:T(8,128)(2,1)}), bf16[768,4096]{1,0:T(8,128)(2,1)}) %all-gather.2.cloned.1.call-update) | async-done | bytes 6291472 | tf_op jit(solution)/shard_map/all_gather | solution.py:98
  58.7 9.9 %convolution_convert_fusion = bf16[1024,4096]{1,0:T(8,128)(2,1)S(1)} fusion(bf16[1024,768]{1,0:T(8,128)(2,1)S(1)} %bitcast.153, bf16[768,4096]{1,0:T(8,128)(2,1)} %all-gather.2.cloned.1.call-done), kind=kOutput, calls=%fused_computation.17 | convolution fusion | flops 6446645248 | bytes 16252928 | tf_op jit(solution)/shard_map/dot_general | solution.py:96
  85.4 37.0 %collective-permute-done.3 = bf16[1]{0:T(256)(128)(2,1)} collective-permute-done((bf16[1]{0:T(256)(128)(2,1)}, bf16[1]{0:T(256)(128)(2,1)}, u32[]{:S(2)}, u32[]{:S(2)}) %collective-permute-start.3) | collective-permute-done | bytes 34 | tf_op jit(solution)/shard_map/ppermute | solution.py:18
  123.1 6.3 %slice.74 = bf16[768,4096]{1,0:T(8,128)(2,1)} slice(bf16[1024,4096]{1,0:T(8,128)(2,1)} %copy-done.5), slice={[0:768], [0:4096]} | slice | bytes 12582912 | tf_op jit(solution)/shard_map/slice | solution.py:105
  129.4 8.6 %copy.83 = bf16[3,256,4096]{1,2,0:T(8,128)(2,1)} copy(bf16[3,256,4096]{2,1,0:T(8,128)(2,1)} %bitcast.155) | data formatting | bytes 12582912 | tf_op jit(solution)/shard_map/slice | solution.py:105
  158.3 30.6 %fusion.31 = bf16[4,16,256,128]{2,3,1,0:T(8,128)(2,1)} fusion(f32[4,16,256,64]{2,3,1,0:T(8,128)} %fusion.43, bf16[4,64,16,128]{3,2,1,0:T(8,128)(2,1)S(1)} %bitcast.164, f32[4,16,64,256]{3,2,1,0:T(8,128)} %copy-done.19, f32[4,16,64]{2,1,0:T(8,128)S(1)} %get-tuple-element.28), kind=kOutput, calls=%fused_computation.58 | convolution fusion | flops 275779840 | bytes 13647872 | tf_op jit(solution)/shard_map/...hqk,...qhd->...khd/dot_general | solution.py:42
  188.9 6.3 %copy.108 = bf16[4,256,2048]{2,1,0:T(8,128)(2,1)} copy(bf16[4,256,2048]{1,2,0:T(8,128)(2,1)} %bitcast.167) | data formatting | bytes 8388608 | tf_op jit(solution)/shard_map/reshape | solution.py:127
  195.2 6.3 %copy.107 = bf16[4,256,2048]{2,1,0:T(8,128)(2,1)} copy(bf16[4,256,2048]{1,2,0:T(8,128)(2,1)} %bitcast.168) | data formatting | bytes 8388608 | tf_op jit(solution)/shard_map/reshape | solution.py:126
  201.5 4.9 fusion.4
  211.2 45.0 %collective-permute-done.6 = bf16[256,4096]{1,0:T(8,128)(2,1)S(1)} collective-permute-done((bf16[256,4096]{1,0:T(8,128)(2,1)S(1)}, bf16[256,4096]{1,0:T(8,128)(2,1)S(1)}, u32[]{:S(2)}, u32[]{:S(2)}) %collective-permute-start.6) | collective-permute-done | bytes 2097184 | tf_op jit(solution)/shard_map/ppermute | solution.py:18
  256.2 6.7 %pad_maximum_fusion = bf16[4,256,4096]{2,1,0:T(8,128)(2,1)} fusion(bf16[1,256,4096]{2,1,0:T(8,128)(2,1)S(1)} %bitcast.182, bf16[3,256,4096]{2,1,0:T(8,128)(2,1)} %slice.81), kind=kLoop, calls=%fused_computation.8 | loop fusion | flops 4194304 | bytes 16777216 | tf_op jit(solution)/shard_map/concatenate | solution.py:134
  262.9 12.9 %convolution_bitcast_fusion = f32[768,4096]{0,1:T(8,128)} fusion(bf16[1024,4096]{1,0:T(8,128)(2,1)} %bitcast.160, bf16[1024,768]{1,0:T(8,128)(2,1)S(1)} %bitcast.154), kind=kOutput, calls=%fused_computation.16 | convolution fusion | flops 6442450944 | bytes 22544384 | tf_op jit(solution)/shard_map/re,rc->ec/dot_general | solution.py:139
  275.8 12.7 %copy.121 = f32[768,4096]{1,0:T(8,128)} copy(f32[768,4096]{0,1:T(8,128)} %convolution_bitcast_fusion) | data formatting | bytes 25165824
  290.1 5.5 %collective-permute-start.1 = (bf16[1,256,2048]{1,2,0:T(8,128)(2,1)S(1)}, bf16[1,256,2048]{1,2,0:T(8,128)(2,1)}, u32[]{:S(2)}, u32[]{:S(2)}) collective-permute-start(bf16[1,256,2048]{1,2,0:T(8,128)(2,1)S(1)} %copy.76), channel_id=1, source_target_pairs={{0,4},{4,8},{8,12},{12,16},{16,20},{20,24},{24,28},{1,5},{5,9},{9,... | collective-permute-start | bytes 3145736 | tf_op jit(solution)/shard_map/ppermute | solution.py:18
  306.1 12.1 %collective-permute-done.1 = bf16[1,256,2048]{1,2,0:T(8,128)(2,1)} collective-permute-done((bf16[1,256,2048]{1,2,0:T(8,128)(2,1)S(1)}, bf16[1,256,2048]{1,2,0:T(8,128)(2,1)}, u32[]{:S(2)}, u32[]{:S(2)}) %collective-permute-start.1) | collective-permute-done | bytes 1048608 | tf_op jit(solution)/shard_map/ppermute | solution.py:18
  322.8 5.5 %fusion.68 = (f32[16,256]{1,0:T(8,128)S(1)}, f32[16,256,512]{1,2,0:T(8,128)}) fusion(f32[16,512,256]{2,1,0:T(8,128)S(1)} %fusion.34, pred[256,512]{0,1:T(8,128)(4,1)S(1)} %fusion.49), kind=kOutput, calls=%fused_computation.107 | output fusion | flops 12583423 | bytes 16924672 | tf_op jit(solution)/shard_map/sub | solution.py:28
  328.3 5.4 %convolution_bitcast_fusion.1 = f32[512,16,128]{0,2,1:T(8,128)S(1)} fusion(bf16[256,16,128]{0,2,1:T(8,128)(2,1)S(1)} %bitcast.176, f32[16,256,512]{1,2,0:T(8,128)} %get-tuple-element.27, f32[16,256]{1,0:T(8,128)S(1)} %get-tuple-element.26), kind=kOutput, calls=%fused_computation.39 | convolution fusion | flops 541065216 | bytes 13647872 | tf_op jit(solution)/shard_map/...hqk,...qhd->...khd/dot_general | solution.py:45
  340.6 6.8 %fusion.35 = f32[16,512,256]{2,1,0:T(8,128)} fusion(bf16[256,16,128]{0,2,1:T(8,128)(2,1)} %bitcast.175, bf16[256,16,128]{0,2,1:T(8,128)(2,1)S(1)} %bitcast.173, bf16[256,16,128]{0,2,1:T(8,128)(2,1)} %bitcast.179), kind=kOutput, calls=%fused_computation.62 | convolution fusion | flops 541065216 | bytes 11534336 | tf_op jit(solution)/shard_map/...qhd,...khd->...hqk/dot_general | solution.py:34
  347.3 14.5 %fusion.23 = f32[512,16,128]{0,2,1:T(8,128)} fusion(bf16[256,16,128]{0,2,1:T(8,128)(2,1)S(1)} %bitcast.178, f32[16,512,256]{2,1,0:T(8,128)} %fusion.35, f32[16,256,512]{1,2,0:T(8,128)} %get-tuple-element.27, f32[16,256]{1,0:T(8,128)S(1)} %get-tuple-element.26), kind=kOutput, calls=%fused_computation.38 | convolution fusion | flops 551555584 | bytes 22036480 | tf_op jit(solution)/shard_map/...hqk,...qhd->...khd/dot_general | solution.py:42
  368.2 6.1 %fusion.27 = f32[16,128,256]{2,1,0:T(8,128)} fusion(bf16[256,16,128]{0,2,1:T(8,128)(2,1)S(1)} %bitcast.174, bf16[256,16,128]{0,2,1:T(8,128)(2,1)} %bitcast.180, f32[16,256,512]{1,2,0:T(8,128)} %get-tuple-element.27, f32[16,256]{1,0:T(8,128)S(1)} %get-tuple-element.26), kind=kOutput, calls=%fused_computation.54 | convolution fusion | flops 545259520 | bytes 12599296 | tf_op jit(solution)/shard_map/...hqk,...khd->...qhd/dot_general | solution.py:31
  377.4 14.2 %fusion.33 = bf16[16,128,256]{2,1,0:T(8,128)(2,1)} fusion(f32[16,512,256]{2,1,0:T(8,128)} %fusion.35, bf16[256,16,128]{2,0,1:T(8,128)(2,1)S(1)} %copy-done.9, bf16[256,16,128]{2,0,1:T(8,128)(2,1)S(1)} %copy-done.12, f32[16,256,512]{1,2,0:T(8,128)} %get-tuple-element.27, f32[16,256]{1,0:T(8,128)S(1)} %get-tuple-element.26), kind=kOutput, calls=%fused_computation.60 | convolution fusion | flops 556274176 | bytes 19939328 | tf_op jit(solution)/shard_map/...hqk,...khd->...qhd/dot_general | solution.py:39
  408.3 16.1 %collective-permute-done.5 = bf16[256,2048]{1,0:T(8,128)(2,1)} collective-permute-done((bf16[256,2048]{1,0:T(8,128)(2,1)}, bf16[256,2048]{1,0:T(8,128)(2,1)}, u32[]{:S(2)}, u32[]{:S(2)}) %collective-permute-start.5) | collective-permute-done | bytes 1048608 | tf_op jit(solution)/shard_map/ppermute | solution.py:18
  434.5 30.4 %fusion.36 = bf16[4,64,16,128]{3,1,2,0:T(8,128)(2,1)} fusion(bf16[4,256,16,128]{1,3,2,0:T(8,128)(2,1)} %bitcast.157, f32[4,16,256,64]{2,3,1,0:T(8,128)} %fusion.43, pred[4]{0:T(512)(128)(4,1)S(1)} %compare_or_fusion, f32[4,16,64,256]{3,2,1,0:T(8,128)} %copy-done.19, f32[4,16,64]{2,1,0:T(8,128)S(1)} %get-tuple-element.28), kind=kOutput, calls=%fused_computation.63 | convolution fusion | flops 276828416 | bytes 13647876 | tf_op jit(solution)/shard_map/...hqk,...khd->...qhd/dot_general | solution.py:39
  471.7 14.9 %reduce-scatter.4.cloned.1.call-done = f32[24,4096]{1,0:T(8,128)} async-done(((f32[768,4096]{1,0:T(8,128)}), f32[24,4096]{1,0:T(8,128)}) %reduce-scatter.4.cloned.1.call-update) | async-done | bytes 393232
  (102 shorter events, 109.8 us)
Async XLA Ops:
  7.2 51.5 %copy-start = (bf16[1,4,256,768]{3,2,1,0:T(8,128)(2,1)S(1)}, bf16[1,4,256,768]{3,2,1,0:T(8,128)(2,1)}, u32[]{:S(2)}) copy-start(bf16[1,4,256,768]{3,2,1,0:T(8,128)(2,1)} %param.12) | copy-start | bytes 4718596
  7.2 51.5 %all-gather.2.cloned.1.call-start = ((), (), s32[]{:S(2)}) async-start(), calls=%async_computation.1 | async-start | bytes 7864320 | tf_op jit(solution)/shard_map/all_gather | solution.py:98
  7.9 478.7 %reduce-scatter.4.cloned.1.call-start = ((), (), s32[]{:S(2)}) async-start(), calls=%async_computation.2 | async-start | bytes 12976128
  71.8 6.2 %copy-start.18 = (s32[1,4]{1,0:T(1,128)S(1)}, s32[1,4]{1,0:T(1,128)}, u32[]{:S(2)}) copy-start(s32[1,4]{1,0:T(1,128)} %param.13) | copy-start | bytes 52
  73.4 64.6 %collective-permute-start.2 = (bf16[256,4096]{1,0:T(8,128)(2,1)}, bf16[256,4096]{1,0:T(8,128)(2,1)}, u32[]{:S(2)}, u32[]{:S(2)}) collective-permute-start(bf16[256,4096]{1,0:T(8,128)(2,1)} %slice.73), channel_id=1, source_target_pairs={{0,4},{4,8},{8,12},{12,16},{16,20},{20,24},{24,28},{1,5},{5,9},{9,... | collective-permute-start | bytes 6291464 | tf_op jit(solution)/shard_map/ppermute | solution.py:18
  78.6 43.7 %collective-permute-start.3 = (bf16[1]{0:T(256)(128)(2,1)}, bf16[1]{0:T(256)(128)(2,1)}, u32[]{:S(2)}, u32[]{:S(2)}) collective-permute-start(bf16[1]{0:T(256)(128)(2,1)} %bitcast.11), channel_id=1, source_target_pairs={{0,4},{4,8},{8,12},{12,16},{16,20},{20,24},{24,28},{1,5},{5,9},{9,... | collective-permute-start | bytes 14 | tf_op jit(solution)/shard_map/ppermute | solution.py:18
  142.2 4.0 copy-start.6
  146.2 3.2 copy-start.3
  146.2 4.6 copy-start.2
  206.6 49.6 %collective-permute-start.6 = (bf16[256,4096]{1,0:T(8,128)(2,1)S(1)}, bf16[256,4096]{1,0:T(8,128)(2,1)S(1)}, u32[]{:S(2)}, u32[]{:S(2)}) collective-permute-start(bf16[256,4096]{1,0:T(8,128)(2,1)S(1)} %slice_bitcast_fusion), channel_id=1, source_target_pairs={{4,0},{8,4},{12,8},{16,12},{20,16},{24,20},{28,24},{5,1},{9,5},{13... | collective-permute-start | bytes 6291464 | tf_op jit(solution)/shard_map/ppermute | solution.py:18
  288.5 12.8 %copy-start.7 = (bf16[1,256,2048]{2,1,0:T(8,128)(2,1)S(1)}, bf16[1,256,2048]{2,1,0:T(8,128)(2,1)}, u32[]{:S(2)}) copy-start(bf16[1,256,2048]{2,1,0:T(8,128)(2,1)} %param.15) | copy-start | bytes 3145732
  290.1 28.1 %collective-permute-start.1 = (bf16[1,256,2048]{1,2,0:T(8,128)(2,1)S(1)}, bf16[1,256,2048]{1,2,0:T(8,128)(2,1)}, u32[]{:S(2)}, u32[]{:S(2)}) collective-permute-start(bf16[1,256,2048]{1,2,0:T(8,128)(2,1)S(1)} %copy.76), channel_id=1, source_target_pairs={{0,4},{4,8},{8,12},{12,16},{16,20},{20,24},{24,28},{1,5},{5,9},{9,... | collective-permute-start | bytes 3145736 | tf_op jit(solution)/shard_map/ppermute | solution.py:18
  295.6 42.7 %collective-permute-start = (bf16[1,256,2048]{2,1,0:T(8,128)(2,1)}, bf16[1,256,2048]{2,1,0:T(8,128)(2,1)}, u32[]{:S(2)}, u32[]{:S(2)}) collective-permute-start(bf16[1,256,2048]{2,1,0:T(8,128)(2,1)} %param.10), channel_id=1, source_target_pairs={{0,4},{4,8},{8,12},{12,16},{16,20},{20,24},{24,28},{1,5},{5,9},{9,... | collective-permute-start | bytes 3145736 | tf_op jit(solution)/shard_map/ppermute | solution.py:18
  303.3 19.5 %copy-start.8 = (bf16[256,16,128]{2,0,1:T(8,128)(2,1)}, bf16[256,16,128]{2,0,1:T(8,128)(2,1)S(1)}, u32[]{:S(2)}) copy-start(bf16[256,16,128]{2,0,1:T(8,128)(2,1)S(1)} %copy.79) | copy-start | bytes 3145732
  322.8 5.5 %copy-start.13 = (bf16[1,256,2048]{1,2,0:T(8,128)(2,1)S(1)}, bf16[1,256,2048]{1,2,0:T(8,128)(2,1)}, u32[]{:S(2)}) copy-start(bf16[1,256,2048]{1,2,0:T(8,128)(2,1)} %copy.124) | copy-start | bytes 3145732
  335.7 4.9 copy-start.10
  340.6 6.8 %copy-start.14 = (bf16[1,256,2048]{1,2,0:T(8,128)(2,1)S(1)}, bf16[1,256,2048]{1,2,0:T(8,128)(2,1)}, u32[]{:S(2)}) copy-start(bf16[1,256,2048]{1,2,0:T(8,128)(2,1)} %copy.123) | copy-start | bytes 3145732
  365.1 9.2 %copy-start.16 = (f32[512,16,128]{0,2,1:T(8,128)S(1)}, f32[512,16,128]{0,2,1:T(8,128)}, u32[]{:S(2)}) copy-start(f32[512,16,128]{0,2,1:T(8,128)} %copy-done.15) | copy-start | bytes 12582916
  365.1 39.9 %collective-permute-start.4 = (bf16[256,2048]{1,0:T(8,128)(2,1)}, bf16[256,2048]{1,0:T(8,128)(2,1)}, u32[]{:S(2)}, u32[]{:S(2)}) collective-permute-start(bf16[256,2048]{1,0:T(8,128)(2,1)} %copy.95), channel_id=1, source_target_pairs={{4,0},{8,4},{12,8},{16,12},{20,16},{24,20},{28,24},{5,1},{9,5},{13... | collective-permute-start | bytes 3145736 | tf_op jit(solution)/shard_map/ppermute | solution.py:18
  366.6 57.7 %collective-permute-start.5 = (bf16[256,2048]{1,0:T(8,128)(2,1)}, bf16[256,2048]{1,0:T(8,128)(2,1)}, u32[]{:S(2)}, u32[]{:S(2)}) collective-permute-start(bf16[256,2048]{1,0:T(8,128)(2,1)} %copy.99), channel_id=1, source_target_pairs={{4,0},{8,4},{12,8},{16,12},{20,16},{24,20},{28,24},{5,1},{9,5},{13... | collective-permute-start | bytes 3145736 | tf_op jit(solution)/shard_map/ppermute | solution.py:18
  368.2 7.7 %copy-start.17 = (f32[512,16,128]{0,2,1:T(8,128)S(1)}, f32[512,16,128]{0,2,1:T(8,128)}, u32[]{:S(2)}) copy-start(f32[512,16,128]{0,2,1:T(8,128)} %fusion.23) | copy-start | bytes 12582916
  402.6 24.8 %copy-start.4 = (bf16[4,256,2048]{1,2,0:T(8,128)(2,1)S(1)}, bf16[4,256,2048]{1,2,0:T(8,128)(2,1)}, u32[]{:S(2)}) copy-start(bf16[4,256,2048]{1,2,0:T(8,128)(2,1)} %copy-done.3) | copy-start | bytes 12582916
  402.6 24.8 %copy-start.20 = (f32[4,16,64,256]{3,2,1,0:T(8,128)S(1)}, f32[4,16,64,256]{3,2,1,0:T(8,128)}, u32[]{:S(2)}) copy-start(f32[4,16,64,256]{3,2,1,0:T(8,128)} %copy-done.19) | copy-start | bytes 12582916
  464.9 21.7 %copy-start.1 = (bf16[1,4,256,768]{3,2,1,0:T(8,128)(2,1)S(1)}, bf16[1,4,256,768]{3,2,1,0:T(8,128)(2,1)}, u32[]{:S(2)}) copy-start(bf16[1,4,256,768]{3,2,1,0:T(8,128)(2,1)} %param.12) | copy-start | bytes 4718596
  (6 other events, 16.4 us)
Sparse Core Ops, SparseCore 0:
  9.6 49.0 all-gather.1
  288.6 197.9 reduce-scatter.3
where the time goes:
time: 498 us; the launch traced here: 494 us
  waiting for transfers between devices  180 us (36%)
  matrix products  142 us (29%)
  local copies, waits for them, and re-layouts  102 us (20%)
  other arithmetic  33.7 us (7%)
  starting transfers between devices  21.1 us (4%)
  between operations  14.8 us (3%)
    ppermute x7, waiting for transfers between devices, from_behind(): lax.ppermute(value, axis, [(source, source + steps) for source in range(f...  114 us
    all_gather x1, waiting for transfers between devices, on_device(): lax.all_gather(kv_weight, 'fsdp', axis=0, tiled=True)  50.7 us
    dot_general x2, matrix products, attend(): jnp.einsum('...hqk,...qhd->...khd', score_grad, queries, preferred_elemen...  45.1 us
    dot_general x2, matrix products, attend(): jnp.einsum('...hqk,...khd->...qhd', score_grad, keys_in, preferred_elemen...  44.6 us
    unnamed x48, local copies, waits for them, and re-layouts  31.3 us
    ppermute x7, starting transfers between devices, from_behind(): lax.ppermute(value, axis, [(source, source + steps) for source in range(f...  21 us
    unnamed x3, waiting for transfers between devices  15.6 us
    slice x2, local copies, waits for them, and re-layouts, on_device(): kv_proj = jnp.concatenate([last_proj[None], own_proj[:groups - 1]], 0)  14.9 us
  transfers between devices with their start and end apart: 9, of which 8 were waited for; matrix products, arithmetic and copies ran while one was open for 33% of the time, Pallas kernels for 0%

commit v1 on v0

v1 whole, which is shorter than its diff:
```python
import functools

import numpy as np
import jax
import jax.numpy as jnp
from jax import lax
from jax.experimental import pallas as pl
from jax.experimental.pallas import tpu as pltpu
from jax.sharding import PartitionSpec as P

HEADS = 16
HD = 128
GROUP = 64
RLEN = 128
PAIR = 2 * HD
CHUNKS = 4
SCALE = HD ** (-0.5)
LOG2E = 1.4426950408889634
NEG = -1e30
BF = jnp.bfloat16
F32 = jnp.float32

NT = (((1,), (1,)), ((), ()))
TN = (((0,), (0,)), ((), ()))
NN = (((1,), (0,)), ((), ()))


def mm(a, b, dims):
    return lax.dot_general(a, b, dims, preferred_element_type=F32)


def shift(value, axis, steps):
    count = lax.axis_size(axis)
    first, last = max(0, -steps), min(count, count - steps)
    return lax.ppermute(value, axis, [(i, i + steps) for i in range(first, last)])


def swap(value, axis, bit):
    return lax.ppermute(value, axis, [(i, i ^ bit) for i in range(lax.axis_size(axis))])


def cross_kernel(
    pieces, groups, info_ref, count_ref, nb_ref, nbt_ref, *refs
):
    weights, refs = refs[: 2 * pieces], refs[2 * pieces :]
    cq_ref, do_ref, out_ref, dq_ref, keep_ref, send_ref, w_ref, kv_ref, dkv_ref = refs
    shard = info_ref[0]
    rows = weights[0].shape[0]
    for piece in range(pieces):
        at = pl.ds(pl.multiple_of((shard ^ piece) * rows, 16), rows)
        w_ref[at, :PAIR] = weights[2 * piece][...]
        w_ref[at, PAIR:] = weights[2 * piece + 1][...]
    kv_ref[...] = mm(nb_ref[...], w_ref[...], NN).astype(BF)
    per = 2 * RLEN
    zero = jnp.zeros((GROUP, HD), BF)

    def diagonal(ref, u):
        block = ref[u * GROUP : (u + 1) * GROUP, :]
        return jnp.concatenate(
            [
                jnp.concatenate([block[:, :HD], zero], 1),
                jnp.concatenate([zero, block[:, HD:]], 1),
            ],
            0,
        )

    for u in range(groups):
        count = count_ref[u]
        at = slice(u * per, (u + 1) * per)
        keys, values = kv_ref[at, :PAIR], kv_ref[at, PAIR:]
        queries, grads = diagonal(cq_ref, u), diagonal(do_ref, u)
        scores = mm(keys, queries, NT)
        prob_grad = mm(values, grads, NT)
        row = lax.broadcasted_iota(jnp.int32, (per, 2 * GROUP), 0)
        scores = jnp.where(row < count * RLEN, scores, NEG)
        peak = jnp.max(scores, axis=0, keepdims=True)
        weight = jnp.exp2((scores - peak) * (SCALE * LOG2E))
        total = jnp.sum(weight, axis=0, keepdims=True)
        inverse = jnp.where(count > 0, 1.0 / total, 0.0)
        probs = weight * inverse
        delta = jnp.sum(probs * prob_grad, axis=0, keepdims=True)
        score_grad = (probs * (prob_grad - delta)).astype(BF)
        low = probs.astype(BF)
        out = mm(low, values, TN).astype(BF)
        dq = (mm(score_grad, keys, TN) * SCALE).astype(BF)
        tok = slice(u * GROUP, (u + 1) * GROUP)
        out_ref[tok, :HD] = out[:GROUP, :HD]
        out_ref[tok, HD:] = out[GROUP:, HD:]
        dq_ref[tok, :HD] = dq[:GROUP, :HD]
        dq_ref[tok, HD:] = dq[GROUP:, HD:]
        dkv_ref[at, :PAIR] = (mm(score_grad, queries, NN) * SCALE).astype(BF)
        dkv_ref[at, PAIR:] = mm(low, grads, NN).astype(BF)
    half = keep_ref.shape[1]
    bit = shard & 1
    for ref, which in ((send_ref, 1 - bit), (keep_ref, bit)):
        at = pl.ds(pl.multiple_of(which * half, 16), half)
        part = mm(nbt_ref[at, :], dkv_ref[...], NN).astype(BF)
        ref[0] = part[:, :PAIR]
        ref[1] = part[:, PAIR:]


def cross(chunk, info, count, nb, nbt, weights, cq, do):
    pieces = len(weights)
    pairs = HEADS // 2 // CHUNKS
    first = chunk * pairs
    groups = cq.shape[0] // GROUP
    tokens, enc = cq.shape[0], nb.shape[1]
    shard_rows = enc // pieces
    whole = lambda p: (0, 0)
    here = lambda p: (0, first + p)
    specs, operands = [], []
    for piece in weights:
        width = piece.shape[1]
        start = first if width == 2 * HEADS * HD else 0
        other = width // PAIR // 2
        specs.append(pl.BlockSpec((shard_rows, PAIR), lambda p, s=start: (0, s + p)))
        specs.append(pl.BlockSpec((shard_rows, PAIR), lambda p, s=start + other: (0, s + p)))
        operands += [piece, piece]
    part = jax.ShapeDtypeStruct((2, enc // 2, pairs * PAIR), BF)
    part_spec = pl.BlockSpec((2, enc // 2, PAIR), lambda p: (0, 0, p))
    tok_spec = pl.BlockSpec((tokens, PAIR), lambda p: (0, p))
    tok_shape = jax.ShapeDtypeStruct((tokens, pairs * PAIR), BF)
    smem = pl.BlockSpec(memory_space=pltpu.SMEM)
    return pl.pallas_call(
        functools.partial(cross_kernel, pieces, groups),
        grid=(pairs,),
        in_specs=[smem, smem, pl.BlockSpec(nb.shape, whole), pl.BlockSpec(nbt.shape, whole)]
        + specs
        + [pl.BlockSpec((tokens, PAIR), here)] * 2,
        out_specs=[tok_spec, tok_spec, part_spec, part_spec],
        out_shape=[tok_shape, tok_shape, part, part],
        scratch_shapes=[
            pltpu.VMEM((enc, 2 * PAIR), BF),
            pltpu.VMEM((nb.shape[0], 2 * PAIR), BF),
            pltpu.VMEM((nb.shape[0], 2 * PAIR), BF),
        ],
        compiler_params=pltpu.CompilerParams(vmem_limit_bytes=40 * 2**20),
        cost_estimate=pl.CostEstimate(
            flops=pairs * 2_200_000_000, bytes_accessed=8_000_000, transcendentals=0
        ),
    )(info, count, nb, nbt, *operands, cq, do)


def self_kernel(
    heads, info_ref, q_ref, do_ref, kp_ref, ko_ref, vp_ref, vo_ref, co_ref,
    out_ref, dq_ref, dk_ref, dv_ref, stat_ref,
):
    later = info_ref[1] > 0
    tokens = q_ref.shape[0]
    half = tokens // 2
    key_at = lax.broadcasted_iota(jnp.int32, (half, half), 0)
    query_at = lax.broadcasted_iota(jnp.int32, (half, half), 1)
    above = jnp.logical_and(key_at > query_at, later)
    below = key_at <= query_at
    zero = jnp.zeros((half, half), BF)
    lo, hi = slice(0, half), slice(half, None)
    for head in range(heads):
        at = slice(head * HD, (head + 1) * HD)
        queries, grads = q_ref[:, at], do_ref[:, at]
        kp, ko, vp, vo = kp_ref[:, at], ko_ref[:, at], vp_ref[:, at], vo_ref[:, at]
        sp, so = mm(kp, queries, NT), mm(ko, queries, NT)
        gp, go = mm(vp, grads, NT), mm(vo, grads, NT)
        rows = []
        for a in (0, 1):
            if a == 0:
                blocks = (sp[lo, lo], sp[hi, lo], so[lo, lo])
                pgrads = (gp[lo, lo], gp[hi, lo], go[lo, lo])
                middle = jnp.where(later, blocks[1], NEG)
            else:
                blocks = (sp[hi, hi], so[lo, hi], so[hi, hi])
                pgrads = (gp[hi, hi], go[lo, hi], go[hi, hi])
                middle = blocks[1]
            scores = (jnp.where(above, blocks[0], NEG), middle, jnp.where(below, blocks[2], NEG))
            peak = jnp.max(
                jnp.maximum(jnp.maximum(scores[0], scores[1]), scores[2]), axis=0, keepdims=True
            )
            weight = [jnp.exp2((s - peak) * (SCALE * LOG2E)) for s in scores]
            total = jnp.sum(weight[0] + weight[1] + weight[2], axis=0, keepdims=True)
            inverse = 1.0 / total
            probs = [w * inverse for w in weight]
            delta = jnp.sum(
                probs[0] * pgrads[0] + probs[1] * pgrads[1] + probs[2] * pgrads[2],
                axis=0,
                keepdims=True,
            )
            score_grad = [(p * (g - delta)).astype(BF) for p, g in zip(probs, pgrads)]
            rows.append(([p.astype(BF) for p in probs], score_grad))
            lanes = slice(a * half, (a + 1) * half)
            stat_ref[head, 0:1, lanes] = peak * (SCALE * LOG2E) + jnp.log2(total)
            stat_ref[head, 1:2, lanes] = delta

        def spread(which):
            first, second = rows[0][which], rows[1][which]
            before = jnp.concatenate(
                [
                    jnp.concatenate([first[0], zero], 1),
                    jnp.concatenate([first[1], second[0]], 1),
                ],
                0,
            )
            own = jnp.concatenate(
                [
                    jnp.concatenate([first[2], second[1]], 1),
                    jnp.concatenate([zero, second[2]], 1),
                ],
                0,
            )
            return before, own

        (pp, po), (dp, do) = spread(0), spread(1)
        out = mm(pp, vp, TN) + mm(po, vo, TN) + co_ref[:, at].astype(F32)
        out_ref[:, at] = out.astype(BF)
        dq_ref[:, at] = ((mm(dp, kp, TN) + mm(do, ko, TN)) * SCALE).astype(BF)
        dk_ref[:, at] = mm(do, queries, NN) * SCALE
        dv_ref[:, at] = mm(po, grads, NN)


def self_part(info, q, do, kp, ko, vp, vo, co):
    heads = 2
    tokens, width = q.shape
    spec = pl.BlockSpec((tokens, heads * HD), lambda p: (0, p))
    shape = jax.ShapeDtypeStruct(q.shape, BF)
    wide = jax.ShapeDtypeStruct(q.shape, F32)
    return pl.pallas_call(
        functools.partial(self_kernel, heads),
        grid=(width // (heads * HD),),
        in_specs=[pl.BlockSpec(memory_space=pltpu.SMEM)] + [spec] * 7,
        out_specs=[spec] * 4 + [pl.BlockSpec((heads, 2, tokens), lambda p: (p, 0, 0))],
        out_shape=[shape, shape, wide, wide, jax.ShapeDtypeStruct((width // HD, 2, tokens), F32)],
        compiler_params=pltpu.CompilerParams(vmem_limit_bytes=40 * 2**20),
        cost_estimate=pl.CostEstimate(
            flops=10_000_000_000, bytes_accessed=14_000_000, transcendentals=0
        ),
    )(info, q, do, kp, ko, vp, vo, co)


def next_kernel(
    heads, q_ref, do_ref, k_ref, v_ref, stat_ref, dkp_ref, dvp_ref, dk_ref, dv_ref
):
    tokens = q_ref.shape[0]
    half = tokens // 2
    key_at = lax.broadcasted_iota(jnp.int32, (half, half), 0)
    query_at = lax.broadcasted_iota(jnp.int32, (half, half), 1)
    above = key_at > query_at
    zero = jnp.zeros((half, half), BF)
    lo, hi = slice(0, half), slice(half, None)
    for head in range(heads):
        at = slice(head * HD, (head + 1) * HD)
        queries, grads = q_ref[:, at], do_ref[:, at]
        scores = mm(k_ref[:, at], queries, NT)
        prob_grad = mm(v_ref[:, at], grads, NT)
        level, delta = stat_ref[head, 0:1, :], stat_ref[head, 1:2, :]

        def block(rows, lanes, mask):
            exponent = scores[rows, lanes] * (SCALE * LOG2E) - level[:, lanes]
            if mask:
                exponent = jnp.where(above, exponent, NEG)
            probs = jnp.exp2(exponent)
            return probs.astype(BF), (probs * (prob_grad[rows, lanes] - delta[:, lanes])).astype(BF)

        first, middle, last = block(lo, lo, True), block(hi, lo, False), block(hi, hi, True)
        low, score_grad = [
            jnp.concatenate(
                [
                    jnp.concatenate([first[i], zero], 1),
                    jnp.concatenate([middle[i], last[i]], 1),
                ],
                0,
            )
            for i in (0, 1)
        ]
        dk_ref[:, at] = (dkp_ref[:, at] + mm(score_grad, queries, NN) * SCALE).astype(BF)
        dv_ref[:, at] = (dvp_ref[:, at] + mm(low, grads, NN)).astype(BF)


def next_part(q, do, k, v, stats, dk, dv):
    heads = 2
    tokens, width = q.shape
    spec = pl.BlockSpec((tokens, heads * HD), lambda p: (0, p))
    shape = jax.ShapeDtypeStruct(q.shape, BF)
    return pl.pallas_call(
        functools.partial(next_kernel, heads),
        grid=(width // (heads * HD),),
        in_specs=[spec] * 4
        + [pl.BlockSpec((heads, 2, tokens), lambda p: (p, 0, 0))]
        + [spec] * 2,
        out_specs=[spec] * 2,
        out_shape=[shape, shape],
        compiler_params=pltpu.CompilerParams(vmem_limit_bytes=40 * 2**20),
        cost_estimate=pl.CostEstimate(
            flops=6_000_000_000, bytes_accessed=10_000_000, transcendentals=0
        ),
    )(q, do, k, v, stats, dk, dv)


def halving_order(fsdp, seq):
    bits = [("fsdp", 1 << i) for i in range(fsdp.bit_length() - 1)]
    seq_bits = [("seq", 1 << i) for i in range(seq.bit_length() - 1)]
    return bits + seq_bits[1:] + seq_bits[:1]


def row_order(fsdp, seq, rows):
    index = np.arange(rows).reshape(seq * fsdp, -1)
    block = np.arange(seq * fsdp)
    keys = []
    for axis, bit in halving_order(fsdp, seq):
        value = block % fsdp if axis == "fsdp" else block // fsdp
        keys.append((value // bit) % 2)
    order = np.lexsort(keys[::-1])
    return index[order].reshape(-1)


def take_half(value, upper):
    half = value.shape[1] // 2
    return lax.dynamic_slice_in_dim(value, upper * half, half, 1)


def halve(keep, received, bit, dtype):
    mine = take_half(keep, bit).astype(F32) + take_half(received, bit).astype(F32)
    other = take_half(keep, 1 - bit).astype(F32) + take_half(received, 1 - bit).astype(F32)
    return mine.astype(dtype), other.astype(BF)


def on_device(
    self_query, self_key, self_value, cross_query, neighbours, neighbour_count, kv_weight, out_grad
):
    fsdp, seq = lax.axis_size("fsdp"), lax.axis_size("seq")
    shard, slab = lax.axis_index("fsdp"), lax.axis_index("seq")
    q, k, v, cq, do = (x[0] for x in (self_query, self_key, self_value, cross_query, out_grad))
    nb, counts = neighbours[0], neighbour_count[0]
    tokens, width = q.shape
    groups, enc = nb.shape[0], nb.shape[2]
    info = jnp.stack([shard, slab]).astype(jnp.int32)

    nb_last, count_last = shift((nb[groups - 1], counts[groups - 1 :].astype(F32)), "seq", 1)
    rows = kv_weight.shape[0]
    per = width // CHUNKS
    columns = kv_weight.reshape(rows, 2, CHUNKS, per)
    pieces = [[kv_weight, swap(kv_weight, "fsdp", 1)] for _ in range(1)][0]
    far = []
    for chunk in range(CHUNKS):
        piece = columns[:, :, chunk].reshape(rows, 2 * per)
        if chunk >= 2:
            piece, _ = lax.optimization_barrier((piece, far[chunk - 2][0]))
        piece = swap(piece, "fsdp", 2)
        far.append((piece, swap(piece, "fsdp", 1)))
    k_before, v_before = shift((k, v), "seq", 1)
    q_late, do_late, _, _ = lax.optimization_barrier((q, do, k_before, v_before))
    q_after, do_after = shift((q_late, do_late), "seq", -1)

    nb_used = jnp.concatenate([nb_last[None], nb[: groups - 1]], 0).reshape(-1, enc)
    count_used = jnp.concatenate(
        [count_last.astype(jnp.int32), counts[: groups - 1]], 0
    )
    order = row_order(fsdp, seq, enc)
    pick = (jnp.asarray(order, jnp.int32)[:, None] == jnp.arange(enc, dtype=jnp.int32)).astype(BF)
    nb_turned = mm(pick, nb_used, NT).astype(BF)

    stages = halving_order(fsdp, seq)

    def my_bit(stage):
        axis, bit = stages[stage]
        return ((shard if axis == "fsdp" else slab) // bit) % 2

    cross_out, cross_grad, parts = [], [], []
    for chunk in range(CHUNKS):
        out, dq, keep, send = cross(
            chunk, info, count_used, nb_used, nb_turned, pieces + list(far[chunk]), cq, do
        )
        cross_out.append(out)
        cross_grad.append(dq)
        for stage in range(len(stages)):
            received = swap(send, *stages[stage])
            if stage + 1 < len(stages):
                keep, send = halve(keep, received, my_bit(stage + 1), BF)
            else:
                keep = keep.astype(F32) + received.astype(F32)
        parts.append(keep)
    weight_grad = jnp.concatenate(parts, -1).transpose(1, 0, 2).reshape(-1, 2 * width)
    cross_out = jnp.concatenate(cross_out, 1)
    cross_grad = jnp.concatenate(cross_grad, 1)

    block_out, query_grad, dk, dv, stats = self_part(
        info, q, do, k_before, k, v_before, v, cross_out
    )
    stats_after = shift(stats, "seq", -1)
    key_grad, value_grad = next_part(q_after, do_after, k, v, stats_after, dk, dv)
    return (
        block_out[None],
        query_grad[None],
        key_grad[None],
        value_grad[None],
        cross_grad[None],
        weight_grad,
    )


def solution(mesh):
    in_specs = (
        P("fsdp", "seq", None),
        P("fsdp", "seq", None),
        P("fsdp", "seq", None),
        P("fsdp", "seq", None),
        P("fsdp", "seq", None, None),
        P("fsdp", "seq"),
        P("fsdp", None),
        P("fsdp", "seq", None),
    )
    out_specs = (
        P("fsdp", "seq", None),
        P("fsdp", "seq", None),
        P("fsdp", "seq", None),
        P("fsdp", "seq", None),
        P("fsdp", "seq", None),
        P(("seq", "fsdp"), None),
    )
    return jax.shard_map(
        on_device, mesh=mesh, in_specs=in_specs, out_specs=out_specs, check_vma=False
    )
```

time: 498 us -> 218 us (0.44)
  waiting for transfers between devices: 180 us -> 31.9 us
  matrix products: 142 us -> 1.43 us
  starting transfers between devices: 21.1 us -> 97.4 us
  local copies, waits for them, and re-layouts: 102 us -> 26.1 us
  Pallas kernels: 0 us -> 54.5 us
  other arithmetic: 33.7 us -> 3.23 us
  between operations: 14.8 us -> 2.28 us
    dot_general x14 -> x1, matrix products: 142 us -> 1.43 us  [mm(): return lax.dot_general(a, b, dims, preferred_element_type=F32)]
    ppermute x7 -> x36, waiting for transfers between devices: 114 us -> 31.9 us  [the longest x29 24.4 us: swap(): lax.ppermute(value, axis, [(i, i ^ bit) for i in range(lax.axis_size(axis...]
    ppermute x7 -> x36, starting transfers between devices: 21 us -> 97.4 us  [the longest x7 50.9 us: shift(): lax.ppermute(value, axis, [(i, i + steps) for i in range(first, last)])]
    pallas_call x0 -> x6, Pallas kernels: none -> 54.5 us  [the longest x4 33.6 us: cross(): pl.pallas_call(functools.partial(cross_kernel, pieces, groups), grid=(pai...]
    all_gather x1 -> x0, waiting for transfers between devices: 50.7 us -> none  [on_device(): lax.all_gather(kv_weight, 'fsdp', axis=0, tiled=True)]
    unnamed x48 -> x24, local copies, waits for them, and re-layouts: 31.3 us -> 5.23 us
    slice x11 -> x3, local copies, waits for them, and re-layouts: 31 us -> 14.5 us  [the longest x1 12.5 us: on_device(): piece = columns[:, :, chunk].reshape(rows, 2 * per)]
    unnamed x3 -> x0, waiting for transfers between devices: 15.6 us -> none
  transfers between devices with their start and end apart: 9 -> 36, of which waited for: 8 -> 12; matrix products, arithmetic and copies ran while one was open for 33% -> 14% of each run, Pallas kernels for 0% -> 25%
where the time goes in v1:
time: 218 us; the launch traced here: 217 us
  starting transfers between devices  97.4 us (45%)
  Pallas kernels  54.5 us (25%)
  waiting for transfers between devices  31.9 us (15%)
  local copies, waits for them, and re-layouts  26.1 us (12%)
  other arithmetic  3.23 us (1%)
  between operations  2.28 us (1%)
    ppermute x7, starting transfers between devices, shift(): lax.ppermute(value, axis, [(i, i + steps) for i in range(first, last)])  50.9 us
    ppermute x29, starting transfers between devices, swap(): lax.ppermute(value, axis, [(i, i ^ bit) for i in range(lax.axis_size(axis...  46.6 us
    pallas_call x4, Pallas kernels, cross(): pl.pallas_call(functools.partial(cross_kernel, pieces, groups), grid=(pai...  33.6 us
    ppermute x29, waiting for transfers between devices, swap(): lax.ppermute(value, axis, [(i, i ^ bit) for i in range(lax.axis_size(axis...  24.4 us
    pallas_call x1, Pallas kernels, self_part(): pl.pallas_call(functools.partial(self_kernel, heads), grid=(width // (hea...  13 us
    slice x1, local copies, waits for them, and re-layouts, on_device(): piece = columns[:, :, chunk].reshape(rows, 2 * per)  12.5 us
    pallas_call x1, Pallas kernels, next_part(): pl.pallas_call(functools.partial(next_kernel, heads), grid=(width // (hea...  7.82 us
    ppermute x7, waiting for transfers between devices, shift(): lax.ppermute(value, axis, [(i, i + steps) for i in range(first, last)])  7.52 us
  transfers between devices with their start and end apart: 36, of which 12 were waited for; matrix products, arithmetic and copies ran while one was open for 14% of the time, Pallas kernels for 25%

profile of v1, /device:TPU:0, one launch (start us, length us, event | category | flops | bytes accessed | tf_op | source)
XLA Modules:
  0.0 216.9 jit_solution(14978569132554764097)
XLA Ops:
  1.1 3.9 %reshape.29 = bf16[192,2,4,512]{3,2,1,0:T(4,128)(2,1)} reshape(bf16[192,4096]{1,0:T(8,128)(2,1)} %refs_1_.7) | data formatting | bytes 3145728 | tf_op jit(solution)/shard_map/reshape | solution.py:338
  5.0 12.5 %slice_reduce_fusion.3 = (bf16[192,2,512]{2,1,0:T(2,128)(2,1)S(1)}, bf16[192,2,512]{2,1,0:T(2,128)(2,1)}, bf16[192,2,512]{2,1,0:T(2,128)(2,1)S(1)}, bf16[192,2,512]{2,1,0:T(2,128)(2,1)}) fusion(bf16[192,2,4,512]{3,2,1,0:T(4,128)(2,1)} %reshape.29), kind=kLoop, calls=%fused_computation.11 | loop fusion | bytes 3145728 | tf_op jit(solution)/shard_map/slice | solution.py:342
  18.4 2.5 %collective-permute-start.5 = (bf16[192,1024]{1,0:T(8,128)(2,1)}, bf16[192,1024]{1,0:T(8,128)(2,1)S(1)}, u32[]{:S(2)}, u32[]{:S(2)}) collective-permute-start(bf16[192,1024]{1,0:T(8,128)(2,1)} %bitcast.22), channel_id=1, source_target_pairs={{0,2},{1,3},{2,0},{3,1},{4,6},{5,7},{6,4},{7,5},{8,10},{9,11},{10,... | collective-permute-start | bytes 1179656 | tf_op jit(solution)/shard_map/ppermute | solution.py:39
  21.7 4.9 %collective-permute-start = (bf16[256,2048]{1,0:T(8,128)(2,1)S(1)}, bf16[256,2048]{1,0:T(8,128)(2,1)}, u32[]{:S(2)}, u32[]{:S(2)}) collective-permute-start(bf16[256,2048]{1,0:T(8,128)(2,1)S(1)} %bitcast.52), channel_id=1, source_target_pairs={{0,4},{4,8},{8,12},{12,16},{16,20},{20,24},{24,28},{1,5},{5,9},{9,... | collective-permute-start | bytes 3145736 | tf_op jit(solution)/shard_map/ppermute | solution.py:35
  26.6 3.4 %collective-permute-start.1 = (bf16[256,2048]{1,0:T(8,128)(2,1)}, bf16[256,2048]{1,0:T(8,128)(2,1)}, u32[]{:S(2)}, u32[]{:S(2)}) collective-permute-start(bf16[256,2048]{1,0:T(8,128)(2,1)} %bitcast.5.vo_ref.v_ref), channel_id=1, source_target_pairs={{0,4},{4,8},{8,12},{12,16},{16,20},{20,24},{24,28},{1,5},{5,9},{9,... | collective-permute-start | bytes 3145736 | tf_op jit(solution)/shard_map/ppermute | solution.py:35
  36.7 34.0 %collective-permute-start.2 = (f32[1]{0:T(128)}, f32[1]{0:T(128)}, u32[]{:S(2)}, u32[]{:S(2)}) collective-permute-start(f32[1]{0:T(128)} %bitcast.6), channel_id=1, source_target_pairs={{0,4},{4,8},{8,12},{12,16},{16,20},{20,24},{24,28},{1,5},{5,9},{9,... | collective-permute-start | bytes 20 | tf_op jit(solution)/shard_map/ppermute | solution.py:35
  70.7 4.5 %collective-permute-start.3 = (bf16[256,768]{1,0:T(8,128)(2,1)}, bf16[256,768]{1,0:T(8,128)(2,1)S(1)}, u32[]{:S(2)}, u32[]{:S(2)}) collective-permute-start(bf16[256,768]{1,0:T(8,128)(2,1)} %slice_bitcast_fusion.1), channel_id=1, source_target_pairs={{0,4},{4,8},{8,12},{12,16},{16,20},{20,24},{24,28},{1,5},{5,9},{9,... | collective-permute-start | bytes 1179656 | tf_op jit(solution)/shard_map/ppermute | solution.py:35
  78.8 4.2 %collective-permute-done.3 = bf16[256,768]{1,0:T(8,128)(2,1)S(1)} collective-permute-done((bf16[256,768]{1,0:T(8,128)(2,1)}, bf16[256,768]{1,0:T(8,128)(2,1)S(1)}, u32[]{:S(2)}, u32[]{:S(2)}) %collective-permute-start.3) | collective-permute-done | bytes 393248 | tf_op jit(solution)/shard_map/ppermute | solution.py:35
  88.3 5.3 %collective-permute-done.11.refs_4_.refs_5_ = bf16[192,1024]{1,0:T(8,128)(2,1)S(1)} collective-permute-done((bf16[192,1024]{1,0:T(8,128)(2,1)S(1)}, bf16[192,1024]{1,0:T(8,128)(2,1)S(1)}, u32[]{:S(2)}, u32[]{:S(2)}) %collective-permute-start.11) | collective-permute-done | bytes 393248 | tf_op jit(solution)/shard_map/ppermute | solution.py:39
  97.1 8.1 %shard_map.136 = (bf16[256,512]{1,0:T(8,128)(2,1)S(1)}, bf16[256,512]{1,0:T(8,128)(2,1)S(1)}, bf16[2,384,512]{2,1,0:T(8,128)(2,1)S(1)}, bf16[2,384,512]{2,1,0:T(8,128)(2,1)S(1)}) custom-call(s32[2]{0:T(128)S(1)} %pad_add_fusion.info_ref, s32[4]{0:T(128)S(1)} %pad_add_fusion.1.count_ref, bf16[1024,768]{1,0:T(8,128)(2,1)S(1)} %bitcast.36, ...), custom_call_target="tpu_custom_call" | custom-call | flops 4400000000 | bytes 8000000 | tf_op jit(solution)/shard_map/pallas_call | solution.py:124
  105.7 8.1 %shard_map.137 = (bf16[256,512]{1,0:T(8,128)(2,1)S(1)}, bf16[256,512]{1,0:T(8,128)(2,1)S(1)}, bf16[2,384,512]{2,1,0:T(8,128)(2,1)S(1)}, bf16[2,384,512]{2,1,0:T(8,128)(2,1)S(1)}) custom-call(s32[2]{0:T(128)S(1)} %pad_add_fusion.info_ref, s32[4]{0:T(128)S(1)} %pad_add_fusion.1.count_ref, bf16[1024,768]{1,0:T(8,128)(2,1)S(1)} %bitcast.37, ...), custom_call_target="tpu_custom_call" | custom-call | flops 4400000000 | bytes 8000000 | tf_op jit(solution)/shard_map/pallas_call | solution.py:124
  113.9 8.7 %shard_map.138 = (bf16[256,512]{1,0:T(8,128)(2,1)S(1)}, bf16[256,512]{1,0:T(8,128)(2,1)S(1)}, bf16[2,384,512]{2,1,0:T(8,128)(2,1)S(1)}, bf16[2,384,512]{2,1,0:T(8,128)(2,1)}) custom-call(s32[2]{0:T(128)S(1)} %pad_add_fusion.info_ref, s32[4]{0:T(128)S(1)} %pad_add_fusion.1.count_ref, bf16[1024,768]{1,0:T(8,128)(2,1)S(1)} %bitcast.38, ...), custom_call_target="tpu_custom_call" | custom-call | flops 4400000000 | bytes 8000000 | tf_op jit(solution)/shard_map/pallas_call | solution.py:124
  123.1 8.7 %shard_map.139 = (bf16[256,512]{1,0:T(8,128)(2,1)S(1)}, bf16[256,512]{1,0:T(8,128)(2,1)S(1)}, bf16[2,384,512]{2,1,0:T(8,128)(2,1)S(1)}, bf16[2,384,512]{2,1,0:T(8,128)(2,1)}) custom-call(s32[2]{0:T(128)S(1)} %pad_add_fusion.info_ref, s32[4]{0:T(128)S(1)} %pad_add_fusion.1.count_ref, bf16[1024,768]{1,0:T(8,128)(2,1)S(1)} %bitcast.39, ...), custom_call_target="tpu_custom_call" | custom-call | flops 4400000000 | bytes 8000000 | tf_op jit(solution)/shard_map/pallas_call | solution.py:124
  132.1 13.0 %shard_map.140 = (bf16[256,2048]{1,0:T(8,128)(2,1)}, bf16[256,2048]{1,0:T(8,128)(2,1)}, f32[256,2048]{1,0:T(8,128)S(1)}, f32[256,2048]{1,0:T(8,128)S(1)}, f32[16,2,256]{2,1,0:T(2,128)S(1)}) custom-call(s32[2]{0:T(128)S(1)} %pad_add_fusion.info_ref, bf16[256,2048]{1,0:T(8,128)(2,1)S(1)} %bitcast.45, bf16[256,2048]{1,0:T(8,128)(2,1)S(1)} %bitcast.51, ...), custom_call_target="tpu_custom_call" | custom-call | flops 10000000000 | bytes 14000000 | tf_op jit(solution)/shard_map/pallas_call | solution.py:224
  150.6 3.4 %collective-permute-done.15.stat_ref = f32[16,2,256]{2,1,0:T(2,128)S(1)} collective-permute-done((f32[16,2,256]{2,1,0:T(2,128)S(1)}, f32[16,2,256]{2,1,0:T(2,128)S(1)}, u32[]{:S(2)}, u32[]{:S(2)}) %collective-permute-start.15) | collective-permute-done | bytes 32800 | tf_op jit(solution)/shard_map/ppermute | solution.py:35
  156.0 7.8 %shard_map.141 = (bf16[256,2048]{1,0:T(8,128)(2,1)}, bf16[256,2048]{1,0:T(8,128)(2,1)}) custom-call(bf16[256,2048]{1,0:T(8,128)(2,1)S(1)} %collective-permute-done.13.q_ref, bf16[256,2048]{1,0:T(8,128)(2,1)S(1)} %collective-permute-done.14.do_ref, bf16[256,2048]{1,0:T(8,128)(2,1)S(1)} %bitcast.54, bf16[256,2048]{1,0:T(8,128)(2,1)} %bitcast.5.vo_ref.v_ref, ...), custom_call_target="tpu_custom_call" | custom-call | flops 6000000000 | bytes 10000000 | tf_op jit(solution)/shard_map/pallas_call | solution.py:281
  164.0 3.4 %collective-permute-start.18 = (bf16[2,96,512]{2,1,0:T(8,128)(2,1)S(1)}, bf16[2,96,512]{2,1,0:T(8,128)(2,1)S(1)}, u32[]{:S(2)}, u32[]{:S(2)}) collective-permute-start(bf16[2,96,512]{2,1,0:T(8,128)(2,1)S(1)} %get-tuple-element.73), channel_id=1, source_target_pairs={{0,8},{4,12},{8,0},{12,4},{16,24},{20,28},{24,16},{28,20},{1,9},{5... | collective-permute-start | bytes 589832 | tf_op jit(solution)/shard_map/ppermute | solution.py:39
  168.5 5.8 %collective-permute-start.23 = (bf16[2,96,512]{2,1,0:T(8,128)(2,1)S(1)}, bf16[2,96,512]{2,1,0:T(8,128)(2,1)S(1)}, u32[]{:S(2)}, u32[]{:S(2)}) collective-permute-start(bf16[2,96,512]{2,1,0:T(8,128)(2,1)S(1)} %get-tuple-element.75), channel_id=1, source_target_pairs={{0,8},{4,12},{8,0},{12,4},{16,24},{20,28},{24,16},{28,20},{1,9},{5... | collective-permute-start | bytes 589832 | tf_op jit(solution)/shard_map/ppermute | solution.py:39
  177.0 5.8 %collective-permute-start.28 = (bf16[2,96,512]{2,1,0:T(8,128)(2,1)S(1)}, bf16[2,96,512]{2,1,0:T(8,128)(2,1)S(1)}, u32[]{:S(2)}, u32[]{:S(2)}) collective-permute-start(bf16[2,96,512]{2,1,0:T(8,128)(2,1)S(1)} %get-tuple-element.77), channel_id=1, source_target_pairs={{0,8},{4,12},{8,0},{12,4},{16,24},{20,28},{24,16},{28,20},{1,9},{5... | collective-permute-start | bytes 589832 | tf_op jit(solution)/shard_map/ppermute | solution.py:39
  184.9 5.5 %collective-permute-start.33 = (bf16[2,96,512]{2,1,0:T(8,128)(2,1)S(1)}, bf16[2,96,512]{2,1,0:T(8,128)(2,1)S(1)}, u32[]{:S(2)}, u32[]{:S(2)}) collective-permute-start(bf16[2,96,512]{2,1,0:T(8,128)(2,1)S(1)} %get-tuple-element.79), channel_id=1, source_target_pairs={{0,8},{4,12},{8,0},{12,4},{16,24},{20,28},{24,16},{28,20},{1,9},{5... | collective-permute-start | bytes 589832 | tf_op jit(solution)/shard_map/ppermute | solution.py:39
  190.5 4.2 %collective-permute-start.19 = (bf16[2,48,512]{2,1,0:T(8,128)(2,1)S(1)}, bf16[2,48,512]{2,1,0:T(8,128)(2,1)S(1)}, u32[]{:S(2)}, u32[]{:S(2)}) collective-permute-start(bf16[2,48,512]{2,1,0:T(8,128)(2,1)S(1)} %get-tuple-element.81), channel_id=1, source_target_pairs={{0,16},{4,20},{8,24},{12,28},{16,0},{20,4},{24,8},{28,12},{1,17},{... | collective-permute-start | bytes 294920 | tf_op jit(solution)/shard_map/ppermute | solution.py:39
  194.9 3.0 %collective-permute-start.29 = (bf16[2,48,512]{2,1,0:T(8,128)(2,1)S(1)}, bf16[2,48,512]{2,1,0:T(8,128)(2,1)S(1)}, u32[]{:S(2)}, u32[]{:S(2)}) collective-permute-start(bf16[2,48,512]{2,1,0:T(8,128)(2,1)S(1)} %get-tuple-element.85), channel_id=1, source_target_pairs={{0,16},{4,20},{8,24},{12,28},{16,0},{20,4},{24,8},{28,12},{1,17},{... | collective-permute-start | bytes 294920 | tf_op jit(solution)/shard_map/ppermute | solution.py:39
  197.9 3.0 %collective-permute-start.34 = (bf16[2,48,512]{2,1,0:T(8,128)(2,1)S(1)}, bf16[2,48,512]{2,1,0:T(8,128)(2,1)S(1)}, u32[]{:S(2)}, u32[]{:S(2)}) collective-permute-start(bf16[2,48,512]{2,1,0:T(8,128)(2,1)S(1)} %get-tuple-element.87), channel_id=1, source_target_pairs={{0,16},{4,20},{8,24},{12,28},{16,0},{20,4},{24,8},{28,12},{1,17},{... | collective-permute-start | bytes 294920 | tf_op jit(solution)/shard_map/ppermute | solution.py:39
  201.8 6.7 %collective-permute-done.24 = bf16[2,48,512]{2,1,0:T(8,128)(2,1)S(1)} collective-permute-done((bf16[2,48,512]{2,1,0:T(8,128)(2,1)S(1)}, bf16[2,48,512]{2,1,0:T(8,128)(2,1)S(1)}, u32[]{:S(2)}, u32[]{:S(2)}) %collective-permute-start.24) | collective-permute-done | bytes 98336 | tf_op jit(solution)/shard_map/ppermute | solution.py:39
  (112 shorter events, 44.1 us)
Async XLA Ops:
  0.6 94.9 %collective-permute-start.4 = (bf16[192,4096]{1,0:T(8,128)(2,1)}, bf16[192,4096]{1,0:T(8,128)(2,1)S(1)}, u32[]{:S(2)}, u32[]{:S(2)}) collective-permute-start(bf16[192,4096]{1,0:T(8,128)(2,1)} %refs_1_.7), channel_id=1, source_target_pairs={{0,1},{1,0},{2,3},{3,2},{4,5},{5,4},{6,7},{7,6},{8,9},{9,8},{10,11... | collective-permute-start | bytes 4718600 | tf_op jit(solution)/shard_map/ppermute | solution.py:39
  18.4 18.3 %collective-permute-start.5 = (bf16[192,1024]{1,0:T(8,128)(2,1)}, bf16[192,1024]{1,0:T(8,128)(2,1)S(1)}, u32[]{:S(2)}, u32[]{:S(2)}) collective-permute-start(bf16[192,1024]{1,0:T(8,128)(2,1)} %bitcast.22), channel_id=1, source_target_pairs={{0,2},{1,3},{2,0},{3,1},{4,6},{5,7},{6,4},{7,5},{8,10},{9,11},{10,... | collective-permute-start | bytes 1179656 | tf_op jit(solution)/shard_map/ppermute | solution.py:39
  21.7 53.5 %collective-permute-start.7 = (bf16[192,1024]{1,0:T(8,128)(2,1)}, bf16[192,1024]{1,0:T(8,128)(2,1)S(1)}, u32[]{:S(2)}, u32[]{:S(2)}) collective-permute-start(bf16[192,1024]{1,0:T(8,128)(2,1)} %bitcast.24), channel_id=1, source_target_pairs={{0,2},{1,3},{2,0},{3,1},{4,6},{5,7},{6,4},{7,5},{8,10},{9,11},{10,... | collective-permute-start | bytes 1179656 | tf_op jit(solution)/shard_map/ppermute | solution.py:39
  21.7 72.0 %collective-permute-start = (bf16[256,2048]{1,0:T(8,128)(2,1)S(1)}, bf16[256,2048]{1,0:T(8,128)(2,1)}, u32[]{:S(2)}, u32[]{:S(2)}) collective-permute-start(bf16[256,2048]{1,0:T(8,128)(2,1)S(1)} %bitcast.52), channel_id=1, source_target_pairs={{0,4},{4,8},{8,12},{12,16},{16,20},{20,24},{24,28},{1,5},{5,9},{9,... | collective-permute-start | bytes 3145736 | tf_op jit(solution)/shard_map/ppermute | solution.py:35
  26.6 67.5 %collective-permute-start.1 = (bf16[256,2048]{1,0:T(8,128)(2,1)}, bf16[256,2048]{1,0:T(8,128)(2,1)}, u32[]{:S(2)}, u32[]{:S(2)}) collective-permute-start(bf16[256,2048]{1,0:T(8,128)(2,1)} %bitcast.5.vo_ref.v_ref), channel_id=1, source_target_pairs={{0,4},{4,8},{8,12},{12,16},{16,20},{20,24},{24,28},{1,5},{5,9},{9,... | collective-permute-start | bytes 3145736 | tf_op jit(solution)/shard_map/ppermute | solution.py:35
  36.7 34.0 %collective-permute-start.2 = (f32[1]{0:T(128)}, f32[1]{0:T(128)}, u32[]{:S(2)}, u32[]{:S(2)}) collective-permute-start(f32[1]{0:T(128)} %bitcast.6), channel_id=1, source_target_pairs={{0,4},{4,8},{8,12},{12,16},{16,20},{20,24},{24,28},{1,5},{5,9},{9,... | collective-permute-start | bytes 20 | tf_op jit(solution)/shard_map/ppermute | solution.py:35
  93.6 20.1 %collective-permute-start.10 = (bf16[192,1024]{1,0:T(8,128)(2,1)S(1)}, bf16[192,1024]{1,0:T(8,128)(2,1)S(1)}, u32[]{:S(2)}, u32[]{:S(2)}) collective-permute-start(bf16[192,1024]{1,0:T(8,128)(2,1)S(1)} %collective-permute-done.9.refs_4_.refs_5_), channel_id=1, source_target_pairs={{0,1},{1,0},{2,3},{3,2},{4,5},{5,4},{6,7},{7,6},{8,9},{9,8},{10,11... | collective-permute-start | bytes 1179656 | tf_op jit(solution)/shard_map/ppermute | solution.py:39
  94.2 28.5 %collective-permute-start.12 = (bf16[192,1024]{1,0:T(8,128)(2,1)S(1)}, bf16[192,1024]{1,0:T(8,128)(2,1)S(1)}, u32[]{:S(2)}, u32[]{:S(2)}) collective-permute-start(bf16[192,1024]{1,0:T(8,128)(2,1)S(1)} %collective-permute-done.11.refs_4_.refs_5_), channel_id=1, source_target_pairs={{0,1},{1,0},{2,3},{3,2},{4,5},{5,4},{6,7},{7,6},{8,9},{9,8},{10,11... | collective-permute-start | bytes 1179656 | tf_op jit(solution)/shard_map/ppermute | solution.py:39
  94.2 61.3 %collective-permute-start.13 = (bf16[256,2048]{1,0:T(8,128)(2,1)S(1)}, bf16[256,2048]{1,0:T(8,128)(2,1)S(1)}, u32[]{:S(2)}, u32[]{:S(2)}) collective-permute-start(bf16[256,2048]{1,0:T(8,128)(2,1)S(1)} %bitcast.44), channel_id=1, source_target_pairs={{4,0},{8,4},{12,8},{16,12},{20,16},{24,20},{28,24},{5,1},{9,5},{13... | collective-permute-start | bytes 3145736 | tf_op jit(solution)/shard_map/ppermute | solution.py:35
  95.5 60.5 %collective-permute-start.14 = (bf16[256,2048]{1,0:T(8,128)(2,1)S(1)}, bf16[256,2048]{1,0:T(8,128)(2,1)S(1)}, u32[]{:S(2)}, u32[]{:S(2)}) collective-permute-start(bf16[256,2048]{1,0:T(8,128)(2,1)S(1)} %bitcast.46), channel_id=1, source_target_pairs={{4,0},{8,4},{12,8},{16,12},{20,16},{24,20},{28,24},{5,1},{9,5},{13... | collective-permute-start | bytes 3145736 | tf_op jit(solution)/shard_map/ppermute | solution.py:35
  105.2 26.8 %collective-permute-start.16 = (bf16[2,384,512]{2,1,0:T(8,128)(2,1)S(1)}, bf16[2,384,512]{2,1,0:T(8,128)(2,1)S(1)}, u32[]{:S(2)}, u32[]{:S(2)}) collective-permute-start(bf16[2,384,512]{2,1,0:T(8,128)(2,1)S(1)} %get-tuple-element.53), channel_id=1, source_target_pairs={{0,1},{1,0},{2,3},{3,2},{4,5},{5,4},{6,7},{7,6},{8,9},{9,8},{10,11... | collective-permute-start | bytes 2359304 | tf_op jit(solution)/shard_map/ppermute | solution.py:39
  113.7 32.7 %collective-permute-start.21 = (bf16[2,384,512]{2,1,0:T(8,128)(2,1)S(1)}, bf16[2,384,512]{2,1,0:T(8,128)(2,1)S(1)}, u32[]{:S(2)}, u32[]{:S(2)}) collective-permute-start(bf16[2,384,512]{2,1,0:T(8,128)(2,1)S(1)} %get-tuple-element.55), channel_id=1, source_target_pairs={{0,1},{1,0},{2,3},{3,2},{4,5},{5,4},{6,7},{7,6},{8,9},{9,8},{10,11... | collective-permute-start | bytes 2359304 | tf_op jit(solution)/shard_map/ppermute | solution.py:39
  122.6 25.4 %collective-permute-start.26 = (bf16[2,384,512]{2,1,0:T(8,128)(2,1)}, bf16[2,384,512]{2,1,0:T(8,128)(2,1)S(1)}, u32[]{:S(2)}, u32[]{:S(2)}) collective-permute-start(bf16[2,384,512]{2,1,0:T(8,128)(2,1)} %get-tuple-element.57), channel_id=1, source_target_pairs={{0,1},{1,0},{2,3},{3,2},{4,5},{5,4},{6,7},{7,6},{8,9},{9,8},{10,11... | collective-permute-start | bytes 2359304 | tf_op jit(solution)/shard_map/ppermute | solution.py:39
  131.9 17.9 %collective-permute-start.31 = (bf16[2,384,512]{2,1,0:T(8,128)(2,1)}, bf16[2,384,512]{2,1,0:T(8,128)(2,1)S(1)}, u32[]{:S(2)}, u32[]{:S(2)}) collective-permute-start(bf16[2,384,512]{2,1,0:T(8,128)(2,1)} %get-tuple-element.59), channel_id=1, source_target_pairs={{0,1},{1,0},{2,3},{3,2},{4,5},{5,4},{6,7},{7,6},{8,9},{9,8},{10,11... | collective-permute-start | bytes 2359304 | tf_op jit(solution)/shard_map/ppermute | solution.py:39
  148.0 15.8 %collective-permute-start.17 = (bf16[2,192,512]{2,1,0:T(8,128)(2,1)S(1)}, bf16[2,192,512]{2,1,0:T(8,128)(2,1)S(1)}, u32[]{:S(2)}, u32[]{:S(2)}) collective-permute-start(bf16[2,192,512]{2,1,0:T(8,128)(2,1)S(1)} %get-tuple-element.65), channel_id=1, source_target_pairs={{0,2},{1,3},{2,0},{3,1},{4,6},{5,7},{6,4},{7,5},{8,10},{9,11},{10,... | collective-permute-start | bytes 1179656 | tf_op jit(solution)/shard_map/ppermute | solution.py:39
  149.8 18.6 %collective-permute-start.22 = (bf16[2,192,512]{2,1,0:T(8,128)(2,1)S(1)}, bf16[2,192,512]{2,1,0:T(8,128)(2,1)S(1)}, u32[]{:S(2)}, u32[]{:S(2)}) collective-permute-start(bf16[2,192,512]{2,1,0:T(8,128)(2,1)S(1)} %get-tuple-element.67), channel_id=1, source_target_pairs={{0,2},{1,3},{2,0},{3,1},{4,6},{5,7},{6,4},{7,5},{8,10},{9,11},{10,... | collective-permute-start | bytes 1179656 | tf_op jit(solution)/shard_map/ppermute | solution.py:39
  154.0 22.9 %collective-permute-start.27 = (bf16[2,192,512]{2,1,0:T(8,128)(2,1)S(1)}, bf16[2,192,512]{2,1,0:T(8,128)(2,1)S(1)}, u32[]{:S(2)}, u32[]{:S(2)}) collective-permute-start(bf16[2,192,512]{2,1,0:T(8,128)(2,1)S(1)} %get-tuple-element.69), channel_id=1, source_target_pairs={{0,2},{1,3},{2,0},{3,1},{4,6},{5,7},{6,4},{7,5},{8,10},{9,11},{10,... | collective-permute-start | bytes 1179656 | tf_op jit(solution)/shard_map/ppermute | solution.py:39
  155.5 29.3 %collective-permute-start.32 = (bf16[2,192,512]{2,1,0:T(8,128)(2,1)S(1)}, bf16[2,192,512]{2,1,0:T(8,128)(2,1)S(1)}, u32[]{:S(2)}, u32[]{:S(2)}) collective-permute-start(bf16[2,192,512]{2,1,0:T(8,128)(2,1)S(1)} %get-tuple-element.71), channel_id=1, source_target_pairs={{0,2},{1,3},{2,0},{3,1},{4,6},{5,7},{6,4},{7,5},{8,10},{9,11},{10,... | collective-permute-start | bytes 1179656 | tf_op jit(solution)/shard_map/ppermute | solution.py:39
  164.0 26.5 %collective-permute-start.18 = (bf16[2,96,512]{2,1,0:T(8,128)(2,1)S(1)}, bf16[2,96,512]{2,1,0:T(8,128)(2,1)S(1)}, u32[]{:S(2)}, u32[]{:S(2)}) collective-permute-start(bf16[2,96,512]{2,1,0:T(8,128)(2,1)S(1)} %get-tuple-element.73), channel_id=1, source_target_pairs={{0,8},{4,12},{8,0},{12,4},{16,24},{20,28},{24,16},{28,20},{1,9},{5... | collective-permute-start | bytes 589832 | tf_op jit(solution)/shard_map/ppermute | solution.py:39
  168.5 26.1 %collective-permute-start.23 = (bf16[2,96,512]{2,1,0:T(8,128)(2,1)S(1)}, bf16[2,96,512]{2,1,0:T(8,128)(2,1)S(1)}, u32[]{:S(2)}, u32[]{:S(2)}) collective-permute-start(bf16[2,96,512]{2,1,0:T(8,128)(2,1)S(1)} %get-tuple-element.75), channel_id=1, source_target_pairs={{0,8},{4,12},{8,0},{12,4},{16,24},{20,28},{24,16},{28,20},{1,9},{5... | collective-permute-start | bytes 589832 | tf_op jit(solution)/shard_map/ppermute | solution.py:39
  177.0 17.9 %collective-permute-start.28 = (bf16[2,96,512]{2,1,0:T(8,128)(2,1)S(1)}, bf16[2,96,512]{2,1,0:T(8,128)(2,1)S(1)}, u32[]{:S(2)}, u32[]{:S(2)}) collective-permute-start(bf16[2,96,512]{2,1,0:T(8,128)(2,1)S(1)} %get-tuple-element.77), channel_id=1, source_target_pairs={{0,8},{4,12},{8,0},{12,4},{16,24},{20,28},{24,16},{28,20},{1,9},{5... | collective-permute-start | bytes 589832 | tf_op jit(solution)/shard_map/ppermute | solution.py:39
  194.7 13.8 %collective-permute-start.24 = (bf16[2,48,512]{2,1,0:T(8,128)(2,1)S(1)}, bf16[2,48,512]{2,1,0:T(8,128)(2,1)S(1)}, u32[]{:S(2)}, u32[]{:S(2)}) collective-permute-start(bf16[2,48,512]{2,1,0:T(8,128)(2,1)S(1)} %get-tuple-element.83), channel_id=1, source_target_pairs={{0,16},{4,20},{8,24},{12,28},{16,0},{20,4},{24,8},{28,12},{1,17},{... | collective-permute-start | bytes 294920 | tf_op jit(solution)/shard_map/ppermute | solution.py:39
  194.9 15.7 %collective-permute-start.29 = (bf16[2,48,512]{2,1,0:T(8,128)(2,1)S(1)}, bf16[2,48,512]{2,1,0:T(8,128)(2,1)S(1)}, u32[]{:S(2)}, u32[]{:S(2)}) collective-permute-start(bf16[2,48,512]{2,1,0:T(8,128)(2,1)S(1)} %get-tuple-element.85), channel_id=1, source_target_pairs={{0,16},{4,20},{8,24},{12,28},{16,0},{20,4},{24,8},{28,12},{1,17},{... | collective-permute-start | bytes 294920 | tf_op jit(solution)/shard_map/ppermute | solution.py:39
  197.9 14.0 %collective-permute-start.34 = (bf16[2,48,512]{2,1,0:T(8,128)(2,1)S(1)}, bf16[2,48,512]{2,1,0:T(8,128)(2,1)S(1)}, u32[]{:S(2)}, u32[]{:S(2)}) collective-permute-start(bf16[2,48,512]{2,1,0:T(8,128)(2,1)S(1)} %get-tuple-element.87), channel_id=1, source_target_pairs={{0,16},{4,20},{8,24},{12,28},{16,0},{20,4},{24,8},{28,12},{1,17},{... | collective-permute-start | bytes 294920 | tf_op jit(solution)/shard_map/ppermute | solution.py:39
  (22 other events, 258.4 us)

commit v2 on v1

v2 whole, which is shorter than its diff:
```python
import functools

import numpy as np
import jax
import jax.numpy as jnp
from jax import lax
from jax.experimental import pallas as pl
from jax.experimental.pallas import tpu as pltpu
from jax.sharding import PartitionSpec as P

HEADS = 16
HD = 128
GROUP = 64
RLEN = 128
PAIR = 2 * HD
CHUNKS = HEADS // 4
SPLIT = 2
VMEM = 60 * 2**20
SCALE = HD ** (-0.5)
LOG2E = 1.4426950408889634
NEG = -1e30
BF = jnp.bfloat16
F32 = jnp.float32
ANY = pl.BlockSpec(memory_space=pl.ANY)

NT = (((1,), (1,)), ((), ()))
TN = (((0,), (0,)), ((), ()))
NN = (((1,), (0,)), ((), ()))


def cost(micros):
    return pl.CostEstimate(flops=int(micros * 1e9), bytes_accessed=1000, transcendentals=0)


def mm(a, b, dims):
    return lax.dot_general(a, b, dims, preferred_element_type=F32)


def shift(value, axis, steps):
    count = lax.axis_size(axis)
    first, last = max(0, -steps), min(count, count - steps)
    return lax.ppermute(value, axis, [(i, i + steps) for i in range(first, last)])


def after(value, *others):
    return lax.optimization_barrier((value, *others))[0]


def swap(value, axis, bit):
    return lax.ppermute(value, axis, [(i, i ^ bit) for i in range(lax.axis_size(axis))])


def count_rows(count_ref, width):
    row = lax.broadcasted_iota(jnp.int32, (16, width), 0)
    tail = jnp.zeros((16, width), F32)
    for u in range(count_ref.shape[0]):
        tail = jnp.where(row == u, count_ref[u].astype(F32), tail)
    return tail.astype(BF)


def pack_kernel(count_ref, nb_ref, out_ref):
    per, enc = nb_ref.shape[1:]
    out_ref[:per, :] = nb_ref[0]
    out_ref[per:, :] = count_rows(count_ref, enc)


def pack(nb, counts):
    groups, per, enc = nb.shape
    return pl.pallas_call(
        pack_kernel,
        grid=(1,),
        in_specs=[
            pl.BlockSpec(memory_space=pltpu.SMEM),
            pl.BlockSpec((1, per, enc), lambda p: (groups - 1, 0, 0)),
        ],
        out_specs=pl.BlockSpec((per + 16, enc), lambda p: (0, 0)),
        out_shape=jax.ShapeDtypeStruct((per + 16, enc), BF),
        compiler_params=pltpu.CompilerParams(vmem_limit_bytes=VMEM),
        cost_estimate=cost(2),
    )(counts, nb)


def cut_kernel(info_ref, count_ref, *refs):
    sources, refs = refs[:6], refs[6:]
    parts, (first_ref, other_ref, pair_ref) = refs[:-3], refs[-3:]
    for which in (0, 1):
        keys, values = sources[2 * which : 2 * which + 2]
        for chunk in range(CHUNKS):
            at = slice(chunk * PAIR, (chunk + 1) * PAIR)
            part = jnp.concatenate([keys[:, at], values[:, at]], 1)
            if which:
                other_ref[chunk] = part
            else:
                parts[chunk][...] = part
            if which and not chunk:
                first_ref[...] = part
    tokens, width = sources[4].shape
    for index in (0, 1):
        pair_ref[index, :tokens, :] = sources[4 + index][...]
        pair_ref[index, tokens:, :] = count_rows(count_ref, width)


def cut(info, counts, weight, cq, do):
    rows = weight.shape[0]
    tokens, width = cq.shape
    whole = lambda p, info: (0, 0)
    part = jax.ShapeDtypeStruct((rows, 2 * PAIR), BF)
    parts = jax.ShapeDtypeStruct((CHUNKS, rows, 2 * PAIR), BF)
    half = jax.ShapeDtypeStruct((2, tokens + 16, width // 2), BF)

    def columns(height, other, value):
        return pl.BlockSpec(
            (height, width // 2), lambda p, info: (0, 2 * value + ((info[0] & 1) ^ other))
        )

    *mine, first, other, pair = pl.pallas_call(
        cut_kernel,
        grid_spec=pltpu.PrefetchScalarGridSpec(
            num_scalar_prefetch=1,
            grid=(1,),
            in_specs=[pl.BlockSpec(memory_space=pltpu.SMEM)]
            + [columns(rows, other, value) for other in (0, 1) for value in (0, 1)]
            + [columns(tokens, 1, 0)] * 2,
            out_specs=[pl.BlockSpec(part.shape, whole)] * (CHUNKS + 1)
            + [pl.BlockSpec(x.shape, lambda p, info: (0, 0, 0)) for x in (parts, half)],
        ),
        out_shape=[part] * (CHUNKS + 1) + [parts, half],
        compiler_params=pltpu.CompilerParams(vmem_limit_bytes=VMEM),
        cost_estimate=cost(3),
    )(info, counts, weight, weight, weight, weight, cq, do)
    return mine, first, other, pair


def stack_kernel(*refs):
    mine, near_ref, outs = refs[: CHUNKS - 1], refs[CHUNKS - 1], refs[CHUNKS:]
    for chunk, (ref, out) in enumerate(zip(mine, outs)):
        rows = ref.shape[0]
        out[:rows, :] = ref[...]
        out[rows:, :] = near_ref[chunk + 1]


def stack(mine, near):
    rows, width = mine[0].shape
    return pl.pallas_call(
        stack_kernel,
        out_shape=[jax.ShapeDtypeStruct((2 * rows, width), BF)] * (CHUNKS - 1),
        compiler_params=pltpu.CompilerParams(vmem_limit_bytes=VMEM),
        cost_estimate=cost(2),
    )(*mine[1:], near)


def join_kernel(first, second, *refs):
    for index, ref in enumerate(refs):
        width = ref.shape[1] // 2
        at = slice(index * width, (index + 1) * width)
        ref[:, :width] = first[:, at]
        ref[:, width:] = second[:, at]


def join(first, second, parts):
    tokens, width = first.shape
    rows = tokens // 4
    return pl.pallas_call(
        join_kernel,
        grid=(4,),
        in_specs=[pl.BlockSpec((rows, width), lambda p: (p, 0))] * 2,
        out_specs=[pl.BlockSpec((rows, 2 * width // parts), lambda p: (p, 0))] * parts,
        out_shape=[jax.ShapeDtypeStruct((tokens, 2 * width // parts), BF)] * parts,
        compiler_params=pltpu.CompilerParams(vmem_limit_bytes=VMEM),
        cost_estimate=cost(2),
    )(first, second)


def cross_kernel(chunk, slot, turns, pieces, info_ref, count_ref, *refs):
    (turn_ref, nb_last, nb_own, peer_last, nb_peer), refs = refs[:5], refs[5:]
    weights, refs = refs[:pieces], refs[pieces:]
    (cq_ref, do_ref, peer_ref), refs = refs[:3], refs[3:]
    refs = refs[len(refs) - 17 - turns :]
    (own_out, peer_out, keep_out, send_out), refs = refs[:4], refs[4:]
    turned_out, refs = (refs[0], refs[1:]) if turns else (None, refs)
    (w_ref, nb_ref, turned_ref, kv_ref, dkv_ref, q_ref, g_ref, tail_ref), refs = refs[:8], refs[8:]
    out_ref, dw_ref, pick_ref, sem, out_sem = refs
    shard = info_ref[0]
    enc = w_ref.shape[0]
    tokens = q_ref.shape[1]
    groups = tokens // GROUP
    per = 2 * RLEN
    size = groups * per
    rows = enc // 4
    loads = []

    def load(source, target):
        copy = pltpu.make_async_copy(source, target, sem.at[len(loads)])
        copy.start()
        loads.append(copy)
        return copy

    waits_w, piece = [], 0
    for ref in weights:
        source = ref.at[chunk] if len(ref.shape) == 3 else ref
        for start in range(0, source.shape[0], rows):
            at = pl.ds(pl.multiple_of((shard ^ piece) * rows, 16), rows)
            waits_w.append(load(source.at[start : start + rows, :], w_ref.at[at, :]))
            piece += 1
    waits_nb = [
        load(nb_last.at[:per, :], nb_ref.at[:per, :]),
        *[load(nb_own.at[u - 1], nb_ref.at[u * per : (u + 1) * per, :]) for u in range(1, groups)],
        load(peer_last.at[:per, :], nb_ref.at[size : size + per, :]),
        *[
            load(nb_peer.at[u - 1], nb_ref.at[size + u * per : size + (u + 1) * per, :])
            for u in range(1, groups)
        ],
    ]
    lanes = pl.ds(pl.multiple_of(((shard & 1) * CHUNKS + chunk) * PAIR, PAIR), PAIR)
    there = slice(chunk * PAIR, (chunk + 1) * PAIR)
    waits_q = [
        load(cq_ref.at[:, lanes], q_ref.at[0]),
        load(do_ref.at[:, lanes], g_ref.at[0]),
        load(peer_ref.at[0, :tokens, there], q_ref.at[1]),
        load(peer_ref.at[1, :tokens, there], g_ref.at[1]),
        load(nb_last.at[per:, : 2 * GROUP], tail_ref.at[0]),
        load(peer_last.at[per:, : 2 * GROUP], tail_ref.at[1]),
        load(peer_ref.at[0, tokens:, : 2 * GROUP], tail_ref.at[2]),
    ]
    wait_turn = load(turn_ref, pick_ref if turns else turned_ref)
    for copy in waits_w:
        copy.wait()
    for file in (0, 1):
        for start, stop in ((0, 1), (1, groups)):
            for copy in waits_nb[file * groups + start : file * groups + stop]:
                copy.wait()
            at = slice(file * size + start * per, file * size + stop * per)
            kv_ref[at, :] = mm(nb_ref[at, :], w_ref[...], NN).astype(BF)
    for copy in waits_q:
        copy.wait()
    zero = jnp.zeros((GROUP, HD), BF)

    def diagonal(block):
        return jnp.concatenate(
            [
                jnp.concatenate([block[:, :HD], zero], 1),
                jnp.concatenate([zero, block[:, HD:]], 1),
            ],
            0,
        )

    row = lax.broadcasted_iota(jnp.int32, (per, 2 * GROUP), 0).astype(F32)
    for file in (0, 1):
        for u in range(groups):
            if u == 0:
                count = tail_ref[file, groups - 1 : groups, :].astype(F32)
            elif file:
                count = tail_ref[2, u - 1 : u, :].astype(F32)
            else:
                count = count_ref[u - 1].astype(F32)
            unit = file * groups + u
            at = slice(unit * per, (unit + 1) * per)
            tok = slice(u * GROUP, (u + 1) * GROUP)
            keys, values = kv_ref[at, :PAIR], kv_ref[at, PAIR:]
            queries, grads = diagonal(q_ref[file, tok, :]), diagonal(g_ref[file, tok, :])
            scores = mm(keys, queries, NT)
            prob_grad = mm(values, grads, NT)
            scores = jnp.where(row < count * RLEN, scores, NEG)
            peak = jnp.max(scores, axis=0, keepdims=True)
            weight = jnp.exp2((scores - peak) * (SCALE * LOG2E))
            total = jnp.sum(weight, axis=0, keepdims=True)
            inverse = jnp.where(count > 0, 1.0 / total, 0.0)
            probs = weight * inverse
            delta = jnp.sum(probs * prob_grad, axis=0, keepdims=True)
            score_grad = (probs * (prob_grad - delta)).astype(BF)
            low = probs.astype(BF)
            out = mm(low, values, TN).astype(BF)
            dq = (mm(score_grad, keys, TN) * SCALE).astype(BF)
            for index, value in enumerate((out, dq)):
                out_ref[file, index, tok, :HD] = value[:GROUP, :HD]
                out_ref[file, index, tok, HD:] = value[GROUP:, HD:]
            dkv_ref[at, :PAIR] = (mm(score_grad, queries, NN) * SCALE).astype(BF)
            dkv_ref[at, PAIR:] = mm(low, grads, NN).astype(BF)
    stores = []

    def store(source, target):
        copy = pltpu.make_async_copy(source, target, out_sem.at[len(stores)])
        copy.start()
        stores.append(copy)

    store(out_ref.at[0], own_out.at[:, :, there])
    store(out_ref.at[1], peer_out.at[:, :, there])
    wait_turn.wait()
    if turns:
        turned_ref[...] = mm(pick_ref[...], nb_ref[...], NT).astype(BF)
        store(turned_ref, turned_out)
    half = enc // 2
    bit = (shard // 2) % 2
    for index, (target, which) in enumerate(((send_out, 1 - bit), (keep_out, bit))):
        at = pl.ds(pl.multiple_of(which * half, 16), half)
        dw_ref[index] = mm(turned_ref[at, :], dkv_ref[...], NN).astype(BF)
        store(dw_ref.at[index], target.at[slot])
    for copy in stores:
        copy.wait()


def cross(chunk, info, counts, turn, nbs, weights, cq, do, peer, crossed, kept):
    tokens, half = peer.shape[1] - 16, peer.shape[2]
    groups, per, enc = nbs[1].shape
    size = 2 * groups * per
    slot = chunk % 2
    turns = chunk == 0
    held = [*crossed, *kept]
    smem = pl.BlockSpec(memory_space=pltpu.SMEM)
    operands = [info, counts, turn, *nbs, *weights, cq, do, peer]
    shapes = [jax.ShapeDtypeStruct((2, tokens, half), BF)] * 2
    shapes += [jax.ShapeDtypeStruct((2, enc // 2, 2 * PAIR), BF)] * 2
    aliases = {len(operands) + i: (i if crossed else 2 + i) for i in range(len(held))}
    if turns:
        shapes.append(jax.ShapeDtypeStruct((enc, size), BF))
    return pl.pallas_call(
        functools.partial(cross_kernel, chunk, slot, int(turns), len(weights)),
        in_specs=[smem, smem] + [ANY] * (len(operands) - 2 + len(held)),
        out_specs=[ANY] * len(shapes),
        out_shape=shapes,
        scratch_shapes=[
            pltpu.VMEM((enc, 2 * PAIR), BF),
            pltpu.VMEM((size, enc), BF),
            pltpu.VMEM((enc, size), BF),
            pltpu.VMEM((size, 2 * PAIR), BF),
            pltpu.VMEM((size, 2 * PAIR), BF),
            pltpu.VMEM((2, tokens, PAIR), BF),
            pltpu.VMEM((2, tokens, PAIR), BF),
            pltpu.VMEM((3, 16, 2 * GROUP), BF),
            pltpu.VMEM((2, 2, tokens, PAIR), BF),
            pltpu.VMEM((2, enc // 2, 2 * PAIR), BF),
            pltpu.VMEM((enc, enc) if turns else (16, 128), BF),
            pltpu.SemaphoreType.DMA((2 * groups + 12,)),
            pltpu.SemaphoreType.DMA((5,)),
        ],
        input_output_aliases=aliases,
        compiler_params=pltpu.CompilerParams(vmem_limit_bytes=VMEM),
        cost_estimate=cost(9),
    )(*operands, *held)


def self_kernel(
    heads, info_ref, q_ref, do_ref, kp_ref, ko_ref, vp_ref, vo_ref, *refs
):
    own_ref, back_ref, out_ref, dq_ref, cross_ref, dk_ref, dv_ref, stat_ref = refs
    first_half = pl.program_id(0) < pl.num_programs(0) // 2
    crossed = jnp.where(first_half, own_ref[0], back_ref[0])
    cross_ref[...] = jnp.where(first_half, own_ref[1], back_ref[1])
    later = info_ref[1] > 0
    tokens = q_ref.shape[0]
    half = tokens // 2
    key_at = lax.broadcasted_iota(jnp.int32, (half, half), 0)
    query_at = lax.broadcasted_iota(jnp.int32, (half, half), 1)
    above = jnp.logical_and(key_at > query_at, later)
    below = key_at <= query_at
    zero = jnp.zeros((half, half), BF)
    lo, hi = slice(0, half), slice(half, None)
    for head in range(heads):
        at = slice(head * HD, (head + 1) * HD)
        queries, grads = q_ref[:, at], do_ref[:, at]
        kp, ko, vp, vo = kp_ref[:, at], ko_ref[:, at], vp_ref[:, at], vo_ref[:, at]
        sp, so = mm(kp, queries, NT), mm(ko, queries, NT)
        gp, go = mm(vp, grads, NT), mm(vo, grads, NT)
        rows = []
        for a in (0, 1):
            if a == 0:
                blocks = (sp[lo, lo], sp[hi, lo], so[lo, lo])
                pgrads = (gp[lo, lo], gp[hi, lo], go[lo, lo])
                middle = jnp.where(later, blocks[1], NEG)
            else:
                blocks = (sp[hi, hi], so[lo, hi], so[hi, hi])
                pgrads = (gp[hi, hi], go[lo, hi], go[hi, hi])
                middle = blocks[1]
            scores = (jnp.where(above, blocks[0], NEG), middle, jnp.where(below, blocks[2], NEG))
            peak = jnp.max(
                jnp.maximum(jnp.maximum(scores[0], scores[1]), scores[2]), axis=0, keepdims=True
            )
            weight = [jnp.exp2((s - peak) * (SCALE * LOG2E)) for s in scores]
            total = jnp.sum(weight[0] + weight[1] + weight[2], axis=0, keepdims=True)
            inverse = 1.0 / total
            probs = [w * inverse for w in weight]
            delta = jnp.sum(
                probs[0] * pgrads[0] + probs[1] * pgrads[1] + probs[2] * pgrads[2],
                axis=0,
                keepdims=True,
            )
            score_grad = [(p * (g - delta)).astype(BF) for p, g in zip(probs, pgrads)]
            rows.append(([p.astype(BF) for p in probs], score_grad))
            lanes = slice(a * half, (a + 1) * half)
            stat_ref[head, 0:1, lanes] = peak * (SCALE * LOG2E) + jnp.log2(total)
            stat_ref[head, 1:2, lanes] = delta

        def spread(which):
            first, second = rows[0][which], rows[1][which]
            before = jnp.concatenate(
                [
                    jnp.concatenate([first[0], zero], 1),
                    jnp.concatenate([first[1], second[0]], 1),
                ],
                0,
            )
            own = jnp.concatenate(
                [
                    jnp.concatenate([first[2], second[1]], 1),
                    jnp.concatenate([zero, second[2]], 1),
                ],
                0,
            )
            return before, own

        (pp, po), (dp, do) = spread(0), spread(1)
        out = mm(pp, vp, TN) + mm(po, vo, TN) + crossed[:, at].astype(F32)
        out_ref[:, at] = out.astype(BF)
        dq_ref[:, at] = ((mm(dp, kp, TN) + mm(do, ko, TN)) * SCALE).astype(BF)
        dk_ref[:, at] = mm(do, queries, NN) * SCALE
        dv_ref[:, at] = mm(po, grads, NN)


def self_part(info, q, do, before, k, v, own, back):
    heads = 2
    tokens, width = q.shape
    steps = width // (heads * HD)
    half = steps // 2
    shape = (tokens, heads * HD)

    def place(p, info):
        return (p + (info[0] & 1) * half) % steps

    spec = pl.BlockSpec(shape, lambda p, info: (0, place(p, info)))
    vp_spec = pl.BlockSpec(shape, lambda p, info: (0, steps + place(p, info)))
    own_spec = pl.BlockSpec((2, *shape), lambda p, info: (0, 0, jnp.minimum(p, half - 1)))
    back_spec = pl.BlockSpec((2, *shape), lambda p, info: (0, 0, jnp.maximum(p - half, 0)))
    stat_spec = pl.BlockSpec((heads, 2, tokens), lambda p, info: (place(p, info), 0, 0))
    full = jax.ShapeDtypeStruct(q.shape, BF)
    wide = jax.ShapeDtypeStruct(q.shape, F32)
    stats = jax.ShapeDtypeStruct((width // HD, 2, tokens), F32)
    return pl.pallas_call(
        functools.partial(self_kernel, heads),
        grid_spec=pltpu.PrefetchScalarGridSpec(
            num_scalar_prefetch=1,
            grid=(steps,),
            in_specs=[spec, spec, spec, spec, vp_spec, spec, own_spec, back_spec],
            out_specs=[spec] * 5 + [stat_spec],
        ),
        out_shape=[full] * 3 + [wide] * 2 + [stats],
        compiler_params=pltpu.CompilerParams(vmem_limit_bytes=VMEM),
        cost_estimate=cost(14),
    )(info, q, do, before, k, before, v, own, back)


def next_kernel(
    heads, q_ref, do_ref, k_ref, v_ref, stat_ref, dkp_ref, dvp_ref, *refs
):
    dk_ref, dv_ref = refs[-2:]
    tokens = q_ref.shape[0]
    half = tokens // 2
    key_at = lax.broadcasted_iota(jnp.int32, (half, half), 0)
    query_at = lax.broadcasted_iota(jnp.int32, (half, half), 1)
    above = key_at > query_at
    zero = jnp.zeros((half, half), BF)
    lo, hi = slice(0, half), slice(half, None)
    for head in range(heads):
        at = slice(head * HD, (head + 1) * HD)
        queries, grads = q_ref[:, at], do_ref[:, at]
        scores = mm(k_ref[:, at], queries, NT)
        prob_grad = mm(v_ref[:, at], grads, NT)
        level, delta = stat_ref[head, 0:1, :], stat_ref[head, 1:2, :]

        def block(rows, lanes, mask):
            exponent = scores[rows, lanes] * (SCALE * LOG2E) - level[:, lanes]
            if mask:
                exponent = jnp.where(above, exponent, NEG)
            probs = jnp.exp2(exponent)
            return probs.astype(BF), (probs * (prob_grad[rows, lanes] - delta[:, lanes])).astype(BF)

        first, middle, last = block(lo, lo, True), block(hi, lo, False), block(hi, hi, True)
        low, score_grad = [
            jnp.concatenate(
                [
                    jnp.concatenate([first[i], zero], 1),
                    jnp.concatenate([middle[i], last[i]], 1),
                ],
                0,
            )
            for i in (0, 1)
        ]
        dk_ref[:, at] = (dkp_ref[:, at] + mm(score_grad, queries, NN) * SCALE).astype(BF)
        dv_ref[:, at] = (dvp_ref[:, at] + mm(low, grads, NN)).astype(BF)


def next_part(part, late, k, v, stats, dk, dv, held):
    heads = 2
    tokens, width = k.shape
    steps = width // (heads * HD) // SPLIT
    shape = (tokens, heads * HD)
    spec = pl.BlockSpec(shape, lambda p: (0, part * steps + p))
    q_spec = pl.BlockSpec(shape, lambda p: (0, p))
    do_spec = pl.BlockSpec(shape, lambda p: (0, steps + p))
    stat_spec = pl.BlockSpec((heads, 2, tokens), lambda p: (part * steps + p, 0, 0))
    full = jax.ShapeDtypeStruct(k.shape, BF)
    return pl.pallas_call(
        functools.partial(next_kernel, heads),
        grid=(steps,),
        in_specs=[q_spec, do_spec, spec, spec, stat_spec, spec, spec] + [ANY] * len(held),
        out_specs=[spec] * 2,
        out_shape=[full] * 2,
        input_output_aliases={7 + i: i for i in range(len(held))},
        compiler_params=pltpu.CompilerParams(vmem_limit_bytes=VMEM),
        cost_estimate=cost(4),
    )(late, late, k, v, stats, dk, dv, *held)


def halving_order(fsdp, seq):
    bits = [("fsdp", 1 << i) for i in range(1, fsdp.bit_length() - 1)]
    seq_bits = [("seq", 1 << i) for i in range(seq.bit_length() - 1)]
    return bits + seq_bits[1:] + seq_bits[:1]


def row_order(fsdp, seq, rows):
    index = np.arange(rows).reshape(seq * fsdp, -1)
    block = np.arange(seq * fsdp)
    keys = []
    for axis, bit in halving_order(fsdp, seq) + [("fsdp", 1)]:
        value = block % fsdp if axis == "fsdp" else block // fsdp
        keys.append((value // bit) % 2)
    order = np.lexsort(keys[::-1])
    return index[order].reshape(-1)


def take_half(value, upper):
    half = value.shape[0] // 2
    return lax.dynamic_slice_in_dim(value, upper * half, half, 0)


def halve_kernel(parts, axis, bit, info_ref, *refs):
    keep_ref, got_ref, mine_ref, other_ref = refs
    half, width = mine_ref.shape
    width //= parts
    upper = (info_ref[0 if axis == "fsdp" else 1] // bit) % 2
    for ref, which in ((mine_ref, upper), (other_ref, 1 - upper)):
        at = pl.ds(pl.multiple_of(which * half, 16), half)
        for part in range(parts):
            total = keep_ref[part, at, :].astype(F32) + got_ref[part, at, :].astype(F32)
            ref[:, part * width : (part + 1) * width] = total.astype(BF)


def halve(info, keep, received, stage):
    axis, bit = stage
    if keep.ndim == 2:
        keep, received = keep[None], received[None]
    parts, rows, width = keep.shape
    shape = (rows // 2, parts * width)
    if shape[0] % 16:
        upper = (info[0 if axis == "fsdp" else 1] // bit) % 2
        total = keep.astype(F32) + received.astype(F32)
        total = total.transpose(1, 0, 2).reshape(rows, parts * width)
        return take_half(total, upper).astype(BF), take_half(total, 1 - upper).astype(BF)
    return pl.pallas_call(
        functools.partial(halve_kernel, parts, axis, bit),
        in_specs=[pl.BlockSpec(memory_space=pltpu.SMEM)]
        + [pl.BlockSpec(memory_space=pltpu.VMEM)] * 2,
        out_shape=[jax.ShapeDtypeStruct(shape, BF)] * 2,
        cost_estimate=cost(1),
    )(info, keep, received)


def on_device(
    self_query, self_key, self_value, cross_query, neighbours, neighbour_count, kv_weight, out_grad
):
    fsdp, seq = lax.axis_size("fsdp"), lax.axis_size("seq")
    shard, slab = lax.axis_index("fsdp"), lax.axis_index("seq")
    q, k, v, cq, do = (x[0] for x in (self_query, self_key, self_value, cross_query, out_grad))
    nb, counts = neighbours[0], neighbour_count[0]
    tokens, width = q.shape
    groups, per, enc = nb.shape
    info = jnp.stack([shard, slab]).astype(jnp.int32)

    last = pack(nb, counts)
    nb_last = shift(last, "seq", 1)

    mine, first, other, pair = cut(after(info, last), counts, kv_weight, cq, do)
    near = swap(other, "fsdp", 1)
    both = stack(mine, near)
    weights = [[mine[0], near]]
    for piece in range(2, fsdp, 2):
        weights[0] += [swap(mine[0], "fsdp", piece), swap(first, "fsdp", piece + 1)]
    for chunk in range(1, CHUNKS):
        weights.append([mine[chunk], near])
        for piece in range(2, fsdp, 2):
            weights[chunk].append(swap(both[chunk - 1], "fsdp", piece))
    nb_peer = swap(after(nb, near), "fsdp", 1)
    peer = swap(pair, "fsdp", 1)
    keyed, = join(k, v, 1)
    nb_last = after(nb_last, both[0], keyed, weights[0][-1], weights[0][-2])
    peer_last = swap(nb_last, "fsdp", 1)
    nbs = [nb_last, nb, peer_last, nb_peer]

    before = shift(after(keyed, nb_last), "seq", 1)

    stages = halving_order(fsdp, seq)
    split_at = fsdp.bit_length() - 2

    turn = jnp.asarray(np.eye(enc)[row_order(fsdp, seq, enc)], BF)
    crossed, pairs = [], []
    for chunk in range(0, CHUNKS, 2):
        kept = []
        for c in (chunk, chunk + 1):
            results = cross(c, info, counts, turn, nbs, weights[c], cq, do, peer, crossed, kept)
            crossed, kept = results[:2], results[2:4]
            if not c:
                turn = results[4]
        keep, send = kept
        received = swap(send, *stages[0])
        for stage in range(1, split_at):
            keep, send = halve(info, keep, received, stages[stage])
            received = swap(send, *stages[stage])
        pairs.append((keep, received))
    own, away = crossed
    back = swap(away, "fsdp", 1)

    asked = join(q, do, SPLIT)
    late = [shift(after(x, pairs[0][0]), "seq", -1) for x in asked]

    halves = [halve(info, *pairs[0], stages[split_at])]
    block_out, query_grad, cross_grad, dk, dv, stats = self_part(
        after(info, halves[0][1]), q, do, before, k, v, own, back
    )
    halves.append(halve(after(info, stats), *pairs[1], stages[split_at]))
    stats_after = shift(stats, "seq", -1)

    done = []
    for keep, send in halves:
        received = swap(send, *stages[split_at])
        for stage in range(split_at + 1, len(stages)):
            keep, send = halve(after(info, stats), keep, received, stages[stage])
            received = swap(send, *stages[stage])
        total = keep.astype(F32) + received.astype(F32)
        core = shard % 2
        away = swap(take_half(total, 1 - core).astype(BF), "fsdp", 1)
        done.append((take_half(total, core), away.astype(F32)))
    columns = [
        jnp.concatenate(
            [
                group[side][:, (2 * c + part) * PAIR : (2 * c + part + 1) * PAIR]
                for group in done
                for c in range(CHUNKS // SPLIT)
            ],
            -1,
        )
        for part in (0, 1)
        for side in (0, 1)
    ]
    key_mine, key_away, value_mine, value_away = columns
    low = shard % 2 == 0
    weight_grad = jnp.concatenate(
        [
            jnp.where(low, key_mine, key_away),
            jnp.where(low, key_away, key_mine),
            jnp.where(low, value_mine, value_away),
            jnp.where(low, value_away, value_mine),
        ],
        -1,
    )

    held = []
    for part in range(SPLIT):
        held = next_part(part, late[part], k, v, stats_after, dk, dv, held)
    key_grad, value_grad = held
    return (
        block_out[None],
        query_grad[None],
        key_grad[None],
        value_grad[None],
        cross_grad[None],
        weight_grad,
    )


def solution(mesh):
    in_specs = (
        P("fsdp", "seq", None),
        P("fsdp", "seq", None),
        P("fsdp", "seq", None),
        P("fsdp", "seq", None),
        P("fsdp", "seq", None, None),
        P("fsdp", "seq"),
        P("fsdp", None),
        P("fsdp", "seq", None),
    )
    out_specs = (
        P("fsdp", "seq", None),
        P("fsdp", "seq", None),
        P("fsdp", "seq", None),
        P("fsdp", "seq", None),
        P("fsdp", "seq", None),
        P(("seq", "fsdp"), None),
    )
    return jax.shard_map(
        on_device, mesh=mesh, in_specs=in_specs, out_specs=out_specs, check_vma=False
    )
```

time: 218 us -> 189 us (0.87)
  starting transfers between devices: 97.4 us -> 33.3 us
  Pallas kernels: 54.5 us -> 98.6 us
  local copies, waits for them, and re-layouts: 26.1 us -> 5.02 us
  waiting for transfers between devices: 31.9 us -> 47.7 us
    pallas_call x6 -> x18, Pallas kernels: 54.5 us -> 98.6 us  [the longest x4 45.2 us: cross(): pl.pallas_call(functools.partial(cross_kernel, chunk, slot, int(turns), l...]
    ppermute x7 -> x5, starting transfers between devices: 50.9 us -> 13.4 us  [shift(): lax.ppermute(value, axis, [(i, i + steps) for i in range(first, last)])]
    ppermute x29 -> x20, starting transfers between devices: 46.6 us -> 19.9 us  [swap(): lax.ppermute(value, axis, [(i, i ^ bit) for i in range(lax.axis_size(axis...]
    ppermute x29 -> x20, waiting for transfers between devices: 24.4 us -> 47.7 us  [swap(): lax.ppermute(value, axis, [(i, i ^ bit) for i in range(lax.axis_size(axis...]
    slice x4, local copies, waits for them, and re-layouts: 14.5 us -> 0.06 us  [on_device(): group[side][:, (2 * c + part) * PAIR:(2 * c + part + 1) * PAIR]]
    ppermute x7 -> x5, waiting for transfers between devices: 7.52 us -> 0.01 us  [shift(): lax.ppermute(value, axis, [(i, i + steps) for i in range(first, last)])]
    reshape x2 -> x0, local copies, waits for them, and re-layouts: 4.65 us -> none  [the longest x1 3.88 us: on_device(): columns = kv_weight.reshape(rows, 2, CHUNKS, per)]
    unnamed x24 -> x26, local copies, waits for them, and re-layouts: 5.23 us -> 4.93 us
  transfers between devices with their start and end apart: 36 -> 25, of which waited for: 12 -> 8; matrix products, arithmetic and copies ran while one was open for 14% -> 0% of each run, Pallas kernels for 25% -> 49%
where the time goes in v2:
time: 189 us; the launch traced here: 188 us
  Pallas kernels  98.6 us (52%)
  waiting for transfers between devices  47.7 us (25%)
  starting transfers between devices  33.3 us (18%)
  local copies, waits for them, and re-layouts  5.02 us (3%)
  other arithmetic  2.33 us (1%)
    ppermute x20, waiting for transfers between devices, swap(): lax.ppermute(value, axis, [(i, i ^ bit) for i in range(lax.axis_size(axis...  47.7 us
    pallas_call x4, Pallas kernels, cross(): pl.pallas_call(functools.partial(cross_kernel, chunk, slot, int(turns), l...  45.2 us
    ppermute x20, starting transfers between devices, swap(): lax.ppermute(value, axis, [(i, i ^ bit) for i in range(lax.axis_size(axis...  19.9 us
    pallas_call x1, Pallas kernels, self_part(): pl.pallas_call(functools.partial(self_kernel, heads), grid_spec=pltpu.Pre...  14.9 us
    ppermute x5, starting transfers between devices, shift(): lax.ppermute(value, axis, [(i, i + steps) for i in range(first, last)])  13.4 us
    pallas_call x6, Pallas kernels, halve(): pl.pallas_call(functools.partial(halve_kernel, parts, axis, bit), in_spec...  12.2 us
    pallas_call x2, Pallas kernels, next_part(): pl.pallas_call(functools.partial(next_kernel, heads), grid=(steps,), in_s...  10.4 us
    pallas_call x2, Pallas kernels, join(): pl.pallas_call(join_kernel, grid=(4,), in_specs=[pl.BlockSpec((rows, widt...  7.58 us
  transfers between devices with their start and end apart: 25, of which 8 were waited for; matrix products, arithmetic and copies ran while one was open for 0% of the time, Pallas kernels for 49%

profile of v2, /device:TPU:0, one launch (start us, length us, event | category | flops | bytes accessed | tf_op | source)
XLA Modules:
  0.0 187.9 jit_solution(17196474009611347090)
XLA Ops:
  3.0 4.0 %shard_map.137 = (bf16[192,512]{1,0:T(8,128)(2,1)}, bf16[192,512]{1,0:T(8,128)(2,1)}, bf16[192,512]{1,0:T(8,128)(2,1)}, bf16[192,512]{1,0:T(8,128)(2,1)}, bf16[1...) custom-call(s32[2]{0:T(128)} %pad_add_fusion.info_ref, s32[4]{0:T(128)} %bitcast.49, ...), custom_call_target="tpu_custom_call" | custom-call | flops 3000000000 | bytes 1000 | tf_op jit(solution)/shard_map/pallas_call | solution.py:116
  7.4 2.1 %collective-permute-done.1.refs_3_.refs_6_ = bf16[4,192,512]{2,1,0:T(8,128)(2,1)S(1)} collective-permute-done((bf16[4,192,512]{2,1,0:T(8,128)(2,1)}, bf16[4,192,512]{2,1,0:T(8,128)(2,1)S(1)}, u32[]{:S(2)}, u32[]{:S(2)}) %collective-permute-start.1) | collective-permute-done | bytes 786464 | tf_op jit(solution)/shard_map/ppermute | solution.py:50
  10.8 4.6 %collective-permute-start = (bf16[272,768]{1,0:T(8,128)(2,1)}, bf16[272,768]{1,0:T(8,128)(2,1)S(1)}, u32[]{:S(2)}, u32[]{:S(2)}) collective-permute-start(bf16[272,768]{1,0:T(8,128)(2,1)} %shard_map.136), channel_id=1, source_target_pairs={{0,4},{4,8},{8,12},{12,16},{16,20},{20,24},{24,28},{1,5},{5,9},{9,... | collective-permute-start | bytes 1253384 | tf_op jit(solution)/shard_map/ppermute | solution.py:42
  16.9 3.8 %shard_map.139 = bf16[256,4096]{1,0:T(8,128)(2,1)} custom-call(bf16[256,2048]{1,0:T(8,128)(2,1)} %bitcast.36, bf16[256,2048]{1,0:T(8,128)(2,1)} %bitcast.40), custom_call_target="tpu_custom_call" | custom-call | flops 2000000000 | bytes 1000 | tf_op jit(solution)/shard_map/pallas_call | solution.py:163
  20.7 2.6 %shard_map.138 = (bf16[384,512]{1,0:T(8,128)(2,1)}, bf16[384,512]{1,0:T(8,128)(2,1)}, bf16[384,512]{1,0:T(8,128)(2,1)}) custom-call(bf16[192,512]{1,0:T(8,128)(2,1)} %get-tuple-element.66.refs_0_.refs_5_, bf16[192,512]{1,0:T(8,128)(2,1)} %get-tuple-element.67.refs_1_.refs_5_, bf16[192,512]{1,0:T(8,128)(2,1)} %get-tuple-element.68.refs_2_.refs_5_, ...), custom_call_target="tpu_custom_call" | custom-call | flops 2000000000 | bytes 1000 | tf_op jit(solution)/shard_map/pallas_call | solution.py:144
  23.4 2.6 %collective-permute-done.2.refs_8_ = bf16[192,512]{1,0:T(8,128)(2,1)} collective-permute-done((bf16[192,512]{1,0:T(8,128)(2,1)}, bf16[192,512]{1,0:T(8,128)(2,1)}, u32[]{:S(2)}, u32[]{:S(2)}) %collective-permute-start.2) | collective-permute-done | bytes 196640 | tf_op jit(solution)/shard_map/ppermute | solution.py:50
  30.2 4.7 %collective-permute-start.9 = (bf16[256,4096]{1,0:T(8,128)(2,1)S(1)}, bf16[256,4096]{1,0:T(8,128)(2,1)}, u32[]{:S(2)}, u32[]{:S(2)}) collective-permute-start(bf16[256,4096]{1,0:T(8,128)(2,1)S(1)} %copy-done.1), channel_id=1, source_target_pairs={{0,4},{4,8},{8,12},{12,16},{16,20},{20,24},{24,28},{1,5},{5,9},{9,... | collective-permute-start | bytes 6291464 | tf_op jit(solution)/shard_map/ppermute | solution.py:42
  35.0 13.1 %shard_map.140 = (bf16[2,256,1024]{2,1,0:T(8,128)(2,1)}, bf16[2,256,1024]{2,1,0:T(8,128)(2,1)}, bf16[2,384,512]{2,1,0:T(8,128)(2,1)}, bf16[2,384,512]{2,1,0:T(8,128)(2,1)}, bf16[768,2048]{1,0:T(8,128)(2,1)}) custom-call(s32[2]{0:T(128)} %pad_add_fusion.info_ref, s32[4]{0:T(128)} %bitcast.50, bf16[768,768]{1,0:T(8,128)(2,1)} %constant.34.clone.refs_0_, ...), custom_call_target="tpu_custom_call" | custom-call | flops 8999999488 | bytes 1000 | tf_op jit(solution)/shard_map/pallas_call | solution.py:316
  48.1 10.6 %shard_map.141 = (bf16[2,256,1024]{2,1,0:T(8,128)(2,1)}, bf16[2,256,1024]{2,1,0:T(8,128)(2,1)}, bf16[2,384,512]{2,1,0:T(8,128)(2,1)}, bf16[2,384,512]{2,1,0:T(8,128)(2,1)}) custom-call(s32[2]{0:T(128)} %pad_add_fusion.info_ref, s32[4]{0:T(128)} %bitcast.51, ...), custom_call_target="tpu_custom_call", output_to_operand_aliasing={{0}: (13, {}), {1}: (14, {}), {2}: (15, {}), {3}: (16, {})} | custom-call | flops 8999999488 | bytes 1000 | tf_op jit(solution)/shard_map/pallas_call | solution.py:316
  58.8 10.8 %shard_map.143 = (bf16[2,256,1024]{2,1,0:T(8,128)(2,1)}, bf16[2,256,1024]{2,1,0:T(8,128)(2,1)}, bf16[2,384,512]{2,1,0:T(8,128)(2,1)}, bf16[2,384,512]{2,1,0:T(8,128)(2,1)}) custom-call(s32[2]{0:T(128)} %pad_add_fusion.info_ref, s32[4]{0:T(128)} %bitcast.52, ...), custom_call_target="tpu_custom_call", output_to_operand_aliasing={{0}: (13, {}), {1}: (14, {})} | custom-call | flops 8999999488 | bytes 1000 | tf_op jit(solution)/shard_map/pallas_call | solution.py:316
  69.6 10.7 %shard_map.144 = (bf16[2,256,1024]{2,1,0:T(8,128)(2,1)}, bf16[2,256,1024]{2,1,0:T(8,128)(2,1)}, bf16[2,384,512]{2,1,0:T(8,128)(2,1)}, bf16[2,384,512]{2,1,0:T(8,128)(2,1)}) custom-call(s32[2]{0:T(128)} %pad_add_fusion.info_ref, s32[4]{0:T(128)} %bitcast.53, ...), custom_call_target="tpu_custom_call", output_to_operand_aliasing={{0}: (13, {}), {1}: (14, {}), {2}: (15, {}), {3}: (16, {})} | custom-call | flops 8999999488 | bytes 1000 | tf_op jit(solution)/shard_map/pallas_call | solution.py:316
  81.0 3.8 %shard_map.146 = (bf16[256,2048]{1,0:T(8,128)(2,1)}, bf16[256,2048]{1,0:T(8,128)(2,1)}) custom-call(bf16[256,2048]{1,0:T(8,128)(2,1)} %bitcast.27, bf16[256,2048]{1,0:T(8,128)(2,1)} %bitcast.34), custom_call_target="tpu_custom_call" | custom-call | flops 2000000000 | bytes 1000 | tf_op jit(solution)/shard_map/pallas_call | solution.py:163
  87.6 13.5 %collective-permute-done.8.refs_1_ = bf16[2,384,512]{2,1,0:T(8,128)(2,1)} collective-permute-done((bf16[2,384,512]{2,1,0:T(8,128)(2,1)}, bf16[2,384,512]{2,1,0:T(8,128)(2,1)}, u32[]{:S(2)}, u32[]{:S(2)}) %collective-permute-start.8) | collective-permute-done | bytes 786464 | tf_op jit(solution)/shard_map/ppermute | solution.py:50
  102.6 2.4 %shard_map.142 = (bf16[192,1024]{1,0:T(8,128)(2,1)}, bf16[192,1024]{1,0:T(8,128)(2,1)}) custom-call(s32[2]{0:T(128)} %pad_add_fusion.info_ref, bf16[2,384,512]{2,1,0:T(8,128)(2,1)} %get-tuple-element.81.refs_0_, bf16[2,384,512]{2,1,0:T(8,128)(2,1)} %collective-permute-done.8.refs_1_), custom_call_target="tpu_custom_call" | custom-call | flops 1000000000 | bytes 1000 | tf_op jit(solution)/shard_map/pallas_call | solution.py:558
  105.0 2.5 %collective-permute-start.16 = (bf16[192,1024]{1,0:T(8,128)(2,1)}, bf16[192,1024]{1,0:T(8,128)(2,1)S(1)}, u32[]{:S(2)}, u32[]{:S(2)}) collective-permute-start(bf16[192,1024]{1,0:T(8,128)(2,1)} %get-tuple-element.83), channel_id=1, source_target_pairs={{0,8},{4,12},{8,0},{12,4},{16,24},{20,28},{24,16},{28,20},{1,9},{5... | collective-permute-start | bytes 1179656 | tf_op jit(solution)/shard_map/ppermute | solution.py:50
  108.5 14.9 %shard_map.145 = (bf16[256,2048]{1,0:T(8,128)(2,1)}, bf16[256,2048]{1,0:T(8,128)(2,1)}, bf16[256,2048]{1,0:T(8,128)(2,1)}, f32[256,2048]{1,0:T(8,128)}, f32[256,2048]{1,0:T(8,128)}, /*index=5*/f32[16,2,256]{2,1,0:T(2,128)}) custom-call(s32[2]{0:T(128)} %pad_add_fusion.info_ref, bf16[256,2048]{1,0:T(8,128)(2,1)} %bitcast.28, bf16[256,2048]{1,0:T(8,128)(2,1)} %bitcast.35, ...), custom_call_target="tpu_custom_call" | custom-call | flops 14000000000 | bytes 1000 | tf_op jit(solution)/shard_map/pallas_call | solution.py:437
  124.7 2.4 %shard_map.151 = (bf16[192,1024]{1,0:T(8,128)(2,1)}, bf16[192,1024]{1,0:T(8,128)(2,1)}) custom-call(s32[2]{0:T(128)} %pad_add_fusion.info_ref, bf16[2,384,512]{2,1,0:T(8,128)(2,1)} %get-tuple-element.116.refs_0_, bf16[2,384,512]{2,1,0:T(8,128)(2,1)} %collective-permute-done.19.refs_1_), custom_call_target="tpu_custom_call" | custom-call | flops 1000000000 | bytes 1000 | tf_op jit(solution)/shard_map/pallas_call | solution.py:558
  127.0 2.5 %collective-permute-start.20 = (bf16[192,1024]{1,0:T(8,128)(2,1)}, bf16[192,1024]{1,0:T(8,128)(2,1)S(1)}, u32[]{:S(2)}, u32[]{:S(2)}) collective-permute-start(bf16[192,1024]{1,0:T(8,128)(2,1)} %get-tuple-element.119), channel_id=1, source_target_pairs={{0,8},{4,12},{8,0},{12,4},{16,24},{20,28},{24,16},{28,20},{1,9},{5... | collective-permute-start | bytes 1179656 | tf_op jit(solution)/shard_map/ppermute | solution.py:50
  129.5 15.6 %collective-permute-done.16 = bf16[192,1024]{1,0:T(8,128)(2,1)S(1)} collective-permute-done((bf16[192,1024]{1,0:T(8,128)(2,1)}, bf16[192,1024]{1,0:T(8,128)(2,1)S(1)}, u32[]{:S(2)}, u32[]{:S(2)}) %collective-permute-start.16) | collective-permute-done | bytes 393248 | tf_op jit(solution)/shard_map/ppermute | solution.py:50
  147.8 2.6 %collective-permute-start.17 = (bf16[96,1024]{1,0:T(8,128)(2,1)}, bf16[96,1024]{1,0:T(8,128)(2,1)S(1)}, u32[]{:S(2)}, u32[]{:S(2)}) collective-permute-start(bf16[96,1024]{1,0:T(8,128)(2,1)} %get-tuple-element.113), channel_id=1, source_target_pairs={{0,16},{4,20},{8,24},{12,28},{16,0},{20,4},{24,8},{28,12},{1,17},{... | collective-permute-start | bytes 589832 | tf_op jit(solution)/shard_map/ppermute | solution.py:50
  151.0 5.2 %shard_map.147 = (bf16[256,2048]{1,0:T(8,128)(2,1)}, bf16[256,2048]{1,0:T(8,128)(2,1)}) custom-call(bf16[256,2048]{1,0:T(8,128)(2,1)} %collective-permute-done.15.q_ref.do_ref, bf16[256,2048]{1,0:T(8,128)(2,1)} %collective-permute-done.15.q_ref.do_ref, bf16[256,2048]{1,0:T(8,128)(2,1)} %bitcast.38, bf16[256,2048]{1,0:T(8,128)(2,1)} %bitcast.42, ...), custom_call_target="tpu_custom_call" | custom-call | flops 4000000000 | bytes 1000 | tf_op jit(solution)/shard_map/pallas_call | solution.py:501
  158.6 5.2 %shard_map.148 = (bf16[256,2048]{1,0:T(8,128)(2,1)}, bf16[256,2048]{1,0:T(8,128)(2,1)}) custom-call(bf16[256,2048]{1,0:T(8,128)(2,1)} %collective-permute-done.13.q_ref.do_ref, bf16[256,2048]{1,0:T(8,128)(2,1)} %collective-permute-done.13.q_ref.do_ref, bf16[256,2048]{1,0:T(8,128)(2,1)} %bitcast.39, ...), custom_call_target="tpu_custom_call", output_to_operand_aliasing={{0}: (7, {}), {1}: (8, {})} | custom-call | flops 4000000000 | bytes 1000 | tf_op jit(solution)/shard_map/pallas_call | solution.py:501
  167.8 9.7 %collective-permute-done.21 = bf16[96,1024]{1,0:T(8,128)(2,1)S(1)} collective-permute-done((bf16[96,1024]{1,0:T(8,128)(2,1)}, bf16[96,1024]{1,0:T(8,128)(2,1)S(1)}, u32[]{:S(2)}, u32[]{:S(2)}) %collective-permute-start.21) | collective-permute-done | bytes 196640 | tf_op jit(solution)/shard_map/ppermute | solution.py:50
  182.0 2.8 %collective-permute-done.22 = bf16[48,1024]{1,0:T(8,128)(2,1)S(1)} collective-permute-done((bf16[48,1024]{1,0:T(8,128)(2,1)}, bf16[48,1024]{1,0:T(8,128)(2,1)S(1)}, u32[]{:S(2)}, u32[]{:S(2)}) %collective-permute-start.22) | collective-permute-done | bytes 98336 | tf_op jit(solution)/shard_map/ppermute | solution.py:50
  (82 shorter events, 34.3 us)
Async XLA Ops:
  7.0 2.6 %collective-permute-start.1 = (bf16[4,192,512]{2,1,0:T(8,128)(2,1)}, bf16[4,192,512]{2,1,0:T(8,128)(2,1)S(1)}, u32[]{:S(2)}, u32[]{:S(2)}) collective-permute-start(bf16[4,192,512]{2,1,0:T(8,128)(2,1)} %get-tuple-element.69), channel_id=1, source_target_pairs={{0,1},{1,0},{2,3},{3,2},{4,5},{5,4},{6,7},{7,6},{8,9},{9,8},{10,11... | collective-permute-start | bytes 2359304 | tf_op jit(solution)/shard_map/ppermute | solution.py:50
  9.5 25.4 %collective-permute-start.5 = (bf16[4,256,768]{2,1,0:T(8,128)(2,1)}, bf16[4,256,768]{2,1,0:T(8,128)(2,1)}, u32[]{:S(2)}, u32[]{:S(2)}) collective-permute-start(bf16[4,256,768]{2,1,0:T(8,128)(2,1)} %bitcast.3.nb_ref.refs_2_), channel_id=1, source_target_pairs={{0,1},{1,0},{2,3},{3,2},{4,5},{5,4},{6,7},{7,6},{8,9},{9,8},{10,11... | collective-permute-start | bytes 4718600 | tf_op jit(solution)/shard_map/ppermute | solution.py:50
  10.4 18.3 %collective-permute-start.6 = (bf16[2,272,1024]{2,1,0:T(8,128)(2,1)}, bf16[2,272,1024]{2,1,0:T(8,128)(2,1)S(1)}, u32[]{:S(2)}, u32[]{:S(2)}) collective-permute-start(bf16[2,272,1024]{2,1,0:T(8,128)(2,1)} %get-tuple-element.75), channel_id=1, source_target_pairs={{0,1},{1,0},{2,3},{3,2},{4,5},{5,4},{6,7},{7,6},{8,9},{9,8},{10,11... | collective-permute-start | bytes 3342344 | tf_op jit(solution)/shard_map/ppermute | solution.py:50
  10.8 15.2 %collective-permute-start = (bf16[272,768]{1,0:T(8,128)(2,1)}, bf16[272,768]{1,0:T(8,128)(2,1)S(1)}, u32[]{:S(2)}, u32[]{:S(2)}) collective-permute-start(bf16[272,768]{1,0:T(8,128)(2,1)} %shard_map.136), channel_id=1, source_target_pairs={{0,4},{4,8},{8,12},{12,16},{16,20},{20,24},{24,28},{1,5},{5,9},{9,... | collective-permute-start | bytes 1253384 | tf_op jit(solution)/shard_map/ppermute | solution.py:42
  15.4 8.0 %collective-permute-start.3 = (bf16[192,512]{1,0:T(8,128)(2,1)}, bf16[192,512]{1,0:T(8,128)(2,1)S(1)}, u32[]{:S(2)}, u32[]{:S(2)}) collective-permute-start(bf16[192,512]{1,0:T(8,128)(2,1)} %get-tuple-element.72.refs_5_), channel_id=1, source_target_pairs={{0,2},{1,3},{2,0},{3,1},{4,6},{5,7},{6,4},{7,5},{8,10},{9,11},{10,... | collective-permute-start | bytes 589832 | tf_op jit(solution)/shard_map/ppermute | solution.py:50
  16.9 9.0 %collective-permute-start.2 = (bf16[192,512]{1,0:T(8,128)(2,1)}, bf16[192,512]{1,0:T(8,128)(2,1)}, u32[]{:S(2)}, u32[]{:S(2)}) collective-permute-start(bf16[192,512]{1,0:T(8,128)(2,1)} %get-tuple-element.71), channel_id=1, source_target_pairs={{0,3},{1,2},{2,1},{3,0},{4,7},{5,6},{6,5},{7,4},{8,11},{9,10},{10,... | collective-permute-start | bytes 589832 | tf_op jit(solution)/shard_map/ppermute | solution.py:50
  26.0 4.2 %collective-permute-start.4 = (bf16[272,768]{1,0:T(8,128)(2,1)S(1)}, bf16[272,768]{1,0:T(8,128)(2,1)S(1)}, u32[]{:S(2)}, u32[]{:S(2)}) collective-permute-start(bf16[272,768]{1,0:T(8,128)(2,1)S(1)} %collective-permute-done.refs_1_), channel_id=1, source_target_pairs={{0,1},{1,0},{2,3},{3,2},{4,5},{5,4},{6,7},{7,6},{8,9},{9,8},{10,11... | collective-permute-start | bytes 1253384 | tf_op jit(solution)/shard_map/ppermute | solution.py:50
  26.7 21.4 %collective-permute-start.7 = (bf16[384,512]{1,0:T(8,128)(2,1)}, bf16[384,512]{1,0:T(8,128)(2,1)}, u32[]{:S(2)}, u32[]{:S(2)}) collective-permute-start(bf16[384,512]{1,0:T(8,128)(2,1)} %get-tuple-element.70), channel_id=1, source_target_pairs={{0,2},{1,3},{2,0},{3,1},{4,6},{5,7},{6,4},{7,5},{8,10},{9,11},{10,... | collective-permute-start | bytes 1179656 | tf_op jit(solution)/shard_map/ppermute | solution.py:50
  28.2 30.6 %collective-permute-start.11 = (bf16[384,512]{1,0:T(8,128)(2,1)}, bf16[384,512]{1,0:T(8,128)(2,1)}, u32[]{:S(2)}, u32[]{:S(2)}) collective-permute-start(bf16[384,512]{1,0:T(8,128)(2,1)} %get-tuple-element.87), channel_id=1, source_target_pairs={{0,2},{1,3},{2,0},{3,1},{4,6},{5,7},{6,4},{7,5},{8,10},{9,11},{10,... | collective-permute-start | bytes 1179656 | tf_op jit(solution)/shard_map/ppermute | solution.py:50
  28.7 40.9 %collective-permute-start.10 = (bf16[384,512]{1,0:T(8,128)(2,1)}, bf16[384,512]{1,0:T(8,128)(2,1)}, u32[]{:S(2)}, u32[]{:S(2)}) collective-permute-start(bf16[384,512]{1,0:T(8,128)(2,1)} %get-tuple-element.86), channel_id=1, source_target_pairs={{0,2},{1,3},{2,0},{3,1},{4,6},{5,7},{6,4},{7,5},{8,10},{9,11},{10,... | collective-permute-start | bytes 1179656 | tf_op jit(solution)/shard_map/ppermute | solution.py:50
  30.2 74.8 %collective-permute-start.9 = (bf16[256,4096]{1,0:T(8,128)(2,1)S(1)}, bf16[256,4096]{1,0:T(8,128)(2,1)}, u32[]{:S(2)}, u32[]{:S(2)}) collective-permute-start(bf16[256,4096]{1,0:T(8,128)(2,1)S(1)} %copy-done.1), channel_id=1, source_target_pairs={{0,4},{4,8},{8,12},{12,16},{16,20},{20,24},{24,28},{1,5},{5,9},{9,... | collective-permute-start | bytes 6291464 | tf_op jit(solution)/shard_map/ppermute | solution.py:42
  80.3 27.2 %collective-permute-start.12 = (bf16[2,256,1024]{2,1,0:T(8,128)(2,1)}, bf16[2,256,1024]{2,1,0:T(8,128)(2,1)S(1)}, u32[]{:S(2)}, u32[]{:S(2)}) collective-permute-start(bf16[2,256,1024]{2,1,0:T(8,128)(2,1)} %get-tuple-element.95), channel_id=1, source_target_pairs={{0,1},{1,0},{2,3},{3,2},{4,5},{5,4},{6,7},{7,6},{8,9},{9,8},{10,11... | collective-permute-start | bytes 3145736 | tf_op jit(solution)/shard_map/ppermute | solution.py:50
  80.4 20.7 %collective-permute-start.8 = (bf16[2,384,512]{2,1,0:T(8,128)(2,1)}, bf16[2,384,512]{2,1,0:T(8,128)(2,1)}, u32[]{:S(2)}, u32[]{:S(2)}) collective-permute-start(bf16[2,384,512]{2,1,0:T(8,128)(2,1)} %get-tuple-element.82), channel_id=1, source_target_pairs={{0,2},{1,3},{2,0},{3,1},{4,6},{5,7},{6,4},{7,5},{8,10},{9,11},{10,... | collective-permute-start | bytes 2359304 | tf_op jit(solution)/shard_map/ppermute | solution.py:50
  84.8 39.9 %collective-permute-start.19 = (bf16[2,384,512]{2,1,0:T(8,128)(2,1)}, bf16[2,384,512]{2,1,0:T(8,128)(2,1)}, u32[]{:S(2)}, u32[]{:S(2)}) collective-permute-start(bf16[2,384,512]{2,1,0:T(8,128)(2,1)} %get-tuple-element.117), channel_id=1, source_target_pairs={{0,2},{1,3},{2,0},{3,1},{4,6},{5,7},{6,4},{7,5},{8,10},{9,11},{10,... | collective-permute-start | bytes 2359304 | tf_op jit(solution)/shard_map/ppermute | solution.py:50
  86.3 64.1 %collective-permute-start.15 = (bf16[256,2048]{1,0:T(8,128)(2,1)}, bf16[256,2048]{1,0:T(8,128)(2,1)}, u32[]{:S(2)}, u32[]{:S(2)}) collective-permute-start(bf16[256,2048]{1,0:T(8,128)(2,1)} %get-tuple-element.104), channel_id=1, source_target_pairs={{4,0},{8,4},{12,8},{16,12},{20,16},{24,20},{28,24},{5,1},{9,5},{13... | collective-permute-start | bytes 3145736 | tf_op jit(solution)/shard_map/ppermute | solution.py:42
  101.1 57.5 %collective-permute-start.13 = (bf16[256,2048]{1,0:T(8,128)(2,1)}, bf16[256,2048]{1,0:T(8,128)(2,1)}, u32[]{:S(2)}, u32[]{:S(2)}) collective-permute-start(bf16[256,2048]{1,0:T(8,128)(2,1)} %get-tuple-element.99), channel_id=1, source_target_pairs={{4,0},{8,4},{12,8},{16,12},{20,16},{24,20},{28,24},{5,1},{9,5},{13... | collective-permute-start | bytes 3145736 | tf_op jit(solution)/shard_map/ppermute | solution.py:42
  105.0 40.1 %collective-permute-start.16 = (bf16[192,1024]{1,0:T(8,128)(2,1)}, bf16[192,1024]{1,0:T(8,128)(2,1)S(1)}, u32[]{:S(2)}, u32[]{:S(2)}) collective-permute-start(bf16[192,1024]{1,0:T(8,128)(2,1)} %get-tuple-element.83), channel_id=1, source_target_pairs={{0,8},{4,12},{8,0},{12,4},{16,24},{20,28},{24,16},{28,20},{1,9},{5... | collective-permute-start | bytes 1179656 | tf_op jit(solution)/shard_map/ppermute | solution.py:50
  123.3 27.0 %collective-permute-start.14 = (f32[16,2,256]{2,1,0:T(2,128)}, f32[16,2,256]{2,1,0:T(2,128)S(1)}, u32[]{:S(2)}, u32[]{:S(2)}) collective-permute-start(f32[16,2,256]{2,1,0:T(2,128)} %get-tuple-element.100), channel_id=1, source_target_pairs={{4,0},{8,4},{12,8},{16,12},{20,16},{24,20},{28,24},{5,1},{9,5},{13... | collective-permute-start | bytes 98312 | tf_op jit(solution)/shard_map/ppermute | solution.py:42
  127.0 36.8 %collective-permute-start.20 = (bf16[192,1024]{1,0:T(8,128)(2,1)}, bf16[192,1024]{1,0:T(8,128)(2,1)S(1)}, u32[]{:S(2)}, u32[]{:S(2)}) collective-permute-start(bf16[192,1024]{1,0:T(8,128)(2,1)} %get-tuple-element.119), channel_id=1, source_target_pairs={{0,8},{4,12},{8,0},{12,4},{16,24},{20,28},{24,16},{28,20},{1,9},{5... | collective-permute-start | bytes 1179656 | tf_op jit(solution)/shard_map/ppermute | solution.py:50
  147.8 8.4 %collective-permute-start.17 = (bf16[96,1024]{1,0:T(8,128)(2,1)}, bf16[96,1024]{1,0:T(8,128)(2,1)S(1)}, u32[]{:S(2)}, u32[]{:S(2)}) collective-permute-start(bf16[96,1024]{1,0:T(8,128)(2,1)} %get-tuple-element.113), channel_id=1, source_target_pairs={{0,16},{4,20},{8,24},{12,28},{16,0},{20,4},{24,8},{28,12},{1,17},{... | collective-permute-start | bytes 589832 | tf_op jit(solution)/shard_map/ppermute | solution.py:50
  158.6 9.1 %collective-permute-start.18 = (bf16[48,1024]{1,0:T(8,128)(2,1)}, bf16[48,1024]{1,0:T(8,128)(2,1)S(1)}, u32[]{:S(2)}, u32[]{:S(2)}) collective-permute-start(bf16[48,1024]{1,0:T(8,128)(2,1)} %get-tuple-element.115), channel_id=1, source_target_pairs={{0,4},{4,0},{8,12},{12,8},{16,20},{20,16},{24,28},{28,24},{1,5},{5... | collective-permute-start | bytes 294920 | tf_op jit(solution)/shard_map/ppermute | solution.py:50
  166.6 11.0 %collective-permute-start.21 = (bf16[96,1024]{1,0:T(8,128)(2,1)}, bf16[96,1024]{1,0:T(8,128)(2,1)S(1)}, u32[]{:S(2)}, u32[]{:S(2)}) collective-permute-start(bf16[96,1024]{1,0:T(8,128)(2,1)} %get-tuple-element.121), channel_id=1, source_target_pairs={{0,16},{4,20},{8,24},{12,28},{16,0},{20,4},{24,8},{28,12},{1,17},{... | collective-permute-start | bytes 589832 | tf_op jit(solution)/shard_map/ppermute | solution.py:50
  167.7 14.3 %collective-permute-start.23 = (bf16[24,1024]{1,0:T(8,128)(2,1)S(1)}, bf16[24,1024]{1,0:T(8,128)(2,1)S(1)}, u32[]{:S(2)}, u32[]{:S(2)}) collective-permute-start(bf16[24,1024]{1,0:T(8,128)(2,1)S(1)} %dynamic-slice_convert_fusion.1), channel_id=1, source_target_pairs={{0,1},{1,0},{2,3},{3,2},{4,5},{5,4},{6,7},{7,6},{8,9},{9,8},{10,11... | collective-permute-start | bytes 147464 | tf_op jit(solution)/shard_map/ppermute | solution.py:50
  180.0 4.8 %collective-permute-start.22 = (bf16[48,1024]{1,0:T(8,128)(2,1)}, bf16[48,1024]{1,0:T(8,128)(2,1)S(1)}, u32[]{:S(2)}, u32[]{:S(2)}) collective-permute-start(bf16[48,1024]{1,0:T(8,128)(2,1)} %get-tuple-element.123), channel_id=1, source_target_pairs={{0,4},{4,0},{8,12},{12,8},{16,20},{20,16},{24,28},{28,24},{1,5},{5... | collective-permute-start | bytes 294920 | tf_op jit(solution)/shard_map/ppermute | solution.py:50
  (14 other events, 50.7 us)

commit v3 on v2

v3 whole, which is shorter than its diff:
```python
import functools

import numpy as np
import jax
import jax.numpy as jnp
from jax import lax
from jax.experimental import pallas as pl
from jax.experimental.pallas import tpu as pltpu
from jax.sharding import PartitionSpec as P

HEADS = 16
HD = 128
GROUP = 64
RLEN = 128
PAIR = 2 * HD
CHUNKS = HEADS // 4
TOGETHER = 2
VMEM = 60 * 2**20
SCALE = HD ** (-0.5)
LOG2E = 1.4426950408889634
NEG = -1e30
BF = jnp.bfloat16
F32 = jnp.float32
ANY = pl.BlockSpec(memory_space=pl.ANY)

NT = (((1,), (1,)), ((), ()))
TN = (((0,), (0,)), ((), ()))
NN = (((1,), (0,)), ((), ()))


def cost(micros):
    return pl.CostEstimate(flops=int(micros * 1e9), bytes_accessed=1000, transcendentals=0)


def mm(a, b, dims):
    return lax.dot_general(a, b, dims, preferred_element_type=F32)


def shift(value, axis, steps):
    count = lax.axis_size(axis)
    first, last = max(0, -steps), min(count, count - steps)
    return lax.ppermute(value, axis, [(i, i + steps) for i in range(first, last)])


def after(value, *others):
    return lax.optimization_barrier((value, *others))[0]


def swap(value, axis, bit):
    return lax.ppermute(value, axis, [(i, i ^ bit) for i in range(lax.axis_size(axis))])


def count_rows(count_ref, width):
    row = lax.broadcasted_iota(jnp.int32, (16, width), 0)
    tail = jnp.zeros((16, width), F32)
    for u in range(count_ref.shape[0]):
        tail = jnp.where(row == u, count_ref[u].astype(F32), tail)
    return tail.astype(BF)


def pack_kernel(count_ref, nb_ref, out_ref):
    per, enc = nb_ref.shape[1:]
    out_ref[:per, :] = nb_ref[0]
    out_ref[per:, :] = count_rows(count_ref, enc)


def pack(nb, counts):
    groups, per, enc = nb.shape
    return pl.pallas_call(
        pack_kernel,
        grid=(1,),
        in_specs=[
            pl.BlockSpec(memory_space=pltpu.SMEM),
            pl.BlockSpec((1, per, enc), lambda p: (groups - 1, 0, 0)),
        ],
        out_specs=pl.BlockSpec((per + 16, enc), lambda p: (0, 0)),
        out_shape=jax.ShapeDtypeStruct((per + 16, enc), BF),
        compiler_params=pltpu.CompilerParams(vmem_limit_bytes=VMEM),
        cost_estimate=cost(2),
    )(counts, nb)


def cut_kernel(info_ref, count_ref, *refs):
    sources, parts, other_ref, pair_ref = refs[:6], refs[6:-2], refs[-2], refs[-1]
    for which in (0, 1):
        keys, values = sources[2 * which : 2 * which + 2]
        for chunk in range(CHUNKS):
            at = slice(chunk * PAIR, (chunk + 1) * PAIR)
            ref = other_ref if which else parts[chunk // TOGETHER]
            where = chunk if which else chunk % TOGETHER
            ref[where, :, :PAIR] = keys[:, at]
            ref[where, :, PAIR:] = values[:, at]
    tokens, width = sources[4].shape
    for index in (0, 1):
        pair_ref[index, :tokens, :] = sources[4 + index][...]
        pair_ref[index, tokens:, :] = count_rows(count_ref, width)


def cut(info, counts, weight, cq, do):
    rows = weight.shape[0]
    tokens, width = cq.shape
    count = CHUNKS // TOGETHER
    part = jax.ShapeDtypeStruct((TOGETHER, rows, 2 * PAIR), BF)
    parts = jax.ShapeDtypeStruct((CHUNKS, rows, 2 * PAIR), BF)
    half = jax.ShapeDtypeStruct((2, tokens + 16, width // 2), BF)

    def columns(height, other, value):
        return pl.BlockSpec(
            (height, width // 2), lambda p, info: (0, 2 * value + ((info[0] & 1) ^ other))
        )

    *mine, other, pair = pl.pallas_call(
        cut_kernel,
        grid_spec=pltpu.PrefetchScalarGridSpec(
            num_scalar_prefetch=1,
            grid=(1,),
            in_specs=[pl.BlockSpec(memory_space=pltpu.SMEM)]
            + [columns(rows, other, value) for other in (0, 1) for value in (0, 1)]
            + [columns(tokens, 1, 0)] * 2,
            out_specs=[
                pl.BlockSpec(x.shape, lambda p, info: (0, 0, 0))
                for x in [part] * count + [parts, half]
            ],
        ),
        out_shape=[part] * count + [parts, half],
        compiler_params=pltpu.CompilerParams(vmem_limit_bytes=VMEM),
        cost_estimate=cost(3),
    )(info, counts, weight, weight, weight, weight, cq, do)
    return mine, other, pair


def stack_kernel(*refs):
    count = CHUNKS // TOGETHER
    mine, near_ref, outs = refs[:count], refs[count], refs[count + 1 :]
    rows = near_ref.shape[1]
    for group, (ref, out) in enumerate(zip(mine, outs)):
        out[:, :rows, :] = ref[...]
        out[:, rows:, :] = near_ref[group * TOGETHER : (group + 1) * TOGETHER]


def stack(mine, near):
    together, rows, width = mine[0].shape
    return pl.pallas_call(
        stack_kernel,
        out_shape=[jax.ShapeDtypeStruct((together, 2 * rows, width), BF)] * len(mine),
        compiler_params=pltpu.CompilerParams(vmem_limit_bytes=VMEM),
        cost_estimate=cost(2),
    )(*mine, near)


def cross_kernel(group, turns, pieces, held, info_ref, count_ref, *refs):
    (turn_ref, nb_last, nb_own, peer_last, nb_peer), refs = refs[:5], refs[5:]
    weights, refs = refs[:pieces], refs[pieces:]
    (cq_ref, do_ref, peer_ref), refs = refs[:3], refs[3 + held :]
    token_outs, (keep_out, send_out), refs = refs[:4], refs[4:6], refs[6:]
    turned_out, refs = (refs[0], refs[1:]) if turns else (None, refs)
    (w_ref, nb_ref, turned_ref, kv_ref, dkv_ref, q_ref, g_ref, tail_ref), refs = refs[:8], refs[8:]
    out_ref, dw_ref, pick_ref, sem, out_sem = refs
    shard = info_ref[0]
    enc = nb_ref.shape[1]
    tokens = q_ref.shape[1]
    groups = tokens // GROUP
    per = 2 * RLEN
    size = groups * per
    rows = weights[0].shape[1]
    wide = TOGETHER * PAIR
    loads, stores = [], []

    def load(source, target):
        copy = pltpu.make_async_copy(source, target, sem.at[len(loads)])
        copy.start()
        loads.append(copy)
        return copy

    def store(source, target):
        copy = pltpu.make_async_copy(source, target, out_sem.at[len(stores)])
        copy.start()
        stores.append(copy)

    def load_weight(index):
        sources = [weights[0].at[index], weights[1].at[group * TOGETHER + index]]
        for ref in weights[2:]:
            sources += [ref.at[index, :rows, :], ref.at[index, rows:, :]]
        waits = []
        for piece, source in enumerate(sources):
            at = pl.ds(pl.multiple_of((shard ^ piece) * rows, 16), rows)
            waits.append(load(source, w_ref.at[index, at, :]))
        return waits

    waits_w = [load_weight(0)]
    waits_nb = [
        load(nb_last.at[:per, :], nb_ref.at[:per, :]),
        *[load(nb_own.at[u - 1], nb_ref.at[u * per : (u + 1) * per, :]) for u in range(1, groups)],
        load(peer_last.at[:per, :], nb_ref.at[size : size + per, :]),
        *[
            load(nb_peer.at[u - 1], nb_ref.at[size + u * per : size + (u + 1) * per, :])
            for u in range(1, groups)
        ],
    ]
    lanes = pl.ds(pl.multiple_of(((shard & 1) * CHUNKS + group * TOGETHER) * PAIR, PAIR), wide)
    there = slice(group * wide, (group + 1) * wide)
    waits_q = [
        load(cq_ref.at[:, lanes], q_ref.at[0]),
        load(do_ref.at[:, lanes], g_ref.at[0]),
        load(peer_ref.at[0, :tokens, there], q_ref.at[1]),
        load(peer_ref.at[1, :tokens, there], g_ref.at[1]),
        load(nb_last.at[per:, : 2 * GROUP], tail_ref.at[0]),
        load(peer_last.at[per:, : 2 * GROUP], tail_ref.at[1]),
        load(peer_ref.at[0, tokens:, : 2 * GROUP], tail_ref.at[2]),
    ]
    wait_turn = load(turn_ref, pick_ref if turns else turned_ref)
    for index in range(1, TOGETHER):
        waits_w.append(load_weight(index))

    def project(index):
        for copy in waits_w[index]:
            copy.wait()
        for file in (0, 1):
            for start, stop in ((0, 1), (1, groups)):
                if index == 0:
                    for copy in waits_nb[file * groups + start : file * groups + stop]:
                        copy.wait()
                at = slice(file * size + start * per, file * size + stop * per)
                kv_ref[index, at, :] = mm(nb_ref[at, :], w_ref[index], NN).astype(BF)

    zero = jnp.zeros((GROUP, HD), BF)

    def diagonal(block):
        return jnp.concatenate(
            [
                jnp.concatenate([block[:, :HD], zero], 1),
                jnp.concatenate([zero, block[:, HD:]], 1),
            ],
            0,
        )

    row = lax.broadcasted_iota(jnp.int32, (per, 2 * GROUP), 0).astype(F32)

    def attend(index, file, u):
        if u == 0:
            count = tail_ref[file, groups - 1 : groups, :].astype(F32)
        elif file:
            count = tail_ref[2, u - 1 : u, :].astype(F32)
        else:
            count = count_ref[u - 1].astype(F32)
        unit = file * groups + u
        at = slice(unit * per, (unit + 1) * per)
        tok = slice(u * GROUP, (u + 1) * GROUP)
        cols = slice(index * PAIR, (index + 1) * PAIR)
        keys, values = kv_ref[index, at, :PAIR], kv_ref[index, at, PAIR:]
        queries, grads = diagonal(q_ref[file, tok, cols]), diagonal(g_ref[file, tok, cols])
        scores = mm(keys, queries, NT)
        prob_grad = mm(values, grads, NT)
        scores = jnp.where(row < count * RLEN, scores, NEG)
        peak = jnp.max(scores, axis=0, keepdims=True)
        weight = jnp.exp2((scores - peak) * (SCALE * LOG2E))
        total = jnp.sum(weight, axis=0, keepdims=True)
        inverse = jnp.where(count > 0, 1.0 / total, 0.0)
        probs = weight * inverse
        delta = jnp.sum(probs * prob_grad, axis=0, keepdims=True)
        score_grad = (probs * (prob_grad - delta)).astype(BF)
        low = probs.astype(BF)
        out = mm(low, values, TN).astype(BF)
        dq = (mm(score_grad, keys, TN) * SCALE).astype(BF)
        for which, value in enumerate((out, dq)):
            out_ref[file, which, tok, index * PAIR : index * PAIR + HD] = value[:GROUP, :HD]
            out_ref[file, which, tok, index * PAIR + HD : (index + 1) * PAIR] = value[GROUP:, HD:]
        dkv_ref[index, at, :PAIR] = (mm(score_grad, queries, NN) * SCALE).astype(BF)
        dkv_ref[index, at, PAIR:] = mm(low, grads, NN).astype(BF)

    half = enc // 2
    bit = (shard // 2) % 2

    def weigh(index, targets):
        for slot, target, which in targets:
            at = pl.ds(pl.multiple_of(which * half, 16), half)
            dw_ref[slot, index] = mm(turned_ref[at, :], dkv_ref[index], NN).astype(BF)
            store(dw_ref.at[slot, index], target.at[index])

    both = ((0, send_out, 1 - bit), (1, keep_out, bit))
    project(0)
    for copy in waits_q:
        copy.wait()
    for index in range(TOGETHER):
        for file in (0, 1):
            for u in range(groups):
                attend(index, file, u)
        if index + 1 < TOGETHER:
            project(index + 1)
        if index == 0:
            wait_turn.wait()
            if turns:
                turned_ref[...] = mm(pick_ref[...], nb_ref[...], NT).astype(BF)
                store(turned_ref, turned_out)
        if index + 1 == TOGETHER:
            for which, target in enumerate(token_outs):
                store(out_ref.at[which // 2, which % 2], target.at[:, there])
        weigh(index, both)
    for copy in stores:
        copy.wait()


def cross(group, info, counts, turn, nbs, weights, cq, do, peer, held):
    tokens, half = peer.shape[1] - 16, peer.shape[2]
    groups, per, enc = nbs[1].shape
    size = 2 * groups * per
    turns = group == 0
    smem = pl.BlockSpec(memory_space=pltpu.SMEM)
    operands = [info, counts, turn, *nbs, *weights, cq, do, peer]
    shapes = [jax.ShapeDtypeStruct((tokens, half), BF)] * 4
    shapes += [jax.ShapeDtypeStruct((TOGETHER, enc // 2, 2 * PAIR), BF)] * 2
    if turns:
        shapes.append(jax.ShapeDtypeStruct((enc, size), BF))
    return pl.pallas_call(
        functools.partial(cross_kernel, group, turns, len(weights), len(held)),
        in_specs=[smem, smem] + [ANY] * (len(operands) - 2 + len(held)),
        out_specs=[ANY] * len(shapes),
        out_shape=shapes,
        scratch_shapes=[
            pltpu.VMEM((TOGETHER, enc, 2 * PAIR), BF),
            pltpu.VMEM((size, enc), BF),
            pltpu.VMEM((enc, size), BF),
            pltpu.VMEM((TOGETHER, size, 2 * PAIR), BF),
            pltpu.VMEM((TOGETHER, size, 2 * PAIR), BF),
            pltpu.VMEM((2, tokens, TOGETHER * PAIR), BF),
            pltpu.VMEM((2, tokens, TOGETHER * PAIR), BF),
            pltpu.VMEM((3, 16, 2 * GROUP), BF),
            pltpu.VMEM((2, 2, tokens, TOGETHER * PAIR), BF),
            pltpu.VMEM((2, TOGETHER, enc // 2, 2 * PAIR), BF),
            pltpu.VMEM((enc, enc) if turns else (16, 128), BF),
            pltpu.SemaphoreType.DMA((2 * groups + 8 + TOGETHER * 2 * len(weights),)),
            pltpu.SemaphoreType.DMA((5 + 2 * TOGETHER,)),
        ],
        input_output_aliases={len(operands) + i: i for i in range(len(held))},
        compiler_params=pltpu.CompilerParams(vmem_limit_bytes=VMEM),
        cost_estimate=cost(9),
    )(*operands, *held)


def self_kernel(
    heads, info_ref, q_ref, do_ref, ko_ref, vo_ref, one_ref, two_ref, three_ref, *refs
):
    own_ref, own_grad, back_ref, back_grad, *refs = refs
    out_ref, dq_ref, cross_ref, dk_ref, dv_ref, stat_ref = refs
    first_half = pl.program_id(0) < pl.num_programs(0) // 2
    crossed = jnp.where(first_half, own_ref[...], back_ref[...])
    cross_ref[...] = jnp.where(first_half, own_grad[...], back_grad[...])
    odd = info_ref[1] % 2 == 1
    keys_before = jnp.where(odd, one_ref[...], two_ref[...])
    values_before = jnp.where(odd, two_ref[...], three_ref[...])
    later = info_ref[1] > 0
    tokens = q_ref.shape[0]
    half = tokens // 2
    key_at = lax.broadcasted_iota(jnp.int32, (half, half), 0)
    query_at = lax.broadcasted_iota(jnp.int32, (half, half), 1)
    above = jnp.logical_and(key_at > query_at, later)
    below = key_at <= query_at
    zero = jnp.zeros((half, half), BF)
    lo, hi = slice(0, half), slice(half, None)
    for head in range(heads):
        at = slice(head * HD, (head + 1) * HD)
        queries, grads = q_ref[:, at], do_ref[:, at]
        kp, vp = keys_before[:, at], values_before[:, at]
        ko, vo = ko_ref[:, at], vo_ref[:, at]
        sp, so = mm(kp, queries, NT), mm(ko, queries, NT)
        gp, go = mm(vp, grads, NT), mm(vo, grads, NT)
        rows = []
        for a in (0, 1):
            if a == 0:
                blocks = (sp[lo, lo], sp[hi, lo], so[lo, lo])
                pgrads = (gp[lo, lo], gp[hi, lo], go[lo, lo])
                middle = jnp.where(later, blocks[1], NEG)
            else:
                blocks = (sp[hi, hi], so[lo, hi], so[hi, hi])
                pgrads = (gp[hi, hi], go[lo, hi], go[hi, hi])
                middle = blocks[1]
            scores = (jnp.where(above, blocks[0], NEG), middle, jnp.where(below, blocks[2], NEG))
            peak = jnp.max(
                jnp.maximum(jnp.maximum(scores[0], scores[1]), scores[2]), axis=0, keepdims=True
            )
            weight = [jnp.exp2((s - peak) * (SCALE * LOG2E)) for s in scores]
            total = jnp.sum(weight[0] + weight[1] + weight[2], axis=0, keepdims=True)
            inverse = 1.0 / total
            probs = [w * inverse for w in weight]
            delta = jnp.sum(
                probs[0] * pgrads[0] + probs[1] * pgrads[1] + probs[2] * pgrads[2],
                axis=0,
                keepdims=True,
            )
            score_grad = [(p * (g - delta)).astype(BF) for p, g in zip(probs, pgrads)]
            rows.append(([p.astype(BF) for p in probs], score_grad))
            lanes = slice(a * half, (a + 1) * half)
            stat_ref[head, 0:1, lanes] = peak * (SCALE * LOG2E) + jnp.log2(total)
            stat_ref[head, 1:2, lanes] = delta

        def spread(which):
            first, second = rows[0][which], rows[1][which]
            before = jnp.concatenate(
                [
                    jnp.concatenate([first[0], zero], 1),
                    jnp.concatenate([first[1], second[0]], 1),
                ],
                0,
            )
            own = jnp.concatenate(
                [
                    jnp.concatenate([first[2], second[1]], 1),
                    jnp.concatenate([zero, second[2]], 1),
                ],
                0,
            )
            return before, own

        (pp, po), (dp, do) = spread(0), spread(1)
        out = mm(pp, vp, TN) + mm(po, vo, TN) + crossed[:, at].astype(F32)
        out_ref[:, at] = out.astype(BF)
        dq_ref[:, at] = ((mm(dp, kp, TN) + mm(do, ko, TN)) * SCALE).astype(BF)
        dk_ref[:, at] = mm(do, queries, NN) * SCALE
        dv_ref[:, at] = mm(po, grads, NN)


def self_part(info, q, do, k, v, one, two, three, own, back):
    heads = 2
    tokens, width = q.shape
    steps = width // (heads * HD)
    half = steps // 2
    shape = (tokens, heads * HD)

    def place(p, info):
        return (p + (info[0] & 1) * half) % steps

    spec = pl.BlockSpec(shape, lambda p, info: (0, place(p, info)))
    own_spec = pl.BlockSpec(shape, lambda p, info: (0, jnp.minimum(p, half - 1)))
    back_spec = pl.BlockSpec(shape, lambda p, info: (0, jnp.maximum(p - half, 0)))
    stat_spec = pl.BlockSpec((heads, 2, tokens), lambda p, info: (place(p, info), 0, 0))
    full = jax.ShapeDtypeStruct(q.shape, BF)
    wide = jax.ShapeDtypeStruct(q.shape, F32)
    stats = jax.ShapeDtypeStruct((width // HD, 2, tokens), F32)
    return pl.pallas_call(
        functools.partial(self_kernel, heads),
        grid_spec=pltpu.PrefetchScalarGridSpec(
            num_scalar_prefetch=1,
            grid=(steps,),
            in_specs=[spec] * 7 + [own_spec] * 2 + [back_spec] * 2,
            out_specs=[spec] * 5 + [stat_spec],
        ),
        out_shape=[full] * 3 + [wide] * 2 + [stats],
        compiler_params=pltpu.CompilerParams(vmem_limit_bytes=VMEM),
        cost_estimate=cost(14),
    )(info, q, do, k, v, one, two, three, *own, *back)


def next_kernel(
    heads, info_ref, one_ref, three_ref, do_ref, k_ref, v_ref, stat_ref, dkp_ref, dvp_ref,
    dk_ref, dv_ref,
):
    all_queries = jnp.where(info_ref[1] % 2 == 1, three_ref[...], one_ref[...])
    tokens = do_ref.shape[0]
    half = tokens // 2
    key_at = lax.broadcasted_iota(jnp.int32, (half, half), 0)
    query_at = lax.broadcasted_iota(jnp.int32, (half, half), 1)
    above = key_at > query_at
    zero = jnp.zeros((half, half), BF)
    lo, hi = slice(0, half), slice(half, None)
    for head in range(heads):
        at = slice(head * HD, (head + 1) * HD)
        queries, grads = all_queries[:, at], do_ref[:, at]
        scores = mm(k_ref[:, at], queries, NT)
        prob_grad = mm(v_ref[:, at], grads, NT)
        level, delta = stat_ref[head, 0:1, :], stat_ref[head, 1:2, :]

        def block(rows, lanes, mask):
            exponent = scores[rows, lanes] * (SCALE * LOG2E) - level[:, lanes]
            if mask:
                exponent = jnp.where(above, exponent, NEG)
            probs = jnp.exp2(exponent)
            return probs.astype(BF), (probs * (prob_grad[rows, lanes] - delta[:, lanes])).astype(BF)

        first, middle, last = block(lo, lo, True), block(hi, lo, False), block(hi, hi, True)
        low, score_grad = [
            jnp.concatenate(
                [
                    jnp.concatenate([first[i], zero], 1),
                    jnp.concatenate([middle[i], last[i]], 1),
                ],
                0,
            )
            for i in (0, 1)
        ]
        dk_ref[:, at] = (dkp_ref[:, at] + mm(score_grad, queries, NN) * SCALE).astype(BF)
        dv_ref[:, at] = (dvp_ref[:, at] + mm(low, grads, NN)).astype(BF)


def next_part(info, one, three, do, k, v, stats, dk, dv):
    heads = 2
    tokens, width = k.shape
    spec = pl.BlockSpec((tokens, heads * HD), lambda p: (0, p))
    stat_spec = pl.BlockSpec((heads, 2, tokens), lambda p: (p, 0, 0))
    full = jax.ShapeDtypeStruct(k.shape, BF)
    return pl.pallas_call(
        functools.partial(next_kernel, heads),
        grid=(width // (heads * HD),),
        in_specs=[pl.BlockSpec(memory_space=pltpu.SMEM)]
        + [spec] * 5
        + [stat_spec]
        + [spec] * 2,
        out_specs=[spec] * 2,
        out_shape=[full] * 2,
        compiler_params=pltpu.CompilerParams(vmem_limit_bytes=VMEM),
        cost_estimate=cost(8),
    )(info, one, three, do, k, v, stats, dk, dv)


def halving_order(fsdp, seq):
    bits = [("fsdp", 1 << i) for i in range(1, fsdp.bit_length() - 1)]
    seq_bits = [("seq", 1 << i) for i in range(seq.bit_length() - 1)]
    return bits + seq_bits[1:] + seq_bits[:1]


def row_order(fsdp, seq, rows):
    index = np.arange(rows).reshape(seq * fsdp, -1)
    block = np.arange(seq * fsdp)
    keys = []
    for axis, bit in halving_order(fsdp, seq) + [("fsdp", 1)]:
        value = block % fsdp if axis == "fsdp" else block // fsdp
        keys.append((value // bit) % 2)
    order = np.lexsort(keys[::-1])
    return index[order].reshape(-1)


def take_half(value, upper):
    half = value.shape[0] // 2
    return lax.dynamic_slice_in_dim(value, upper * half, half, 0)


def halve_kernel(spans, axis, bit, info_ref, *refs):
    sources, (mine_ref, other_ref) = refs[:-2], refs[-2:]
    count = len(sources) // 2
    half = mine_ref.shape[0]
    upper = (info_ref[0 if axis == "fsdp" else 1] // bit) % 2
    for ref, which in ((mine_ref, upper), (other_ref, 1 - upper)):
        at = pl.ds(pl.multiple_of(which * half, 16), half)
        start = 0
        for keep, got, parts in zip(sources[:count], sources[count:], spans):
            width = keep.shape[-1]
            for part in range(parts):
                where = (part, at) if len(keep.shape) == 3 else (at,)
                total = keep[where].astype(F32) + got[where].astype(F32)
                ref[:, start : start + width] = total.astype(BF)
                start += width


def halve(info, keeps, received, stage):
    axis, bit = stage
    spans = [x.shape[0] if x.ndim == 3 else 1 for x in keeps]
    rows = keeps[0].shape[-2]
    width = sum(parts * x.shape[-1] for parts, x in zip(spans, keeps))
    if rows // 2 % 16:
        upper = (info[0 if axis == "fsdp" else 1] // bit) % 2
        sums = [
            (x.astype(F32) + y.astype(F32)).reshape(-1, rows, x.shape[-1])
            for x, y in zip(keeps, received)
        ]
        total = jnp.concatenate([part for x in sums for part in x], -1)
        return take_half(total, upper).astype(BF), take_half(total, 1 - upper).astype(BF)
    return pl.pallas_call(
        functools.partial(halve_kernel, spans, axis, bit),
        in_specs=[pl.BlockSpec(memory_space=pltpu.SMEM)]
        + [pl.BlockSpec(memory_space=pltpu.VMEM)] * (2 * len(keeps)),
        out_shape=[jax.ShapeDtypeStruct((rows // 2, width), BF)] * 2,
        compiler_params=pltpu.CompilerParams(vmem_limit_bytes=VMEM),
        cost_estimate=cost(1),
    )(info, *keeps, *received)


def on_device(
    self_query, self_key, self_value, cross_query, neighbours, neighbour_count, kv_weight, out_grad
):
    fsdp, seq = lax.axis_size("fsdp"), lax.axis_size("seq")
    shard, slab = lax.axis_index("fsdp"), lax.axis_index("seq")
    q, k, v, cq, do = (x[0] for x in (self_query, self_key, self_value, cross_query, out_grad))
    nb, counts = neighbours[0], neighbour_count[0]
    tokens, width = q.shape
    groups, per, enc = nb.shape
    info = jnp.stack([shard, slab]).astype(jnp.int32)

    last = pack(nb, counts)
    nb_last = shift(last, "seq", 1)

    nb_peer = swap(nb, "fsdp", 1)
    mine, other, pair = cut(after(info, last, nb_peer), counts, kv_weight, cq, do)
    near = swap(other, "fsdp", 1)
    weights = [
        [here, near, *[swap(x, "fsdp", piece) for piece in range(2, fsdp, 2)]]
        for here, x in zip(mine, stack(mine, near))
    ]
    peer = swap(pair, "fsdp", 1)

    even = slab % 2 == 0

    def pick(when_even, when_odd, *others):
        return jnp.where(after(even, nb_last, *others), when_even, when_odd)

    def hop(value):
        odds = [(i, i + 2) for i in range(1, seq - 2, 2)]
        return lax.ppermute(value, "seq", odds + [(i, i - 2) for i in range(2, seq, 2)])

    far_one = hop(pick(q, k))
    one = swap(pick(k, q), "seq", 1)

    nb_last = after(nb_last, peer)
    peer_last = swap(nb_last, "fsdp", 1)
    nbs = [nb_last, nb, peer_last, nb_peer]

    stages = halving_order(fsdp, seq)
    split_at = fsdp.bit_length() - 2

    turn = jnp.asarray(np.eye(enc)[row_order(fsdp, seq, enc)], BF)
    held, pairs = [], []
    for group in range(CHUNKS // TOGETHER):
        results = cross(group, info, counts, turn, nbs, weights[group], cq, do, peer, held)
        held, (keep, send) = results[:4], results[4:6]
        if not group:
            turn = results[6]
            two = swap(pick(v, far_one, turn), "seq", 1)
            far_two = hop(pick(do, v, turn))
        received = swap(send, *stages[0])
        for stage in range(1, split_at):
            keep, send = halve(info, [keep], [received], stages[stage])
            received = swap(send, *stages[stage])
        pairs.append((keep, received))
    own = held[:2]
    back = [swap(x, "fsdp", 1) for x in after(held[2:], pairs[0][1], one, two, far_two)]
    third = pick(far_one, far_two, pairs[-1][0])
    three = swap(third, "seq", 1)

    halves = [halve(info, [pairs[0][0]], [pairs[0][1]], stages[split_at])]
    got = [swap(halves[0][1], *stages[split_at])]
    halves.append(
        halve(after(info, halves[0][1], *back), [pairs[1][0]], [pairs[1][1]], stages[split_at])
    )
    got.append(swap(halves[1][1], *stages[split_at]))
    four = swap(pick(far_two, do, halves[1][1], third), "seq", 1)
    keeps = [keep for keep, _ in halves]
    keep, send = halve(after(info, three), keeps, got, stages[split_at + 1])
    keeps, got = [keep], [swap(send, *stages[split_at + 1])]
    block_out, query_grad, cross_grad, dk, dv, stats = self_part(
        after(info, send), q, do, k, v, one, two, three, own, back
    )
    stats_after = shift(stats, "seq", -1)
    key_grad, value_grad = next_part(info, one, three, four, k, v, stats_after, dk, dv)

    for stage in range(split_at + 2, len(stages)):
        keep, send = halve(after(info, stats), keeps, got, stages[stage])
        keeps, got = [keep], [swap(send, *stages[stage])]
    total = keeps[0].astype(F32) + got[0].astype(F32)
    core = shard % 2
    away = swap(take_half(total, 1 - core).astype(BF), "fsdp", 1).astype(F32)
    nearby = take_half(total, core)
    key_mine, key_away, value_mine, value_away = [
        jnp.concatenate(
            [x[:, (2 * c + part) * PAIR : (2 * c + part + 1) * PAIR] for c in range(CHUNKS)], -1
        )
        for part in (0, 1)
        for x in (nearby, away)
    ]
    low = shard % 2 == 0
    weight_grad = jnp.concatenate(
        [
            jnp.where(low, key_mine, key_away),
            jnp.where(low, key_away, key_mine),
            jnp.where(low, value_mine, value_away),
            jnp.where(low, value_away, value_mine),
        ],
        -1,
    )

    return (
        block_out[None],
        query_grad[None],
        key_grad[None],
        value_grad[None],
        cross_grad[None],
        weight_grad,
    )


def solution(mesh):
    in_specs = (
        P("fsdp", "seq", None),
        P("fsdp", "seq", None),
        P("fsdp", "seq", None),
        P("fsdp", "seq", None),
        P("fsdp", "seq", None, None),
        P("fsdp", "seq"),
        P("fsdp", None),
        P("fsdp", "seq", None),
    )
    out_specs = (
        P("fsdp", "seq", None),
        P("fsdp", "seq", None),
        P("fsdp", "seq", None),
        P("fsdp", "seq", None),
        P("fsdp", "seq", None),
        P(("seq", "fsdp"), None),
    )
    return jax.shard_map(
        on_device, mesh=mesh, in_specs=in_specs, out_specs=out_specs, check_vma=False
    )
```

time: 189 us -> 156 us (0.83)
  Pallas kernels: 98.6 us -> 80.3 us
  waiting for transfers between devices: 47.7 us -> 31.7 us
  other arithmetic: 2.33 us -> 5.76 us
    ppermute x20 -> x19, waiting for transfers between devices: 47.7 us -> 24.9 us  [swap(): lax.ppermute(value, axis, [(i, i ^ bit) for i in range(lax.axis_size(axis...]
    pallas_call x15 -> x8, Pallas kernels: 78 us -> 59.2 us  [the longest x2 37.8 us: cross(): pl.pallas_call(functools.partial(cross_kernel, group, turns, len(weights)...]
    ppermute x5 -> x2, starting transfers between devices: 13.4 us -> 6.83 us  [shift(): lax.ppermute(value, axis, [(i, i + steps) for i in range(first, last)])]
    select_n x0 -> x4, other arithmetic: none -> 4.25 us  [pick(): return jnp.where(after(even, nb_last, *others), when_even, when_odd)]
    ppermute x20 -> x19, starting transfers between devices: 19.9 us -> 23.8 us  [swap(): lax.ppermute(value, axis, [(i, i ^ bit) for i in range(lax.axis_size(axis...]
    ppermute x5 -> x2, waiting for transfers between devices: 0.01 us -> 3.67 us  [shift(): lax.ppermute(value, axis, [(i, i + steps) for i in range(first, last)])]
    ppermute x0 -> x2, waiting for transfers between devices: none -> 3.13 us  [hop(): lax.ppermute(value, 'seq', odds + [(i, i - 2) for i in range(2, seq, 2)])]
    ppermute x0 -> x2, starting transfers between devices: none -> 2.56 us  [hop(): lax.ppermute(value, 'seq', odds + [(i, i - 2) for i in range(2, seq, 2)])]
  transfers between devices with their start and end apart: 25 -> 23, of which waited for: 8 -> 8; matrix products, arithmetic and copies ran while one was open for 0% -> 3% of each run, Pallas kernels for 49% -> 49%
where the time goes in v3:
time: 156 us; the launch traced here: 155 us
  Pallas kernels  80.3 us (51%)
  starting transfers between devices  33.2 us (21%)
  waiting for transfers between devices  31.7 us (20%)
  other arithmetic  5.76 us (4%)
  local copies, waits for them, and re-layouts  3.6 us (2%)
    pallas_call x2, Pallas kernels, cross(): pl.pallas_call(functools.partial(cross_kernel, group, turns, len(weights)...  37.8 us
    ppermute x19, waiting for transfers between devices, swap(): lax.ppermute(value, axis, [(i, i ^ bit) for i in range(lax.axis_size(axis...  24.9 us
    ppermute x19, starting transfers between devices, swap(): lax.ppermute(value, axis, [(i, i ^ bit) for i in range(lax.axis_size(axis...  23.8 us
    pallas_call x1, Pallas kernels, self_part(): pl.pallas_call(functools.partial(self_kernel, heads), grid_spec=pltpu.Pre...  15.3 us
    pallas_call x1, Pallas kernels, next_part(): pl.pallas_call(functools.partial(next_kernel, heads), grid=(width // (hea...  9.64 us
    pallas_call x4, Pallas kernels, halve(): pl.pallas_call(functools.partial(halve_kernel, spans, axis, bit), in_spec...  9.09 us
    ppermute x2, starting transfers between devices, shift(): lax.ppermute(value, axis, [(i, i + steps) for i in range(first, last)])  6.83 us
    select_n x4, other arithmetic, pick(): return jnp.where(after(even, nb_last, *others), when_even, when_odd)  4.25 us
  transfers between devices with their start and end apart: 23, of which 8 were waited for; matrix products, arithmetic and copies ran while one was open for 3% of the time, Pallas kernels for 49%

profile of v3, /device:TPU:0, one launch (start us, length us, event | category | flops | bytes accessed | tf_op | source)
XLA Modules:
  0.0 155.4 jit_solution(6555490494326482491)
XLA Ops:
  1.8 1.8 %shard_map.136 = bf16[272,768]{1,0:T(8,128)(2,1)} custom-call(s32[4]{0:T(128)} %bitcast.38, bf16[4,256,768]{2,1,0:T(8,128)(2,1)} %bitcast.32), custom_call_target="tpu_custom_call" | custom-call | flops 2000000000 | bytes 1000 | tf_op jit(solution)/shard_map/pallas_call | solution.py:69
  4.4 3.9 %shard_map.137 = (bf16[2,192,512]{2,1,0:T(8,128)(2,1)}, bf16[2,192,512]{2,1,0:T(8,128)(2,1)}, bf16[4,192,512]{2,1,0:T(8,128)(2,1)}, bf16[2,272,1024]{2,1,0:T(8,128)(2,1)}) custom-call(s32[2]{0:T(128)} %pad_add_fusion.info_ref, s32[4]{0:T(128)} %bitcast.39, bf16[192,4096]{1,0:T(8,128)(2,1)} %refs_3_.1, bf16[192,4096]{1,0:T(8,128)(2,1)} %refs_3_.1, ...), custom_call_target="tpu_custom_call" | custom-call | flops 3000000000 | bytes 1000 | tf_op jit(solution)/shard_map/pallas_call | solution.py:112
  8.8 5.5 %collective-permute-start = (bf16[272,768]{1,0:T(8,128)(2,1)}, bf16[272,768]{1,0:T(8,128)(2,1)}, u32[]{:S(2)}, u32[]{:S(2)}) collective-permute-start(bf16[272,768]{1,0:T(8,128)(2,1)} %shard_map.136), channel_id=1, source_target_pairs={{0,4},{4,8},{8,12},{12,16},{16,20},{20,24},{24,28},{1,5},{5,9},{9,... | collective-permute-start | bytes 1253384 | tf_op jit(solution)/shard_map/ppermute | solution.py:42
  15.3 2.7 %shard_map.138 = (bf16[2,384,512]{2,1,0:T(8,128)(2,1)}, bf16[2,384,512]{2,1,0:T(8,128)(2,1)}) custom-call(bf16[2,192,512]{2,1,0:T(8,128)(2,1)} %get-tuple-element.56.refs_0_.refs_5_, bf16[2,192,512]{2,1,0:T(8,128)(2,1)} %get-tuple-element.58.refs_1_.refs_5_, bf16[4,192,512]{2,1,0:T(8,128)(2,1)} %copy-done.10), custom_call_target="tpu_custom_call" | custom-call | flops 2000000000 | bytes 1000 | tf_op jit(solution)/shard_map/pallas_call | solution.py:143
  19.5 3.7 %collective-permute-done.refs_1_ = bf16[272,768]{1,0:T(8,128)(2,1)} collective-permute-done((bf16[272,768]{1,0:T(8,128)(2,1)}, bf16[272,768]{1,0:T(8,128)(2,1)}, u32[]{:S(2)}, u32[]{:S(2)}) %collective-permute-start) | collective-permute-done | bytes 417824 | tf_op jit(solution)/shard_map/ppermute | solution.py:42
  23.1 1.6 %broadcast_select_fusion.3 = (bf16[256,2048]{1,0:T(8,128)(2,1)}, bf16[256,2048]{1,0:T(8,128)(2,1)}) fusion(pred[]{:T(512)S(6)} %eq.10, bf16[1,256,2048]{2,1,0:T(8,128)(2,1)S(1)} %copy-done.3, bf16[1,256,2048]{2,1,0:T(8,128)(2,1)S(1)} %copy-done.2), kind=kLoop, calls=%fused_computation.3 | loop fusion | flops 1048576 | bytes 4194305 | tf_op jit(solution)/shard_map/jit(_where)/select_n | solution.py:602
  26.1 4.8 %collective-permute-start.11 = (bf16[256,2048]{1,0:T(8,128)(2,1)}, bf16[256,2048]{1,0:T(8,128)(2,1)}, u32[]{:S(2)}, u32[]{:S(2)}) collective-permute-start(bf16[256,2048]{1,0:T(8,128)(2,1)} %get-tuple-element.100), channel_id=1, source_target_pairs={{0,4},{4,0},{8,12},{12,8},{16,20},{20,16},{24,28},{28,24},{1,5},{5... | collective-permute-start | bytes 3145736 | tf_op jit(solution)/shard_map/ppermute | solution.py:50
  32.4 6.3 %collective-permute-done.5.refs_7_ = bf16[2,384,512]{2,1,0:T(8,128)(2,1)} collective-permute-done((bf16[2,384,512]{2,1,0:T(8,128)(2,1)}, bf16[2,384,512]{2,1,0:T(8,128)(2,1)}, u32[]{:S(2)}, u32[]{:S(2)}) %collective-permute-start.5) | collective-permute-done | bytes 786464 | tf_op jit(solution)/shard_map/ppermute | solution.py:50
  38.7 20.2 %shard_map.139 = (bf16[256,1024]{1,0:T(8,128)(2,1)}, bf16[256,1024]{1,0:T(8,128)(2,1)}, bf16[256,1024]{1,0:T(8,128)(2,1)}, bf16[256,1024]{1,0:T(8,128)(2,1)}, bf...) custom-call(s32[2]{0:T(128)} %pad_add_fusion.info_ref, s32[4]{0:T(128)} %bitcast.40, ...), custom_call_target="tpu_custom_call" | custom-call | flops 8999999488 | bytes 1000 | tf_op jit(solution)/shard_map/pallas_call | solution.py:314
  64.2 17.6 %shard_map.140 = (bf16[256,1024]{1,0:T(8,128)(2,1)}, bf16[256,1024]{1,0:T(8,128)(2,1)}, bf16[256,1024]{1,0:T(8,128)(2,1)}, bf16[256,1024]{1,0:T(8,128)(2,1)}, bf...) custom-call(s32[2]{0:T(128)} %pad_add_fusion.info_ref, ...), custom_call_target="tpu_custom_call", output_to_operand_aliasing={{0}: (13, {}), {1}: (14, {}), {2}: (15, {}), {3}: (16, {})} | custom-call | flops 8999999488 | bytes 1000 | tf_op jit(solution)/shard_map/pallas_call | solution.py:314
  83.6 3.1 %collective-permute-done.8 = bf16[256,2048]{1,0:T(8,128)(2,1)S(1)} collective-permute-done((bf16[256,2048]{1,0:T(8,128)(2,1)}, bf16[256,2048]{1,0:T(8,128)(2,1)S(1)}, u32[]{:S(2)}, u32[]{:S(2)}) %collective-permute-start.8) | collective-permute-done | bytes 1048608 | tf_op jit(solution)/shard_map/ppermute | solution.py:606
  88.4 2.4 %shard_map.141 = (bf16[192,1024]{1,0:T(8,128)(2,1)}, bf16[192,1024]{1,0:T(8,128)(2,1)}) custom-call(s32[2]{0:T(128)} %pad_add_fusion.info_ref, bf16[2,384,512]{2,1,0:T(8,128)(2,1)} %get-tuple-element.71.refs_0_, bf16[2,384,512]{2,1,0:T(8,128)(2,1)} %collective-permute-done.10.refs_1_), custom_call_target="tpu_custom_call" | custom-call | flops 1000000000 | bytes 1000 | tf_op jit(solution)/shard_map/pallas_call | solution.py:566
  90.7 2.1 %collective-permute-start.16 = (bf16[192,1024]{1,0:T(8,128)(2,1)}, bf16[192,1024]{1,0:T(8,128)(2,1)S(1)}, u32[]{:S(2)}, u32[]{:S(2)}) collective-permute-start(bf16[192,1024]{1,0:T(8,128)(2,1)} %get-tuple-element.74), channel_id=1, source_target_pairs={{0,8},{4,12},{8,0},{12,4},{16,24},{20,28},{24,16},{28,20},{1,9},{5... | collective-permute-start | bytes 1179656 | tf_op jit(solution)/shard_map/ppermute | solution.py:50
  92.8 6.7 %collective-permute-done.15.refs_1_ = bf16[2,384,512]{2,1,0:T(8,128)(2,1)} collective-permute-done((bf16[2,384,512]{2,1,0:T(8,128)(2,1)}, bf16[2,384,512]{2,1,0:T(8,128)(2,1)}, u32[]{:S(2)}, u32[]{:S(2)}) %collective-permute-start.15) | collective-permute-done | bytes 786464 | tf_op jit(solution)/shard_map/ppermute | solution.py:50
  99.6 2.4 %shard_map.142 = (bf16[192,1024]{1,0:T(8,128)(2,1)}, bf16[192,1024]{1,0:T(8,128)(2,1)}) custom-call(s32[2]{0:T(128)} %pad_add_fusion.info_ref, bf16[2,384,512]{2,1,0:T(8,128)(2,1)} %get-tuple-element.66.refs_0_, bf16[2,384,512]{2,1,0:T(8,128)(2,1)} %collective-permute-done.15.refs_1_), custom_call_target="tpu_custom_call" | custom-call | flops 1000000000 | bytes 1000 | tf_op jit(solution)/shard_map/pallas_call | solution.py:566
  102.0 2.3 %collective-permute-start.17 = (bf16[192,1024]{1,0:T(8,128)(2,1)}, bf16[192,1024]{1,0:T(8,128)(2,1)}, u32[]{:S(2)}, u32[]{:S(2)}) collective-permute-start(bf16[192,1024]{1,0:T(8,128)(2,1)} %get-tuple-element.82), channel_id=1, source_target_pairs={{0,8},{4,12},{8,0},{12,4},{16,24},{20,28},{24,16},{28,20},{1,9},{5... | collective-permute-start | bytes 1179656 | tf_op jit(solution)/shard_map/ppermute | solution.py:50
  104.4 1.7 %collective-permute-start.18 = (bf16[256,2048]{1,0:T(8,128)(2,1)S(1)}, bf16[256,2048]{1,0:T(8,128)(2,1)S(1)}, u32[]{:S(2)}, u32[]{:S(2)}) collective-permute-start(bf16[256,2048]{1,0:T(8,128)(2,1)S(1)} %broadcast_select_fusion), channel_id=1, source_target_pairs={{0,4},{4,0},{8,12},{12,8},{16,20},{20,16},{24,28},{28,24},{1,5},{5... | collective-permute-start | bytes 3145736 | tf_op jit(solution)/shard_map/ppermute | solution.py:50
  106.1 8.6 %collective-permute-done.9.three_ref = bf16[256,2048]{1,0:T(8,128)(2,1)} collective-permute-done((bf16[256,2048]{1,0:T(8,128)(2,1)}, bf16[256,2048]{1,0:T(8,128)(2,1)}, u32[]{:S(2)}, u32[]{:S(2)}) %collective-permute-start.9) | collective-permute-done | bytes 1048608 | tf_op jit(solution)/shard_map/ppermute | solution.py:50
  115.4 2.4 %shard_map.143 = (bf16[96,2048]{1,0:T(8,128)(2,1)}, bf16[96,2048]{1,0:T(8,128)(2,1)}) custom-call(s32[2]{0:T(128)} %pad_add_fusion.info_ref, bf16[192,1024]{1,0:T(8,128)(2,1)} %get-tuple-element.73.refs_0_, bf16[192,1024]{1,0:T(8,128)(2,1)} %get-tuple-element.81.refs_1_, bf16[192,1024]{1,0:T(8,128)(2,1)} %copy-done.11, ...), custom_call_target="tpu_custom_call" | custom-call | flops 1000000000 | bytes 1000 | tf_op jit(solution)/shard_map/pallas_call | solution.py:566
  117.8 2.6 %collective-permute-start.20 = (bf16[96,2048]{1,0:T(8,128)(2,1)}, bf16[96,2048]{1,0:T(8,128)(2,1)S(1)}, u32[]{:S(2)}, u32[]{:S(2)}) collective-permute-start(bf16[96,2048]{1,0:T(8,128)(2,1)} %get-tuple-element.83), channel_id=1, source_target_pairs={{0,16},{4,20},{8,24},{12,28},{16,0},{20,4},{24,8},{28,12},{1,17},{... | collective-permute-start | bytes 1179656 | tf_op jit(solution)/shard_map/ppermute | solution.py:50
  120.4 15.3 %shard_map.144 = (bf16[256,2048]{1,0:T(8,128)(2,1)}, bf16[256,2048]{1,0:T(8,128)(2,1)}, bf16[256,2048]{1,0:T(8,128)(2,1)}, f32[256,2048]{1,0:T(8,128)}, f32[256,2048]{1,0:T(8,128)}, /*index=5*/f32[16,2,256]{2,1,0:T(2,128)}) custom-call(s32[2]{0:T(128)} %pad_add_fusion.info_ref, bf16[256,2048]{1,0:T(8,128)(2,1)} %bitcast.26, bf16[256,2048]{1,0:T(8,128)(2,1)} %bitcast.25, ...), custom_call_target="tpu_custom_call" | custom-call | flops 14000000000 | bytes 1000 | tf_op jit(solution)/shard_map/pallas_call | solution.py:439
  137.8 1.9 %shard_map.146 = (bf16[48,2048]{1,0:T(8,128)(2,1)}, bf16[48,2048]{1,0:T(8,128)(2,1)}) custom-call(s32[2]{0:T(128)} %pad_add_fusion.info_ref, bf16[96,2048]{1,0:T(8,128)(2,1)} %get-tuple-element.97.refs_0_, bf16[96,2048]{1,0:T(8,128)(2,1)} %copy-done.12), custom_call_target="tpu_custom_call" | custom-call | flops 1000000000 | bytes 1000 | tf_op jit(solution)/shard_map/pallas_call | solution.py:566
  139.7 2.6 %collective-permute-start.21 = (bf16[48,2048]{1,0:T(8,128)(2,1)}, bf16[48,2048]{1,0:T(8,128)(2,1)S(1)}, u32[]{:S(2)}, u32[]{:S(2)}) collective-permute-start(bf16[48,2048]{1,0:T(8,128)(2,1)} %get-tuple-element.99), channel_id=1, source_target_pairs={{0,4},{4,0},{8,12},{12,8},{16,20},{20,16},{24,28},{28,24},{1,5},{5... | collective-permute-start | bytes 589832 | tf_op jit(solution)/shard_map/ppermute | solution.py:50
  143.4 9.6 %shard_map.145 = (bf16[256,2048]{1,0:T(8,128)(2,1)}, bf16[256,2048]{1,0:T(8,128)(2,1)}) custom-call(s32[2]{0:T(128)} %pad_add_fusion.info_ref, bf16[256,2048]{1,0:T(8,128)(2,1)} %collective-permute-done.11.one_ref, bf16[256,2048]{1,0:T(8,128)(2,1)} %collective-permute-done.9.three_ref, bf16[256,2048]{1,0:T(8,128)(2,1)} %copy-done.9, ...), custom_call_target="tpu_custom_call" | custom-call | flops 8000000000 | bytes 1000 | tf_op jit(solution)/shard_map/pallas_call | solution.py:500
  (73 shorter events, 22.6 us)
Async XLA Ops:
  0.6 3.8 %collective-permute-start.1 = (bf16[4,256,768]{2,1,0:T(8,128)(2,1)}, bf16[4,256,768]{2,1,0:T(8,128)(2,1)S(1)}, u32[]{:S(2)}, u32[]{:S(2)}) collective-permute-start(bf16[4,256,768]{2,1,0:T(8,128)(2,1)} %bitcast.31), channel_id=1, source_target_pairs={{0,1},{1,0},{2,3},{3,2},{4,5},{5,4},{6,7},{7,6},{8,9},{9,8},{10,11... | collective-permute-start | bytes 4718600 | tf_op jit(solution)/shard_map/ppermute | solution.py:50
  8.3 14.8 %collective-permute-start.2 = (bf16[2,272,1024]{2,1,0:T(8,128)(2,1)}, bf16[2,272,1024]{2,1,0:T(8,128)(2,1)S(1)}, u32[]{:S(2)}, u32[]{:S(2)}) collective-permute-start(bf16[2,272,1024]{2,1,0:T(8,128)(2,1)} %get-tuple-element.54), channel_id=1, source_target_pairs={{0,1},{1,0},{2,3},{3,2},{4,5},{5,4},{6,7},{7,6},{8,9},{9,8},{10,11... | collective-permute-start | bytes 3342344 | tf_op jit(solution)/shard_map/ppermute | solution.py:50
  8.7 5.7 %collective-permute-start.4 = (bf16[4,192,512]{2,1,0:T(8,128)(2,1)}, bf16[4,192,512]{2,1,0:T(8,128)(2,1)S(1)}, u32[]{:S(2)}, u32[]{:S(2)}) collective-permute-start(bf16[4,192,512]{2,1,0:T(8,128)(2,1)} %get-tuple-element.57), channel_id=1, source_target_pairs={{0,1},{1,0},{2,3},{3,2},{4,5},{5,4},{6,7},{7,6},{8,9},{9,8},{10,11... | collective-permute-start | bytes 2359304 | tf_op jit(solution)/shard_map/ppermute | solution.py:50
  8.8 14.3 %collective-permute-start = (bf16[272,768]{1,0:T(8,128)(2,1)}, bf16[272,768]{1,0:T(8,128)(2,1)}, u32[]{:S(2)}, u32[]{:S(2)}) collective-permute-start(bf16[272,768]{1,0:T(8,128)(2,1)} %shard_map.136), channel_id=1, source_target_pairs={{0,4},{4,8},{8,12},{12,16},{16,20},{20,24},{24,28},{1,5},{5,9},{9,... | collective-permute-start | bytes 1253384 | tf_op jit(solution)/shard_map/ppermute | solution.py:42
  18.0 20.7 %collective-permute-start.5 = (bf16[2,384,512]{2,1,0:T(8,128)(2,1)}, bf16[2,384,512]{2,1,0:T(8,128)(2,1)}, u32[]{:S(2)}, u32[]{:S(2)}) collective-permute-start(bf16[2,384,512]{2,1,0:T(8,128)(2,1)} %get-tuple-element.59), channel_id=1, source_target_pairs={{0,2},{1,3},{2,0},{3,1},{4,6},{5,7},{6,4},{7,5},{8,10},{9,11},{10,... | collective-permute-start | bytes 2359304 | tf_op jit(solution)/shard_map/ppermute | solution.py:50
  23.1 9.3 %collective-permute-start.3 = (bf16[272,768]{1,0:T(8,128)(2,1)}, bf16[272,768]{1,0:T(8,128)(2,1)}, u32[]{:S(2)}, u32[]{:S(2)}) collective-permute-start(bf16[272,768]{1,0:T(8,128)(2,1)} %collective-permute-done.refs_1_), channel_id=1, source_target_pairs={{0,1},{1,0},{2,3},{3,2},{4,5},{5,4},{6,7},{7,6},{8,9},{9,8},{10,11... | collective-permute-start | bytes 1253384 | tf_op jit(solution)/shard_map/ppermute | solution.py:50
  24.8 34.2 %collective-permute-start.7 = (bf16[256,2048]{1,0:T(8,128)(2,1)}, bf16[256,2048]{1,0:T(8,128)(2,1)S(1)}, u32[]{:S(2)}, u32[]{:S(2)}) collective-permute-start(bf16[256,2048]{1,0:T(8,128)(2,1)} %get-tuple-element.101), channel_id=1, source_target_pairs={{4,12},{12,20},{20,28},{8,0},{16,8},{24,16},{5,13},{13,21},{21,29}... | collective-permute-start | bytes 3145736 | tf_op jit(solution)/shard_map/ppermute | solution.py:606
  26.1 56.3 %collective-permute-start.11 = (bf16[256,2048]{1,0:T(8,128)(2,1)}, bf16[256,2048]{1,0:T(8,128)(2,1)}, u32[]{:S(2)}, u32[]{:S(2)}) collective-permute-start(bf16[256,2048]{1,0:T(8,128)(2,1)} %get-tuple-element.100), channel_id=1, source_target_pairs={{0,4},{4,0},{8,12},{12,8},{16,20},{20,16},{24,28},{28,24},{1,5},{5... | collective-permute-start | bytes 3145736 | tf_op jit(solution)/shard_map/ppermute | solution.py:50
  30.9 28.1 %copy-start.4 = (bf16[1,256,2048]{2,1,0:T(8,128)(2,1)S(1)}, bf16[1,256,2048]{2,1,0:T(8,128)(2,1)}, u32[]{:S(2)}) copy-start(bf16[1,256,2048]{2,1,0:T(8,128)(2,1)} %param.11) | copy-start | bytes 3145732
  30.9 33.3 %collective-permute-start.6 = (bf16[2,384,512]{2,1,0:T(8,128)(2,1)}, bf16[2,384,512]{2,1,0:T(8,128)(2,1)}, u32[]{:S(2)}, u32[]{:S(2)}) collective-permute-start(bf16[2,384,512]{2,1,0:T(8,128)(2,1)} %get-tuple-element.61), channel_id=1, source_target_pairs={{0,2},{1,3},{2,0},{3,1},{4,6},{5,7},{6,4},{7,5},{8,10},{9,11},{10,... | collective-permute-start | bytes 2359304 | tf_op jit(solution)/shard_map/ppermute | solution.py:50
  60.5 23.1 %collective-permute-start.12 = (bf16[256,2048]{1,0:T(8,128)(2,1)}, bf16[256,2048]{1,0:T(8,128)(2,1)S(1)}, u32[]{:S(2)}, u32[]{:S(2)}) collective-permute-start(bf16[256,2048]{1,0:T(8,128)(2,1)} %get-tuple-element.102), channel_id=1, source_target_pairs={{0,4},{4,0},{8,12},{12,8},{16,20},{20,16},{24,28},{28,24},{1,5},{5... | collective-permute-start | bytes 3145736 | tf_op jit(solution)/shard_map/ppermute | solution.py:50
  61.4 25.4 %collective-permute-start.8 = (bf16[256,2048]{1,0:T(8,128)(2,1)}, bf16[256,2048]{1,0:T(8,128)(2,1)S(1)}, u32[]{:S(2)}, u32[]{:S(2)}) collective-permute-start(bf16[256,2048]{1,0:T(8,128)(2,1)} %get-tuple-element.103), channel_id=1, source_target_pairs={{4,12},{12,20},{20,28},{8,0},{16,8},{24,16},{5,13},{13,21},{21,29}... | collective-permute-start | bytes 3145736 | tf_op jit(solution)/shard_map/ppermute | solution.py:606
  62.7 19.7 %collective-permute-start.10 = (bf16[2,384,512]{2,1,0:T(8,128)(2,1)}, bf16[2,384,512]{2,1,0:T(8,128)(2,1)}, u32[]{:S(2)}, u32[]{:S(2)}) collective-permute-start(bf16[2,384,512]{2,1,0:T(8,128)(2,1)} %get-tuple-element.72), channel_id=1, source_target_pairs={{0,2},{1,3},{2,0},{3,1},{4,6},{5,7},{6,4},{7,5},{8,10},{9,11},{10,... | collective-permute-start | bytes 2359304 | tf_op jit(solution)/shard_map/ppermute | solution.py:50
  81.8 17.8 %collective-permute-start.15 = (bf16[2,384,512]{2,1,0:T(8,128)(2,1)}, bf16[2,384,512]{2,1,0:T(8,128)(2,1)}, u32[]{:S(2)}, u32[]{:S(2)}) collective-permute-start(bf16[2,384,512]{2,1,0:T(8,128)(2,1)} %get-tuple-element.80), channel_id=1, source_target_pairs={{0,2},{1,3},{2,0},{3,1},{4,6},{5,7},{6,4},{7,5},{8,10},{9,11},{10,... | collective-permute-start | bytes 2359304 | tf_op jit(solution)/shard_map/ppermute | solution.py:50
  86.8 6.1 %collective-permute-start.13 = (bf16[256,1024]{1,0:T(8,128)(2,1)}, bf16[256,1024]{1,0:T(8,128)(2,1)}, u32[]{:S(2)}, u32[]{:S(2)}) collective-permute-start(bf16[256,1024]{1,0:T(8,128)(2,1)} %get-tuple-element.77), channel_id=1, source_target_pairs={{0,1},{1,0},{2,3},{3,2},{4,5},{5,4},{6,7},{7,6},{8,9},{9,8},{10,11... | collective-permute-start | bytes 1572872 | tf_op jit(solution)/shard_map/ppermute | solution.py:50
  86.8 6.1 %collective-permute-start.14 = (bf16[256,1024]{1,0:T(8,128)(2,1)}, bf16[256,1024]{1,0:T(8,128)(2,1)}, u32[]{:S(2)}, u32[]{:S(2)}) collective-permute-start(bf16[256,1024]{1,0:T(8,128)(2,1)} %get-tuple-element.78), channel_id=1, source_target_pairs={{0,1},{1,0},{2,3},{3,2},{4,5},{5,4},{6,7},{7,6},{8,9},{9,8},{10,11... | collective-permute-start | bytes 1572872 | tf_op jit(solution)/shard_map/ppermute | solution.py:50
  88.3 26.3 %collective-permute-start.9 = (bf16[256,2048]{1,0:T(8,128)(2,1)}, bf16[256,2048]{1,0:T(8,128)(2,1)}, u32[]{:S(2)}, u32[]{:S(2)}) collective-permute-start(bf16[256,2048]{1,0:T(8,128)(2,1)} %broadcast_select_fusion.5), channel_id=1, source_target_pairs={{0,4},{4,0},{8,12},{12,8},{16,20},{20,16},{24,28},{28,24},{1,5},{5... | collective-permute-start | bytes 3145736 | tf_op jit(solution)/shard_map/ppermute | solution.py:50
  90.7 24.0 %collective-permute-start.16 = (bf16[192,1024]{1,0:T(8,128)(2,1)}, bf16[192,1024]{1,0:T(8,128)(2,1)S(1)}, u32[]{:S(2)}, u32[]{:S(2)}) collective-permute-start(bf16[192,1024]{1,0:T(8,128)(2,1)} %get-tuple-element.74), channel_id=1, source_target_pairs={{0,8},{4,12},{8,0},{12,4},{16,24},{20,28},{24,16},{28,20},{1,9},{5... | collective-permute-start | bytes 1179656 | tf_op jit(solution)/shard_map/ppermute | solution.py:50
  102.0 12.7 %collective-permute-start.17 = (bf16[192,1024]{1,0:T(8,128)(2,1)}, bf16[192,1024]{1,0:T(8,128)(2,1)}, u32[]{:S(2)}, u32[]{:S(2)}) collective-permute-start(bf16[192,1024]{1,0:T(8,128)(2,1)} %get-tuple-element.82), channel_id=1, source_target_pairs={{0,8},{4,12},{8,0},{12,4},{16,24},{20,28},{24,16},{28,20},{1,9},{5... | collective-permute-start | bytes 1179656 | tf_op jit(solution)/shard_map/ppermute | solution.py:50
  104.4 37.9 %collective-permute-start.18 = (bf16[256,2048]{1,0:T(8,128)(2,1)S(1)}, bf16[256,2048]{1,0:T(8,128)(2,1)S(1)}, u32[]{:S(2)}, u32[]{:S(2)}) collective-permute-start(bf16[256,2048]{1,0:T(8,128)(2,1)S(1)} %broadcast_select_fusion), channel_id=1, source_target_pairs={{0,4},{4,0},{8,12},{12,8},{16,20},{20,16},{24,28},{28,24},{1,5},{5... | collective-permute-start | bytes 3145736 | tf_op jit(solution)/shard_map/ppermute | solution.py:50
  117.8 19.2 %collective-permute-start.20 = (bf16[96,2048]{1,0:T(8,128)(2,1)}, bf16[96,2048]{1,0:T(8,128)(2,1)S(1)}, u32[]{:S(2)}, u32[]{:S(2)}) collective-permute-start(bf16[96,2048]{1,0:T(8,128)(2,1)} %get-tuple-element.83), channel_id=1, source_target_pairs={{0,16},{4,20},{8,24},{12,28},{16,0},{20,4},{24,8},{28,12},{1,17},{... | collective-permute-start | bytes 1179656 | tf_op jit(solution)/shard_map/ppermute | solution.py:50
  135.7 6.6 %collective-permute-start.19 = (f32[16,2,256]{2,1,0:T(2,128)}, f32[16,2,256]{2,1,0:T(2,128)S(1)}, u32[]{:S(2)}, u32[]{:S(2)}) collective-permute-start(f32[16,2,256]{2,1,0:T(2,128)} %get-tuple-element.90), channel_id=1, source_target_pairs={{4,0},{8,4},{12,8},{16,12},{20,16},{24,20},{28,24},{5,1},{9,5},{13... | collective-permute-start | bytes 98312 | tf_op jit(solution)/shard_map/ppermute | solution.py:42
  139.7 13.4 %collective-permute-start.21 = (bf16[48,2048]{1,0:T(8,128)(2,1)}, bf16[48,2048]{1,0:T(8,128)(2,1)S(1)}, u32[]{:S(2)}, u32[]{:S(2)}) collective-permute-start(bf16[48,2048]{1,0:T(8,128)(2,1)} %get-tuple-element.99), channel_id=1, source_target_pairs={{0,4},{4,0},{8,12},{12,8},{16,20},{20,16},{24,28},{28,24},{1,5},{5... | collective-permute-start | bytes 589832 | tf_op jit(solution)/shard_map/ppermute | solution.py:50
  153.2 1.4 collective-permute-start.22
  (13 other events, 81.5 us)

commit v4 on v3

--- a/solution.py
+++ b/solution.py
@@ -236,21 +236,23 @@
 
     row = lax.broadcasted_iota(jnp.int32, (per, 2 * GROUP), 0).astype(F32)
 
-    def attend(index, file, u):
+    def first(index, file, u):
+        unit = file * groups + u
+        at = slice(unit * per, (unit + 1) * per)
+        tok = slice(u * GROUP, (u + 1) * GROUP)
+        cols = slice(index * PAIR, (index + 1) * PAIR)
+        keys, values = kv_ref[index, at, :PAIR], kv_ref[index, at, PAIR:]
+        queries, grads = diagonal(q_ref[file, tok, cols]), diagonal(g_ref[file, tok, cols])
+        return keys, values, queries, grads, mm(keys, queries, NT), mm(values, grads, NT)
+
+    def second(index, file, u, state):
+        keys, values, queries, grads, scores, prob_grad = state
         if u == 0:
             count = tail_ref[file, groups - 1 : groups, :].astype(F32)
         elif file:
             count = tail_ref[2, u - 1 : u, :].astype(F32)
         else:
             count = count_ref[u - 1].astype(F32)
-        unit = file * groups + u
-        at = slice(unit * per, (unit + 1) * per)
-        tok = slice(u * GROUP, (u + 1) * GROUP)
-        cols = slice(index * PAIR, (index + 1) * PAIR)
-        keys, values = kv_ref[index, at, :PAIR], kv_ref[index, at, PAIR:]
-        queries, grads = diagonal(q_ref[file, tok, cols]), diagonal(g_ref[file, tok, cols])
-        scores = mm(keys, queries, NT)
-        prob_grad = mm(values, grads, NT)
         scores = jnp.where(row < count * RLEN, scores, NEG)
         peak = jnp.max(scores, axis=0, keepdims=True)
         weight = jnp.exp2((scores - peak) * (SCALE * LOG2E))
@@ -259,7 +261,13 @@
         probs = weight * inverse
         delta = jnp.sum(probs * prob_grad, axis=0, keepdims=True)
         score_grad = (probs * (prob_grad - delta)).astype(BF)
-        low = probs.astype(BF)
+        return keys, values, queries, grads, probs.astype(BF), score_grad
+
+    def third(index, file, u, state):
+        keys, values, queries, grads, low, score_grad = state
+        unit = file * groups + u
+        at = slice(unit * per, (unit + 1) * per)
+        tok = slice(u * GROUP, (u + 1) * GROUP)
         out = mm(low, values, TN).astype(BF)
         dq = (mm(score_grad, keys, TN) * SCALE).astype(BF)
         for which, value in enumerate((out, dq)):
@@ -282,9 +290,15 @@
     for copy in waits_q:
         copy.wait()
     for index in range(TOGETHER):
-        for file in (0, 1):
-            for u in range(groups):
-                attend(index, file, u)
+        units = [(index, file, u) for file in (0, 1) for u in range(groups)]
+        ready, late = first(*units[0]), None
+        for number, unit in enumerate(units):
+            upcoming = first(*units[number + 1]) if number + 1 < len(units) else None
+            done = second(*unit, ready)
+            if late:
+                third(*late)
+            ready, late = upcoming, (*unit, done)
+        third(*late)
         if index + 1 < TOGETHER:
             project(index + 1)
         if index == 0:
@@ -357,13 +371,20 @@
     below = key_at <= query_at
     zero = jnp.zeros((half, half), BF)
     lo, hi = slice(0, half), slice(half, None)
-    for head in range(heads):
+
+    def first(head):
         at = slice(head * HD, (head + 1) * HD)
         queries, grads = q_ref[:, at], do_ref[:, at]
         kp, vp = keys_before[:, at], values_before[:, at]
         ko, vo = ko_ref[:, at], vo_ref[:, at]
-        sp, so = mm(kp, queries, NT), mm(ko, queries, NT)
-        gp, go = mm(vp, grads, NT), mm(vo, grads, NT)
+        return (
+            (queries, grads, kp, vp, ko, vo),
+            (mm(kp, queries, NT), mm(ko, queries, NT)),
+            (mm(vp, grads, NT), mm(vo, grads, NT)),
+        )
+
+    def second(head, state):
+        inputs, (sp, so), (gp, go) = state
         rows = []
         for a in (0, 1):
             if a == 0:
@@ -394,33 +415,35 @@
             stat_ref[head, 1:2, lanes] = delta
 
         def spread(which):
-            first, second = rows[0][which], rows[1][which]
+            one, two = rows[0][which], rows[1][which]
             before = jnp.concatenate(
-                [
-                    jnp.concatenate([first[0], zero], 1),
-                    jnp.concatenate([first[1], second[0]], 1),
-                ],
-                0,
+                [jnp.concatenate([one[0], zero], 1), jnp.concatenate([one[1], two[0]], 1)], 0
             )
             own = jnp.concatenate(
-                [
-                    jnp.concatenate([first[2], second[1]], 1),
-                    jnp.concatenate([zero, second[2]], 1),
-                ],
-                0,
+                [jnp.concatenate([one[2], two[1]], 1), jnp.concatenate([zero, two[2]], 1)], 0
             )
             return before, own
 
-        (pp, po), (dp, do) = spread(0), spread(1)
+        return inputs, spread(0), spread(1)
+
+    def third(head, state):
+        at = slice(head * HD, (head + 1) * HD)
+        (queries, grads, kp, vp, ko, vo), (pp, po), (dp, do) = state
         out = mm(pp, vp, TN) + mm(po, vo, TN) + crossed[:, at].astype(F32)
         out_ref[:, at] = out.astype(BF)
         dq_ref[:, at] = ((mm(dp, kp, TN) + mm(do, ko, TN)) * SCALE).astype(BF)
         dk_ref[:, at] = mm(do, queries, NN) * SCALE
         dv_ref[:, at] = mm(po, grads, NN)
 
+    ready = first(0)
+    for head in range(heads):
+        upcoming = first(head + 1) if head + 1 < heads else None
+        third(head, second(head, ready))
+        ready = upcoming
+
 
 def self_part(info, q, do, k, v, one, two, three, own, back):
-    heads = 2
+    heads = 4
     tokens, width = q.shape
     steps = width // (heads * HD)
     half = steps // 2
@@ -462,11 +485,15 @@
     above = key_at > query_at
     zero = jnp.zeros((half, half), BF)
     lo, hi = slice(0, half), slice(half, None)
-    for head in range(heads):
+
+    def first(head):
         at = slice(head * HD, (head + 1) * HD)
         queries, grads = all_queries[:, at], do_ref[:, at]
-        scores = mm(k_ref[:, at], queries, NT)
-        prob_grad = mm(v_ref[:, at], grads, NT)
+        return queries, grads, mm(k_ref[:, at], queries, NT), mm(v_ref[:, at], grads, NT)
+
+    def second(head, state):
+        at = slice(head * HD, (head + 1) * HD)
+        queries, grads, scores, prob_grad = state
         level, delta = stat_ref[head, 0:1, :], stat_ref[head, 1:2, :]
 
         def block(rows, lanes, mask):
@@ -476,11 +503,11 @@
             probs = jnp.exp2(exponent)
             return probs.astype(BF), (probs * (prob_grad[rows, lanes] - delta[:, lanes])).astype(BF)
 
-        first, middle, last = block(lo, lo, True), block(hi, lo, False), block(hi, hi, True)
+        one, middle, last = block(lo, lo, True), block(hi, lo, False), block(hi, hi, True)
         low, score_grad = [
             jnp.concatenate(
                 [
-                    jnp.concatenate([first[i], zero], 1),
+                    jnp.concatenate([one[i], zero], 1),
                     jnp.concatenate([middle[i], last[i]], 1),
                 ],
                 0,
@@ -490,9 +517,15 @@
         dk_ref[:, at] = (dkp_ref[:, at] + mm(score_grad, queries, NN) * SCALE).astype(BF)
         dv_ref[:, at] = (dvp_ref[:, at] + mm(low, grads, NN)).astype(BF)
 
+    ready = first(0)
+    for head in range(heads):
+        upcoming = first(head + 1) if head + 1 < heads else None
+        second(head, ready)
+        ready = upcoming
+
 
 def next_part(info, one, three, do, k, v, stats, dk, dv):
-    heads = 2
+    heads = 8
     tokens, width = k.shape
     spec = pl.BlockSpec((tokens, heads * HD), lambda p: (0, p))
     stat_spec = pl.BlockSpec((heads, 2, tokens), lambda p: (p, 0, 0))
@@ -607,6 +640,7 @@
 
     far_one = hop(pick(q, k))
     one = swap(pick(k, q), "seq", 1)
+    far_two = hop(pick(do, v))
 
     nb_last = after(nb_last, peer)
     peer_last = swap(nb_last, "fsdp", 1)
@@ -623,14 +657,13 @@
         if not group:
             turn = results[6]
             two = swap(pick(v, far_one, turn), "seq", 1)
-            far_two = hop(pick(do, v, turn))
         received = swap(send, *stages[0])
         for stage in range(1, split_at):
             keep, send = halve(info, [keep], [received], stages[stage])
             received = swap(send, *stages[stage])
         pairs.append((keep, received))
     own = held[:2]
-    back = [swap(x, "fsdp", 1) for x in after(held[2:], pairs[0][1], one, two, far_two)]
+    back = [swap(x, "fsdp", 1) for x in after(held[2:], pairs[0][1], one, two)]
     third = pick(far_one, far_two, pairs[-1][0])
     three = swap(third, "seq", 1)
 

time: 156 us -> 145 us (0.929)
  Pallas kernels: 80.3 us -> 66.1 us
  waiting for transfers between devices: 31.7 us -> 33.5 us
    pallas_call x2, Pallas kernels: 37.8 us -> 30.5 us  [cross(): pl.pallas_call(functools.partial(cross_kernel, group, turns, len(weights)...]
    pallas_call x1, Pallas kernels: 9.64 us -> 6.14 us  [next_part(): pl.pallas_call(functools.partial(next_kernel, heads), grid=(width // (hea...]
    pallas_call x1, Pallas kernels: 15.3 us -> 12 us  [self_part(): pl.pallas_call(functools.partial(self_kernel, heads), grid_spec=pltpu.Pre...]
    ppermute x19, waiting for transfers between devices: 24.9 us -> 27.9 us  [swap(): lax.ppermute(value, axis, [(i, i ^ bit) for i in range(lax.axis_size(axis...]
  transfers between devices with their start and end apart: 23 -> 23, of which waited for: 8 -> 9; matrix products, arithmetic and copies ran while one was open for 3% -> 3% of each run, Pallas kernels for 49% -> 43%
where the time goes in v4:
time: 145 us; the launch traced here: 144 us
  Pallas kernels  66.1 us (46%)
  starting transfers between devices  34.6 us (24%)
  waiting for transfers between devices  33.5 us (23%)
  other arithmetic  5.77 us (4%)
  local copies, waits for them, and re-layouts  3.6 us (2%)
    pallas_call x2, Pallas kernels, cross(): pl.pallas_call(functools.partial(cross_kernel, group, turns, len(weights)...  30.5 us
    ppermute x19, waiting for transfers between devices, swap(): lax.ppermute(value, axis, [(i, i ^ bit) for i in range(lax.axis_size(axis...  27.9 us
    ppermute x19, starting transfers between devices, swap(): lax.ppermute(value, axis, [(i, i ^ bit) for i in range(lax.axis_size(axis...  25 us
    pallas_call x1, Pallas kernels, self_part(): pl.pallas_call(functools.partial(self_kernel, heads), grid_spec=pltpu.Pre...  12 us
    pallas_call x4, Pallas kernels, halve(): pl.pallas_call(functools.partial(halve_kernel, spans, axis, bit), in_spec...  9.09 us
    ppermute x2, starting transfers between devices, shift(): lax.ppermute(value, axis, [(i, i + steps) for i in range(first, last)])  6.83 us
    pallas_call x1, Pallas kernels, next_part(): pl.pallas_call(functools.partial(next_kernel, heads), grid=(width // (hea...  6.14 us
    select_n x4, other arithmetic, pick(): return jnp.where(after(even, nb_last, *others), when_even, when_odd)  4.25 us
  transfers between devices with their start and end apart: 23, of which 9 were waited for; matrix products, arithmetic and copies ran while one was open for 3% of the time, Pallas kernels for 43%

profile of v4, /device:TPU:0, one launch (start us, length us, event | category | flops | bytes accessed | tf_op | source)
XLA Modules:
  0.0 144.4 jit_solution(16235444707989994084)
XLA Ops:
  4.4 3.9 %shard_map.137 = (bf16[2,192,512]{2,1,0:T(8,128)(2,1)}, bf16[2,192,512]{2,1,0:T(8,128)(2,1)}, bf16[4,192,512]{2,1,0:T(8,128)(2,1)}, bf16[2,272,1024]{2,1,0:T(8,128)(2,1)}) custom-call(s32[2]{0:T(128)} %pad_add_fusion.info_ref, s32[4]{0:T(128)} %bitcast.39, bf16[192,4096]{1,0:T(8,128)(2,1)} %refs_3_.1, bf16[192,4096]{1,0:T(8,128)(2,1)} %refs_3_.1, ...), custom_call_target="tpu_custom_call" | custom-call | flops 3000000000 | bytes 1000 | tf_op jit(solution)/shard_map/pallas_call | solution.py:112
  8.8 5.5 %collective-permute-start = (bf16[272,768]{1,0:T(8,128)(2,1)}, bf16[272,768]{1,0:T(8,128)(2,1)}, u32[]{:S(2)}, u32[]{:S(2)}) collective-permute-start(bf16[272,768]{1,0:T(8,128)(2,1)} %shard_map.136), channel_id=1, source_target_pairs={{0,4},{4,8},{8,12},{12,16},{16,20},{20,24},{24,28},{1,5},{5,9},{9,... | collective-permute-start | bytes 1253384 | tf_op jit(solution)/shard_map/ppermute | solution.py:42
  15.3 2.7 %shard_map.138 = (bf16[2,384,512]{2,1,0:T(8,128)(2,1)}, bf16[2,384,512]{2,1,0:T(8,128)(2,1)}) custom-call(bf16[2,192,512]{2,1,0:T(8,128)(2,1)} %get-tuple-element.56.refs_0_.refs_5_, bf16[2,192,512]{2,1,0:T(8,128)(2,1)} %get-tuple-element.58.refs_1_.refs_5_, bf16[4,192,512]{2,1,0:T(8,128)(2,1)} %copy-done.10), custom_call_target="tpu_custom_call" | custom-call | flops 2000000000 | bytes 1000 | tf_op jit(solution)/shard_map/pallas_call | solution.py:143
  19.5 3.7 %collective-permute-done.refs_1_ = bf16[272,768]{1,0:T(8,128)(2,1)} collective-permute-done((bf16[272,768]{1,0:T(8,128)(2,1)}, bf16[272,768]{1,0:T(8,128)(2,1)}, u32[]{:S(2)}, u32[]{:S(2)}) %collective-permute-start) | collective-permute-done | bytes 417824 | tf_op jit(solution)/shard_map/ppermute | solution.py:42
  26.1 4.8 %collective-permute-start.11 = (bf16[256,2048]{1,0:T(8,128)(2,1)}, bf16[256,2048]{1,0:T(8,128)(2,1)}, u32[]{:S(2)}, u32[]{:S(2)}) collective-permute-start(bf16[256,2048]{1,0:T(8,128)(2,1)} %get-tuple-element.100), channel_id=1, source_target_pairs={{0,4},{4,0},{8,12},{12,8},{16,20},{20,16},{24,28},{28,24},{1,5},{5... | collective-permute-start | bytes 3145736 | tf_op jit(solution)/shard_map/ppermute | solution.py:50
  32.4 6.3 %collective-permute-done.5.refs_7_ = bf16[2,384,512]{2,1,0:T(8,128)(2,1)} collective-permute-done((bf16[2,384,512]{2,1,0:T(8,128)(2,1)}, bf16[2,384,512]{2,1,0:T(8,128)(2,1)}, u32[]{:S(2)}, u32[]{:S(2)}) %collective-permute-start.5) | collective-permute-done | bytes 786464 | tf_op jit(solution)/shard_map/ppermute | solution.py:50
  38.7 16.5 %shard_map.139 = (bf16[256,1024]{1,0:T(8,128)(2,1)}, bf16[256,1024]{1,0:T(8,128)(2,1)}, bf16[256,1024]{1,0:T(8,128)(2,1)}, bf16[256,1024]{1,0:T(8,128)(2,1)}, bf...) custom-call(s32[2]{0:T(128)} %pad_add_fusion.info_ref, s32[4]{0:T(128)} %bitcast.40, ...), custom_call_target="tpu_custom_call" | custom-call | flops 8999999488 | bytes 1000 | tf_op jit(solution)/shard_map/pallas_call | solution.py:328
  60.6 14.0 %shard_map.140 = (bf16[256,1024]{1,0:T(8,128)(2,1)}, bf16[256,1024]{1,0:T(8,128)(2,1)}, bf16[256,1024]{1,0:T(8,128)(2,1)}, bf16[256,1024]{1,0:T(8,128)(2,1)}, bf...) custom-call(s32[2]{0:T(128)} %pad_add_fusion.info_ref, ...), custom_call_target="tpu_custom_call", output_to_operand_aliasing={{0}: (13, {}), {1}: (14, {}), {2}: (15, {}), {3}: (16, {})} | custom-call | flops 8999999488 | bytes 1000 | tf_op jit(solution)/shard_map/pallas_call | solution.py:328
  75.2 3.4 %collective-permute-done.10.refs_1_ = bf16[2,384,512]{2,1,0:T(8,128)(2,1)} collective-permute-done((bf16[2,384,512]{2,1,0:T(8,128)(2,1)}, bf16[2,384,512]{2,1,0:T(8,128)(2,1)}, u32[]{:S(2)}, u32[]{:S(2)}) %collective-permute-start.10) | collective-permute-done | bytes 786464 | tf_op jit(solution)/shard_map/ppermute | solution.py:50
  78.7 2.0 %collective-permute-done.12.two_ref = bf16[256,2048]{1,0:T(8,128)(2,1)S(1)} collective-permute-done((bf16[256,2048]{1,0:T(8,128)(2,1)}, bf16[256,2048]{1,0:T(8,128)(2,1)S(1)}, u32[]{:S(2)}, u32[]{:S(2)}) %collective-permute-start.12) | collective-permute-done | bytes 1048608 | tf_op jit(solution)/shard_map/ppermute | solution.py:50
  81.2 1.8 %collective-permute-done.8 = bf16[256,2048]{1,0:T(8,128)(2,1)S(1)} collective-permute-done((bf16[256,2048]{1,0:T(8,128)(2,1)}, bf16[256,2048]{1,0:T(8,128)(2,1)S(1)}, u32[]{:S(2)}, u32[]{:S(2)}) %collective-permute-start.8) | collective-permute-done | bytes 1048608 | tf_op jit(solution)/shard_map/ppermute | solution.py:639
  84.4 2.4 %shard_map.141 = (bf16[192,1024]{1,0:T(8,128)(2,1)}, bf16[192,1024]{1,0:T(8,128)(2,1)}) custom-call(s32[2]{0:T(128)} %pad_add_fusion.info_ref, bf16[2,384,512]{2,1,0:T(8,128)(2,1)} %get-tuple-element.70.refs_0_, bf16[2,384,512]{2,1,0:T(8,128)(2,1)} %collective-permute-done.10.refs_1_), custom_call_target="tpu_custom_call" | custom-call | flops 1000000000 | bytes 1000 | tf_op jit(solution)/shard_map/pallas_call | solution.py:599
  86.8 2.4 %collective-permute-start.16 = (bf16[192,1024]{1,0:T(8,128)(2,1)}, bf16[192,1024]{1,0:T(8,128)(2,1)S(1)}, u32[]{:S(2)}, u32[]{:S(2)}) collective-permute-start(bf16[192,1024]{1,0:T(8,128)(2,1)} %get-tuple-element.73), channel_id=1, source_target_pairs={{0,8},{4,12},{8,0},{12,4},{16,24},{20,28},{24,16},{28,20},{1,9},{5... | collective-permute-start | bytes 1179656 | tf_op jit(solution)/shard_map/ppermute | solution.py:50
  89.2 4.8 %collective-permute-done.15.refs_1_ = bf16[2,384,512]{2,1,0:T(8,128)(2,1)} collective-permute-done((bf16[2,384,512]{2,1,0:T(8,128)(2,1)}, bf16[2,384,512]{2,1,0:T(8,128)(2,1)}, u32[]{:S(2)}, u32[]{:S(2)}) %collective-permute-start.15) | collective-permute-done | bytes 786464 | tf_op jit(solution)/shard_map/ppermute | solution.py:50
  94.0 2.4 %shard_map.142 = (bf16[192,1024]{1,0:T(8,128)(2,1)}, bf16[192,1024]{1,0:T(8,128)(2,1)}) custom-call(s32[2]{0:T(128)} %pad_add_fusion.info_ref, bf16[2,384,512]{2,1,0:T(8,128)(2,1)} %get-tuple-element.66.refs_0_, bf16[2,384,512]{2,1,0:T(8,128)(2,1)} %collective-permute-done.15.refs_1_), custom_call_target="tpu_custom_call" | custom-call | flops 1000000000 | bytes 1000 | tf_op jit(solution)/shard_map/pallas_call | solution.py:599
  96.4 2.4 %collective-permute-start.17 = (bf16[192,1024]{1,0:T(8,128)(2,1)}, bf16[192,1024]{1,0:T(8,128)(2,1)}, u32[]{:S(2)}, u32[]{:S(2)}) collective-permute-start(bf16[192,1024]{1,0:T(8,128)(2,1)} %get-tuple-element.82), channel_id=1, source_target_pairs={{0,8},{4,12},{8,0},{12,4},{16,24},{20,28},{24,16},{28,20},{1,9},{5... | collective-permute-start | bytes 1179656 | tf_op jit(solution)/shard_map/ppermute | solution.py:50
  98.9 2.3 %collective-permute-start.18 = (bf16[256,2048]{1,0:T(8,128)(2,1)S(1)}, bf16[256,2048]{1,0:T(8,128)(2,1)S(1)}, u32[]{:S(2)}, u32[]{:S(2)}) collective-permute-start(bf16[256,2048]{1,0:T(8,128)(2,1)S(1)} %broadcast_select_fusion), channel_id=1, source_target_pairs={{0,4},{4,0},{8,12},{12,8},{16,20},{20,16},{24,28},{28,24},{1,5},{5... | collective-permute-start | bytes 3145736 | tf_op jit(solution)/shard_map/ppermute | solution.py:50
  101.2 9.3 %collective-permute-done.9.three_ref = bf16[256,2048]{1,0:T(8,128)(2,1)} collective-permute-done((bf16[256,2048]{1,0:T(8,128)(2,1)}, bf16[256,2048]{1,0:T(8,128)(2,1)}, u32[]{:S(2)}, u32[]{:S(2)}) %collective-permute-start.9) | collective-permute-done | bytes 1048608 | tf_op jit(solution)/shard_map/ppermute | solution.py:50
  111.2 2.4 %shard_map.143 = (bf16[96,2048]{1,0:T(8,128)(2,1)}, bf16[96,2048]{1,0:T(8,128)(2,1)}) custom-call(s32[2]{0:T(128)} %pad_add_fusion.info_ref, bf16[192,1024]{1,0:T(8,128)(2,1)} %get-tuple-element.72.refs_0_, bf16[192,1024]{1,0:T(8,128)(2,1)} %get-tuple-element.81.refs_1_, bf16[192,1024]{1,0:T(8,128)(2,1)} %copy-done.11, ...), custom_call_target="tpu_custom_call" | custom-call | flops 1000000000 | bytes 1000 | tf_op jit(solution)/shard_map/pallas_call | solution.py:599
  113.6 2.6 %collective-permute-start.20 = (bf16[96,2048]{1,0:T(8,128)(2,1)}, bf16[96,2048]{1,0:T(8,128)(2,1)S(1)}, u32[]{:S(2)}, u32[]{:S(2)}) collective-permute-start(bf16[96,2048]{1,0:T(8,128)(2,1)} %get-tuple-element.83), channel_id=1, source_target_pairs={{0,16},{4,20},{8,24},{12,28},{16,0},{20,4},{24,8},{28,12},{1,17},{... | collective-permute-start | bytes 1179656 | tf_op jit(solution)/shard_map/ppermute | solution.py:50
  116.2 12.0 %shard_map.144 = (bf16[256,2048]{1,0:T(8,128)(2,1)}, bf16[256,2048]{1,0:T(8,128)(2,1)}, bf16[256,2048]{1,0:T(8,128)(2,1)}, f32[256,2048]{1,0:T(8,128)}, f32[256,2048]{1,0:T(8,128)}, /*index=5*/f32[16,2,256]{2,1,0:T(2,128)}) custom-call(s32[2]{0:T(128)} %pad_add_fusion.info_ref, bf16[256,2048]{1,0:T(8,128)(2,1)} %bitcast.26, bf16[256,2048]{1,0:T(8,128)(2,1)} %bitcast.25, ...), custom_call_target="tpu_custom_call" | custom-call | flops 14000000000 | bytes 1000 | tf_op jit(solution)/shard_map/pallas_call | solution.py:462
  130.3 1.9 %shard_map.146 = (bf16[48,2048]{1,0:T(8,128)(2,1)}, bf16[48,2048]{1,0:T(8,128)(2,1)}) custom-call(s32[2]{0:T(128)} %pad_add_fusion.info_ref, bf16[96,2048]{1,0:T(8,128)(2,1)} %get-tuple-element.97.refs_0_, bf16[96,2048]{1,0:T(8,128)(2,1)} %copy-done.12), custom_call_target="tpu_custom_call" | custom-call | flops 1000000000 | bytes 1000 | tf_op jit(solution)/shard_map/pallas_call | solution.py:599
  132.2 2.6 %collective-permute-start.21 = (bf16[48,2048]{1,0:T(8,128)(2,1)}, bf16[48,2048]{1,0:T(8,128)(2,1)S(1)}, u32[]{:S(2)}, u32[]{:S(2)}) collective-permute-start(bf16[48,2048]{1,0:T(8,128)(2,1)} %get-tuple-element.99), channel_id=1, source_target_pairs={{0,4},{4,0},{8,12},{12,8},{16,20},{20,16},{24,28},{28,24},{1,5},{5... | collective-permute-start | bytes 589832 | tf_op jit(solution)/shard_map/ppermute | solution.py:50
  135.9 6.1 %shard_map.145 = (bf16[256,2048]{1,0:T(8,128)(2,1)}, bf16[256,2048]{1,0:T(8,128)(2,1)}) custom-call(s32[2]{0:T(128)} %pad_add_fusion.info_ref, bf16[256,2048]{1,0:T(8,128)(2,1)} %collective-permute-done.11.one_ref, bf16[256,2048]{1,0:T(8,128)(2,1)} %collective-permute-done.9.three_ref, bf16[256,2048]{1,0:T(8,128)(2,1)} %copy-done.9, ...), custom_call_target="tpu_custom_call" | custom-call | flops 8000000000 | bytes 1000 | tf_op jit(solution)/shard_map/pallas_call | solution.py:533
  (73 shorter events, 25.2 us)
Async XLA Ops:
  0.6 3.8 %collective-permute-start.1 = (bf16[4,256,768]{2,1,0:T(8,128)(2,1)}, bf16[4,256,768]{2,1,0:T(8,128)(2,1)S(1)}, u32[]{:S(2)}, u32[]{:S(2)}) collective-permute-start(bf16[4,256,768]{2,1,0:T(8,128)(2,1)} %bitcast.31), channel_id=1, source_target_pairs={{0,1},{1,0},{2,3},{3,2},{4,5},{5,4},{6,7},{7,6},{8,9},{9,8},{10,11... | collective-permute-start | bytes 4718600 | tf_op jit(solution)/shard_map/ppermute | solution.py:50
  8.3 14.8 %collective-permute-start.2 = (bf16[2,272,1024]{2,1,0:T(8,128)(2,1)}, bf16[2,272,1024]{2,1,0:T(8,128)(2,1)S(1)}, u32[]{:S(2)}, u32[]{:S(2)}) collective-permute-start(bf16[2,272,1024]{2,1,0:T(8,128)(2,1)} %get-tuple-element.54), channel_id=1, source_target_pairs={{0,1},{1,0},{2,3},{3,2},{4,5},{5,4},{6,7},{7,6},{8,9},{9,8},{10,11... | collective-permute-start | bytes 3342344 | tf_op jit(solution)/shard_map/ppermute | solution.py:50
  8.7 5.7 %collective-permute-start.4 = (bf16[4,192,512]{2,1,0:T(8,128)(2,1)}, bf16[4,192,512]{2,1,0:T(8,128)(2,1)S(1)}, u32[]{:S(2)}, u32[]{:S(2)}) collective-permute-start(bf16[4,192,512]{2,1,0:T(8,128)(2,1)} %get-tuple-element.57), channel_id=1, source_target_pairs={{0,1},{1,0},{2,3},{3,2},{4,5},{5,4},{6,7},{7,6},{8,9},{9,8},{10,11... | collective-permute-start | bytes 2359304 | tf_op jit(solution)/shard_map/ppermute | solution.py:50
  8.8 14.3 %collective-permute-start = (bf16[272,768]{1,0:T(8,128)(2,1)}, bf16[272,768]{1,0:T(8,128)(2,1)}, u32[]{:S(2)}, u32[]{:S(2)}) collective-permute-start(bf16[272,768]{1,0:T(8,128)(2,1)} %shard_map.136), channel_id=1, source_target_pairs={{0,4},{4,8},{8,12},{12,16},{16,20},{20,24},{24,28},{1,5},{5,9},{9,... | collective-permute-start | bytes 1253384 | tf_op jit(solution)/shard_map/ppermute | solution.py:42
  18.0 20.7 %collective-permute-start.5 = (bf16[2,384,512]{2,1,0:T(8,128)(2,1)}, bf16[2,384,512]{2,1,0:T(8,128)(2,1)}, u32[]{:S(2)}, u32[]{:S(2)}) collective-permute-start(bf16[2,384,512]{2,1,0:T(8,128)(2,1)} %get-tuple-element.59), channel_id=1, source_target_pairs={{0,2},{1,3},{2,0},{3,1},{4,6},{5,7},{6,4},{7,5},{8,10},{9,11},{10,... | collective-permute-start | bytes 2359304 | tf_op jit(solution)/shard_map/ppermute | solution.py:50
  23.1 9.3 %collective-permute-start.3 = (bf16[272,768]{1,0:T(8,128)(2,1)}, bf16[272,768]{1,0:T(8,128)(2,1)}, u32[]{:S(2)}, u32[]{:S(2)}) collective-permute-start(bf16[272,768]{1,0:T(8,128)(2,1)} %collective-permute-done.refs_1_), channel_id=1, source_target_pairs={{0,1},{1,0},{2,3},{3,2},{4,5},{5,4},{6,7},{7,6},{8,9},{9,8},{10,11... | collective-permute-start | bytes 1253384 | tf_op jit(solution)/shard_map/ppermute | solution.py:50
  24.8 30.4 %collective-permute-start.7 = (bf16[256,2048]{1,0:T(8,128)(2,1)}, bf16[256,2048]{1,0:T(8,128)(2,1)S(1)}, u32[]{:S(2)}, u32[]{:S(2)}) collective-permute-start(bf16[256,2048]{1,0:T(8,128)(2,1)} %get-tuple-element.101), channel_id=1, source_target_pairs={{4,12},{12,20},{20,28},{8,0},{16,8},{24,16},{5,13},{13,21},{21,29}... | collective-permute-start | bytes 3145736 | tf_op jit(solution)/shard_map/ppermute | solution.py:639
  26.1 49.1 %collective-permute-start.11 = (bf16[256,2048]{1,0:T(8,128)(2,1)}, bf16[256,2048]{1,0:T(8,128)(2,1)}, u32[]{:S(2)}, u32[]{:S(2)}) collective-permute-start(bf16[256,2048]{1,0:T(8,128)(2,1)} %get-tuple-element.100), channel_id=1, source_target_pairs={{0,4},{4,0},{8,12},{12,8},{16,20},{20,16},{24,28},{28,24},{1,5},{5... | collective-permute-start | bytes 3145736 | tf_op jit(solution)/shard_map/ppermute | solution.py:50
  30.9 24.4 %copy-start.4 = (bf16[1,256,2048]{2,1,0:T(8,128)(2,1)S(1)}, bf16[1,256,2048]{2,1,0:T(8,128)(2,1)}, u32[]{:S(2)}) copy-start(bf16[1,256,2048]{2,1,0:T(8,128)(2,1)} %param.11) | copy-start | bytes 3145732
  30.9 29.8 %collective-permute-start.6 = (bf16[2,384,512]{2,1,0:T(8,128)(2,1)}, bf16[2,384,512]{2,1,0:T(8,128)(2,1)}, u32[]{:S(2)}, u32[]{:S(2)}) collective-permute-start(bf16[2,384,512]{2,1,0:T(8,128)(2,1)} %get-tuple-element.61), channel_id=1, source_target_pairs={{0,2},{1,3},{2,0},{3,1},{4,6},{5,7},{6,4},{7,5},{8,10},{9,11},{10,... | collective-permute-start | bytes 2359304 | tf_op jit(solution)/shard_map/ppermute | solution.py:50
  56.7 23.9 %collective-permute-start.12 = (bf16[256,2048]{1,0:T(8,128)(2,1)}, bf16[256,2048]{1,0:T(8,128)(2,1)S(1)}, u32[]{:S(2)}, u32[]{:S(2)}) collective-permute-start(bf16[256,2048]{1,0:T(8,128)(2,1)} %get-tuple-element.102), channel_id=1, source_target_pairs={{0,4},{4,0},{8,12},{12,8},{16,20},{20,16},{24,28},{28,24},{1,5},{5... | collective-permute-start | bytes 3145736 | tf_op jit(solution)/shard_map/ppermute | solution.py:50
  57.6 25.4 %collective-permute-start.8 = (bf16[256,2048]{1,0:T(8,128)(2,1)}, bf16[256,2048]{1,0:T(8,128)(2,1)S(1)}, u32[]{:S(2)}, u32[]{:S(2)}) collective-permute-start(bf16[256,2048]{1,0:T(8,128)(2,1)} %get-tuple-element.103), channel_id=1, source_target_pairs={{4,12},{12,20},{20,28},{8,0},{16,8},{24,16},{5,13},{13,21},{21,29}... | collective-permute-start | bytes 3145736 | tf_op jit(solution)/shard_map/ppermute | solution.py:639
  59.1 19.6 %collective-permute-start.10 = (bf16[2,384,512]{2,1,0:T(8,128)(2,1)}, bf16[2,384,512]{2,1,0:T(8,128)(2,1)}, u32[]{:S(2)}, u32[]{:S(2)}) collective-permute-start(bf16[2,384,512]{2,1,0:T(8,128)(2,1)} %get-tuple-element.71), channel_id=1, source_target_pairs={{0,2},{1,3},{2,0},{3,1},{4,6},{5,7},{6,4},{7,5},{8,10},{9,11},{10,... | collective-permute-start | bytes 2359304 | tf_op jit(solution)/shard_map/ppermute | solution.py:50
  74.6 19.4 %collective-permute-start.15 = (bf16[2,384,512]{2,1,0:T(8,128)(2,1)}, bf16[2,384,512]{2,1,0:T(8,128)(2,1)}, u32[]{:S(2)}, u32[]{:S(2)}) collective-permute-start(bf16[2,384,512]{2,1,0:T(8,128)(2,1)} %get-tuple-element.80), channel_id=1, source_target_pairs={{0,2},{1,3},{2,0},{3,1},{4,6},{5,7},{6,4},{7,5},{8,10},{9,11},{10,... | collective-permute-start | bytes 2359304 | tf_op jit(solution)/shard_map/ppermute | solution.py:50
  80.7 8.5 %collective-permute-start.13 = (bf16[256,1024]{1,0:T(8,128)(2,1)}, bf16[256,1024]{1,0:T(8,128)(2,1)}, u32[]{:S(2)}, u32[]{:S(2)}) collective-permute-start(bf16[256,1024]{1,0:T(8,128)(2,1)} %get-tuple-element.77), channel_id=1, source_target_pairs={{0,1},{1,0},{2,3},{3,2},{4,5},{5,4},{6,7},{7,6},{8,9},{9,8},{10,11... | collective-permute-start | bytes 1572872 | tf_op jit(solution)/shard_map/ppermute | solution.py:50
  80.7 8.5 %collective-permute-start.14 = (bf16[256,1024]{1,0:T(8,128)(2,1)}, bf16[256,1024]{1,0:T(8,128)(2,1)}, u32[]{:S(2)}, u32[]{:S(2)}) collective-permute-start(bf16[256,1024]{1,0:T(8,128)(2,1)} %get-tuple-element.78), channel_id=1, source_target_pairs={{0,1},{1,0},{2,3},{3,2},{4,5},{5,4},{6,7},{7,6},{8,9},{9,8},{10,11... | collective-permute-start | bytes 1572872 | tf_op jit(solution)/shard_map/ppermute | solution.py:50
  84.1 26.4 %collective-permute-start.9 = (bf16[256,2048]{1,0:T(8,128)(2,1)}, bf16[256,2048]{1,0:T(8,128)(2,1)}, u32[]{:S(2)}, u32[]{:S(2)}) collective-permute-start(bf16[256,2048]{1,0:T(8,128)(2,1)} %broadcast_select_fusion.5), channel_id=1, source_target_pairs={{0,4},{4,0},{8,12},{12,8},{16,20},{20,16},{24,28},{28,24},{1,5},{5... | collective-permute-start | bytes 3145736 | tf_op jit(solution)/shard_map/ppermute | solution.py:50
  86.8 23.7 %collective-permute-start.16 = (bf16[192,1024]{1,0:T(8,128)(2,1)}, bf16[192,1024]{1,0:T(8,128)(2,1)S(1)}, u32[]{:S(2)}, u32[]{:S(2)}) collective-permute-start(bf16[192,1024]{1,0:T(8,128)(2,1)} %get-tuple-element.73), channel_id=1, source_target_pairs={{0,8},{4,12},{8,0},{12,4},{16,24},{20,28},{24,16},{28,20},{1,9},{5... | collective-permute-start | bytes 1179656 | tf_op jit(solution)/shard_map/ppermute | solution.py:50
  96.4 14.1 %collective-permute-start.17 = (bf16[192,1024]{1,0:T(8,128)(2,1)}, bf16[192,1024]{1,0:T(8,128)(2,1)}, u32[]{:S(2)}, u32[]{:S(2)}) collective-permute-start(bf16[192,1024]{1,0:T(8,128)(2,1)} %get-tuple-element.82), channel_id=1, source_target_pairs={{0,8},{4,12},{8,0},{12,4},{16,24},{20,28},{24,16},{28,20},{1,9},{5... | collective-permute-start | bytes 1179656 | tf_op jit(solution)/shard_map/ppermute | solution.py:50
  98.9 36.0 %collective-permute-start.18 = (bf16[256,2048]{1,0:T(8,128)(2,1)S(1)}, bf16[256,2048]{1,0:T(8,128)(2,1)S(1)}, u32[]{:S(2)}, u32[]{:S(2)}) collective-permute-start(bf16[256,2048]{1,0:T(8,128)(2,1)S(1)} %broadcast_select_fusion), channel_id=1, source_target_pairs={{0,4},{4,0},{8,12},{12,8},{16,20},{20,16},{24,28},{28,24},{1,5},{5... | collective-permute-start | bytes 3145736 | tf_op jit(solution)/shard_map/ppermute | solution.py:50
  113.6 15.9 %collective-permute-start.20 = (bf16[96,2048]{1,0:T(8,128)(2,1)}, bf16[96,2048]{1,0:T(8,128)(2,1)S(1)}, u32[]{:S(2)}, u32[]{:S(2)}) collective-permute-start(bf16[96,2048]{1,0:T(8,128)(2,1)} %get-tuple-element.83), channel_id=1, source_target_pairs={{0,16},{4,20},{8,24},{12,28},{16,0},{20,4},{24,8},{28,12},{1,17},{... | collective-permute-start | bytes 1179656 | tf_op jit(solution)/shard_map/ppermute | solution.py:50
  128.2 6.6 %collective-permute-start.19 = (f32[16,2,256]{2,1,0:T(2,128)}, f32[16,2,256]{2,1,0:T(2,128)S(1)}, u32[]{:S(2)}, u32[]{:S(2)}) collective-permute-start(f32[16,2,256]{2,1,0:T(2,128)} %get-tuple-element.90), channel_id=1, source_target_pairs={{4,0},{8,4},{12,8},{16,12},{20,16},{24,20},{28,24},{5,1},{9,5},{13... | collective-permute-start | bytes 98312 | tf_op jit(solution)/shard_map/ppermute | solution.py:42
  132.2 9.9 %collective-permute-start.21 = (bf16[48,2048]{1,0:T(8,128)(2,1)}, bf16[48,2048]{1,0:T(8,128)(2,1)S(1)}, u32[]{:S(2)}, u32[]{:S(2)}) collective-permute-start(bf16[48,2048]{1,0:T(8,128)(2,1)} %get-tuple-element.99), channel_id=1, source_target_pairs={{0,4},{4,0},{8,12},{12,8},{16,20},{20,16},{24,28},{28,24},{1,5},{5... | collective-permute-start | bytes 589832 | tf_op jit(solution)/shard_map/ppermute | solution.py:50
  142.2 1.4 collective-permute-start.22
  (13 other events, 71.3 us)

commit v5 on v4

--- a/solution.py
+++ b/solution.py
@@ -656,7 +656,8 @@
         held, (keep, send) = results[:4], results[4:6]
         if not group:
             turn = results[6]
-            two = swap(pick(v, far_one, turn), "seq", 1)
+            second_load = pick(v, far_one, turn)
+            two = swap(second_load, "seq", 1)
         received = swap(send, *stages[0])
         for stage in range(1, split_at):
             keep, send = halve(info, [keep], [received], stages[stage])
@@ -664,7 +665,7 @@
         pairs.append((keep, received))
     own = held[:2]
     back = [swap(x, "fsdp", 1) for x in after(held[2:], pairs[0][1], one, two)]
-    third = pick(far_one, far_two, pairs[-1][0])
+    third = pick(far_one, far_two, pairs[-1][0], second_load)
     three = swap(third, "seq", 1)
 
     halves = [halve(info, [pairs[0][0]], [pairs[0][1]], stages[split_at])]
@@ -675,7 +676,7 @@
     got.append(swap(halves[1][1], *stages[split_at]))
     four = swap(pick(far_two, do, halves[1][1], third), "seq", 1)
     keeps = [keep for keep, _ in halves]
-    keep, send = halve(after(info, three), keeps, got, stages[split_at + 1])
+    keep, send = halve(info, keeps, got, stages[split_at + 1])
     keeps, got = [keep], [swap(send, *stages[split_at + 1])]
     block_out, query_grad, cross_grad, dk, dv, stats = self_part(
         after(info, send), q, do, k, v, one, two, three, own, back
@@ -686,7 +687,7 @@
     for stage in range(split_at + 2, len(stages)):
         keep, send = halve(after(info, stats), keeps, got, stages[stage])
         keeps, got = [keep], [swap(send, *stages[stage])]
-    total = keeps[0].astype(F32) + got[0].astype(F32)
+    total = keeps[0].astype(F32) + after(got[0], key_grad).astype(F32)
     core = shard % 2
     away = swap(take_half(total, 1 - core).astype(BF), "fsdp", 1).astype(F32)
     nearby = take_half(total, core)

time: 145 us -> 143 us (0.986)
  transfers between devices with their start and end apart: 23 -> 23, of which waited for: 9 -> 10; matrix products, arithmetic and copies ran while one was open for 3% -> 3% of each run, Pallas kernels for 43% -> 44%
where the time goes in v5:
time: 143 us; the launch traced here: 142 us
  Pallas kernels  66.1 us (46%)
  starting transfers between devices  34.4 us (24%)
  waiting for transfers between devices  32.2 us (23%)
  other arithmetic  5.77 us (4%)
  local copies, waits for them, and re-layouts  2.86 us (2%)
    pallas_call x2, Pallas kernels, cross(): pl.pallas_call(functools.partial(cross_kernel, group, turns, len(weights)...  30.5 us
    ppermute x19, waiting for transfers between devices, swap(): lax.ppermute(value, axis, [(i, i ^ bit) for i in range(lax.axis_size(axis...  26.7 us
    ppermute x19, starting transfers between devices, swap(): lax.ppermute(value, axis, [(i, i ^ bit) for i in range(lax.axis_size(axis...  24.9 us
    pallas_call x1, Pallas kernels, self_part(): pl.pallas_call(functools.partial(self_kernel, heads), grid_spec=pltpu.Pre...  12 us
    pallas_call x4, Pallas kernels, halve(): pl.pallas_call(functools.partial(halve_kernel, spans, axis, bit), in_spec...  9.09 us
    ppermute x2, starting transfers between devices, shift(): lax.ppermute(value, axis, [(i, i + steps) for i in range(first, last)])  6.83 us
    pallas_call x1, Pallas kernels, next_part(): pl.pallas_call(functools.partial(next_kernel, heads), grid=(width // (hea...  6.14 us
    select_n x4, other arithmetic, pick(): return jnp.where(after(even, nb_last, *others), when_even, when_odd)  4.25 us
  transfers between devices with their start and end apart: 23, of which 10 were waited for; matrix products, arithmetic and copies ran while one was open for 3% of the time, Pallas kernels for 44%

profile of v5, /device:TPU:0, one launch (start us, length us, event | category | flops | bytes accessed | tf_op | source)
XLA Modules:
  0.0 142.2 jit_solution(2465223843852043498)
XLA Ops:
  4.4 3.9 %shard_map.137 = (bf16[2,192,512]{2,1,0:T(8,128)(2,1)}, bf16[2,192,512]{2,1,0:T(8,128)(2,1)}, bf16[4,192,512]{2,1,0:T(8,128)(2,1)}, bf16[2,272,1024]{2,1,0:T(8,128)(2,1)}) custom-call(s32[2]{0:T(128)} %pad_add_fusion.info_ref, s32[4]{0:T(128)} %bitcast.39, bf16[192,4096]{1,0:T(8,128)(2,1)} %refs_3_.1, bf16[192,4096]{1,0:T(8,128)(2,1)} %refs_3_.1, ...), custom_call_target="tpu_custom_call" | custom-call | flops 3000000000 | bytes 1000 | tf_op jit(solution)/shard_map/pallas_call | solution.py:112
  8.8 5.5 %collective-permute-start = (bf16[272,768]{1,0:T(8,128)(2,1)}, bf16[272,768]{1,0:T(8,128)(2,1)}, u32[]{:S(2)}, u32[]{:S(2)}) collective-permute-start(bf16[272,768]{1,0:T(8,128)(2,1)} %shard_map.136), channel_id=1, source_target_pairs={{0,4},{4,8},{8,12},{12,16},{16,20},{20,24},{24,28},{1,5},{5,9},{9,... | collective-permute-start | bytes 1253384 | tf_op jit(solution)/shard_map/ppermute | solution.py:42
  15.3 2.7 %shard_map.138 = (bf16[2,384,512]{2,1,0:T(8,128)(2,1)}, bf16[2,384,512]{2,1,0:T(8,128)(2,1)}) custom-call(bf16[2,192,512]{2,1,0:T(8,128)(2,1)} %get-tuple-element.56.refs_0_.refs_5_, bf16[2,192,512]{2,1,0:T(8,128)(2,1)} %get-tuple-element.58.refs_1_.refs_5_, bf16[4,192,512]{2,1,0:T(8,128)(2,1)} %copy-done.10), custom_call_target="tpu_custom_call" | custom-call | flops 2000000000 | bytes 1000 | tf_op jit(solution)/shard_map/pallas_call | solution.py:143
  19.5 3.7 %collective-permute-done.refs_1_ = bf16[272,768]{1,0:T(8,128)(2,1)} collective-permute-done((bf16[272,768]{1,0:T(8,128)(2,1)}, bf16[272,768]{1,0:T(8,128)(2,1)}, u32[]{:S(2)}, u32[]{:S(2)}) %collective-permute-start) | collective-permute-done | bytes 417824 | tf_op jit(solution)/shard_map/ppermute | solution.py:42
  26.1 4.8 %collective-permute-start.8 = (bf16[256,2048]{1,0:T(8,128)(2,1)}, bf16[256,2048]{1,0:T(8,128)(2,1)}, u32[]{:S(2)}, u32[]{:S(2)}) collective-permute-start(bf16[256,2048]{1,0:T(8,128)(2,1)} %get-tuple-element.101), channel_id=1, source_target_pairs={{0,4},{4,0},{8,12},{12,8},{16,20},{20,16},{24,28},{28,24},{1,5},{5... | collective-permute-start | bytes 3145736 | tf_op jit(solution)/shard_map/ppermute | solution.py:50
  32.4 6.3 %collective-permute-done.5.refs_7_ = bf16[2,384,512]{2,1,0:T(8,128)(2,1)} collective-permute-done((bf16[2,384,512]{2,1,0:T(8,128)(2,1)}, bf16[2,384,512]{2,1,0:T(8,128)(2,1)}, u32[]{:S(2)}, u32[]{:S(2)}) %collective-permute-start.5) | collective-permute-done | bytes 786464 | tf_op jit(solution)/shard_map/ppermute | solution.py:50
  38.7 16.5 %shard_map.139 = (bf16[256,1024]{1,0:T(8,128)(2,1)}, bf16[256,1024]{1,0:T(8,128)(2,1)}, bf16[256,1024]{1,0:T(8,128)(2,1)}, bf16[256,1024]{1,0:T(8,128)(2,1)}, bf...) custom-call(s32[2]{0:T(128)} %pad_add_fusion.info_ref, s32[4]{0:T(128)} %bitcast.40, ...), custom_call_target="tpu_custom_call" | custom-call | flops 8999999488 | bytes 1000 | tf_op jit(solution)/shard_map/pallas_call | solution.py:328
  60.6 14.0 %shard_map.141 = (bf16[256,1024]{1,0:T(8,128)(2,1)}, bf16[256,1024]{1,0:T(8,128)(2,1)}, bf16[256,1024]{1,0:T(8,128)(2,1)}, bf16[256,1024]{1,0:T(8,128)(2,1)}, bf...) custom-call(s32[2]{0:T(128)} %pad_add_fusion.info_ref, ...), custom_call_target="tpu_custom_call", output_to_operand_aliasing={{0}: (13, {}), {1}: (14, {}), {2}: (15, {}), {3}: (16, {})} | custom-call | flops 8999999488 | bytes 1000 | tf_op jit(solution)/shard_map/pallas_call | solution.py:328
  75.2 3.4 %collective-permute-done.6.refs_1_ = bf16[2,384,512]{2,1,0:T(8,128)(2,1)} collective-permute-done((bf16[2,384,512]{2,1,0:T(8,128)(2,1)}, bf16[2,384,512]{2,1,0:T(8,128)(2,1)}, u32[]{:S(2)}, u32[]{:S(2)}) %collective-permute-start.6) | collective-permute-done | bytes 786464 | tf_op jit(solution)/shard_map/ppermute | solution.py:50
  78.7 2.0 %collective-permute-done.10.two_ref = bf16[256,2048]{1,0:T(8,128)(2,1)S(1)} collective-permute-done((bf16[256,2048]{1,0:T(8,128)(2,1)}, bf16[256,2048]{1,0:T(8,128)(2,1)S(1)}, u32[]{:S(2)}, u32[]{:S(2)}) %collective-permute-start.10) | collective-permute-done | bytes 1048608 | tf_op jit(solution)/shard_map/ppermute | solution.py:50
  84.4 2.4 %shard_map.140 = (bf16[192,1024]{1,0:T(8,128)(2,1)}, bf16[192,1024]{1,0:T(8,128)(2,1)}) custom-call(s32[2]{0:T(128)} %pad_add_fusion.info_ref, bf16[2,384,512]{2,1,0:T(8,128)(2,1)} %get-tuple-element.60.refs_0_, bf16[2,384,512]{2,1,0:T(8,128)(2,1)} %collective-permute-done.6.refs_1_), custom_call_target="tpu_custom_call" | custom-call | flops 1000000000 | bytes 1000 | tf_op jit(solution)/shard_map/pallas_call | solution.py:599
  86.8 2.4 %collective-permute-start.14 = (bf16[192,1024]{1,0:T(8,128)(2,1)}, bf16[192,1024]{1,0:T(8,128)(2,1)S(1)}, u32[]{:S(2)}, u32[]{:S(2)}) collective-permute-start(bf16[192,1024]{1,0:T(8,128)(2,1)} %get-tuple-element.63), channel_id=1, source_target_pairs={{0,8},{4,12},{8,0},{12,4},{16,24},{20,28},{24,16},{28,20},{1,9},{5... | collective-permute-start | bytes 1179656 | tf_op jit(solution)/shard_map/ppermute | solution.py:50
  89.2 4.8 %collective-permute-done.13.refs_1_ = bf16[2,384,512]{2,1,0:T(8,128)(2,1)} collective-permute-done((bf16[2,384,512]{2,1,0:T(8,128)(2,1)}, bf16[2,384,512]{2,1,0:T(8,128)(2,1)}, u32[]{:S(2)}, u32[]{:S(2)}) %collective-permute-start.13) | collective-permute-done | bytes 786464 | tf_op jit(solution)/shard_map/ppermute | solution.py:50
  94.0 2.4 %shard_map.142 = (bf16[192,1024]{1,0:T(8,128)(2,1)}, bf16[192,1024]{1,0:T(8,128)(2,1)}) custom-call(s32[2]{0:T(128)} %pad_add_fusion.info_ref, bf16[2,384,512]{2,1,0:T(8,128)(2,1)} %get-tuple-element.77.refs_0_, bf16[2,384,512]{2,1,0:T(8,128)(2,1)} %collective-permute-done.13.refs_1_), custom_call_target="tpu_custom_call" | custom-call | flops 1000000000 | bytes 1000 | tf_op jit(solution)/shard_map/pallas_call | solution.py:599
  96.4 2.4 %collective-permute-start.15 = (bf16[192,1024]{1,0:T(8,128)(2,1)}, bf16[192,1024]{1,0:T(8,128)(2,1)}, u32[]{:S(2)}, u32[]{:S(2)}) collective-permute-start(bf16[192,1024]{1,0:T(8,128)(2,1)} %get-tuple-element.80), channel_id=1, source_target_pairs={{0,8},{4,12},{8,0},{12,4},{16,24},{20,28},{24,16},{28,20},{1,9},{5... | collective-permute-start | bytes 1179656 | tf_op jit(solution)/shard_map/ppermute | solution.py:50
  98.9 2.3 %collective-permute-start.18 = (bf16[256,2048]{1,0:T(8,128)(2,1)S(1)}, bf16[256,2048]{1,0:T(8,128)(2,1)S(1)}, u32[]{:S(2)}, u32[]{:S(2)}) collective-permute-start(bf16[256,2048]{1,0:T(8,128)(2,1)S(1)} %broadcast_select_fusion), channel_id=1, source_target_pairs={{0,4},{4,0},{8,12},{12,8},{16,20},{20,16},{24,28},{28,24},{1,5},{5... | collective-permute-start | bytes 3145736 | tf_op jit(solution)/shard_map/ppermute | solution.py:50
  101.2 5.5 %collective-permute-done.15.refs_3_ = bf16[192,1024]{1,0:T(8,128)(2,1)} collective-permute-done((bf16[192,1024]{1,0:T(8,128)(2,1)}, bf16[192,1024]{1,0:T(8,128)(2,1)}, u32[]{:S(2)}, u32[]{:S(2)}) %collective-permute-start.15) | collective-permute-done | bytes 393248 | tf_op jit(solution)/shard_map/ppermute | solution.py:50
  106.7 2.4 %shard_map.143 = (bf16[96,2048]{1,0:T(8,128)(2,1)}, bf16[96,2048]{1,0:T(8,128)(2,1)}) custom-call(s32[2]{0:T(128)} %pad_add_fusion.info_ref, bf16[192,1024]{1,0:T(8,128)(2,1)} %get-tuple-element.62.refs_0_, bf16[192,1024]{1,0:T(8,128)(2,1)} %get-tuple-element.79.refs_1_, bf16[192,1024]{1,0:T(8,128)(2,1)} %copy-done.11, ...), custom_call_target="tpu_custom_call" | custom-call | flops 1000000000 | bytes 1000 | tf_op jit(solution)/shard_map/pallas_call | solution.py:599
  109.1 2.8 %collective-permute-start.20 = (bf16[96,2048]{1,0:T(8,128)(2,1)}, bf16[96,2048]{1,0:T(8,128)(2,1)S(1)}, u32[]{:S(2)}, u32[]{:S(2)}) collective-permute-start(bf16[96,2048]{1,0:T(8,128)(2,1)} %get-tuple-element.81), channel_id=1, source_target_pairs={{0,16},{4,20},{8,24},{12,28},{16,0},{20,4},{24,8},{28,12},{1,17},{... | collective-permute-start | bytes 1179656 | tf_op jit(solution)/shard_map/ppermute | solution.py:50
  111.8 12.0 %shard_map.144 = (bf16[256,2048]{1,0:T(8,128)(2,1)}, bf16[256,2048]{1,0:T(8,128)(2,1)}, bf16[256,2048]{1,0:T(8,128)(2,1)}, f32[256,2048]{1,0:T(8,128)}, f32[256,2048]{1,0:T(8,128)}, /*index=5*/f32[16,2,256]{2,1,0:T(2,128)}) custom-call(s32[2]{0:T(128)} %pad_add_fusion.info_ref, bf16[256,2048]{1,0:T(8,128)(2,1)} %bitcast.26, bf16[256,2048]{1,0:T(8,128)(2,1)} %bitcast.25, ...), custom_call_target="tpu_custom_call" | custom-call | flops 14000000000 | bytes 1000 | tf_op jit(solution)/shard_map/pallas_call | solution.py:462
  125.1 2.5 %collective-permute-done.20.refs_1_ = bf16[96,2048]{1,0:T(8,128)(2,1)S(1)} collective-permute-done((bf16[96,2048]{1,0:T(8,128)(2,1)}, bf16[96,2048]{1,0:T(8,128)(2,1)S(1)}, u32[]{:S(2)}, u32[]{:S(2)}) %collective-permute-start.20) | collective-permute-done | bytes 393248 | tf_op jit(solution)/shard_map/ppermute | solution.py:50
  128.4 1.9 %shard_map.146 = (bf16[48,2048]{1,0:T(8,128)(2,1)}, bf16[48,2048]{1,0:T(8,128)(2,1)}) custom-call(s32[2]{0:T(128)} %pad_add_fusion.info_ref, bf16[96,2048]{1,0:T(8,128)(2,1)} %get-tuple-element.96.refs_0_, bf16[96,2048]{1,0:T(8,128)(2,1)} %copy-done.12), custom_call_target="tpu_custom_call" | custom-call | flops 1000000000 | bytes 1000 | tf_op jit(solution)/shard_map/pallas_call | solution.py:599
  130.4 2.3 %collective-permute-start.21 = (bf16[48,2048]{1,0:T(8,128)(2,1)}, bf16[48,2048]{1,0:T(8,128)(2,1)S(1)}, u32[]{:S(2)}, u32[]{:S(2)}) collective-permute-start(bf16[48,2048]{1,0:T(8,128)(2,1)} %get-tuple-element.98), channel_id=1, source_target_pairs={{0,4},{4,0},{8,12},{12,8},{16,20},{20,16},{24,28},{28,24},{1,5},{5... | collective-permute-start | bytes 589832 | tf_op jit(solution)/shard_map/ppermute | solution.py:50
  133.8 6.1 %shard_map.145 = (bf16[256,2048]{1,0:T(8,128)(2,1)}, bf16[256,2048]{1,0:T(8,128)(2,1)}) custom-call(s32[2]{0:T(128)} %pad_add_fusion.info_ref, bf16[256,2048]{1,0:T(8,128)(2,1)} %collective-permute-done.8.one_ref, bf16[256,2048]{1,0:T(8,128)(2,1)} %collective-permute-done.17.three_ref, bf16[256,2048]{1,0:T(8,128)(2,1)} %copy-done.9, ...), custom_call_target="tpu_custom_call" | custom-call | flops 8000000000 | bytes 1000 | tf_op jit(solution)/shard_map/pallas_call | solution.py:533
  (73 shorter events, 26.3 us)
Async XLA Ops:
  0.6 3.8 %collective-permute-start.1 = (bf16[4,256,768]{2,1,0:T(8,128)(2,1)}, bf16[4,256,768]{2,1,0:T(8,128)(2,1)S(1)}, u32[]{:S(2)}, u32[]{:S(2)}) collective-permute-start(bf16[4,256,768]{2,1,0:T(8,128)(2,1)} %bitcast.31), channel_id=1, source_target_pairs={{0,1},{1,0},{2,3},{3,2},{4,5},{5,4},{6,7},{7,6},{8,9},{9,8},{10,11... | collective-permute-start | bytes 4718600 | tf_op jit(solution)/shard_map/ppermute | solution.py:50
  8.3 14.8 %collective-permute-start.2 = (bf16[2,272,1024]{2,1,0:T(8,128)(2,1)}, bf16[2,272,1024]{2,1,0:T(8,128)(2,1)S(1)}, u32[]{:S(2)}, u32[]{:S(2)}) collective-permute-start(bf16[2,272,1024]{2,1,0:T(8,128)(2,1)} %get-tuple-element.54), channel_id=1, source_target_pairs={{0,1},{1,0},{2,3},{3,2},{4,5},{5,4},{6,7},{7,6},{8,9},{9,8},{10,11... | collective-permute-start | bytes 3342344 | tf_op jit(solution)/shard_map/ppermute | solution.py:50
  8.7 5.7 %collective-permute-start.4 = (bf16[4,192,512]{2,1,0:T(8,128)(2,1)}, bf16[4,192,512]{2,1,0:T(8,128)(2,1)S(1)}, u32[]{:S(2)}, u32[]{:S(2)}) collective-permute-start(bf16[4,192,512]{2,1,0:T(8,128)(2,1)} %get-tuple-element.57), channel_id=1, source_target_pairs={{0,1},{1,0},{2,3},{3,2},{4,5},{5,4},{6,7},{7,6},{8,9},{9,8},{10,11... | collective-permute-start | bytes 2359304 | tf_op jit(solution)/shard_map/ppermute | solution.py:50
  8.8 14.3 %collective-permute-start = (bf16[272,768]{1,0:T(8,128)(2,1)}, bf16[272,768]{1,0:T(8,128)(2,1)}, u32[]{:S(2)}, u32[]{:S(2)}) collective-permute-start(bf16[272,768]{1,0:T(8,128)(2,1)} %shard_map.136), channel_id=1, source_target_pairs={{0,4},{4,8},{8,12},{12,16},{16,20},{20,24},{24,28},{1,5},{5,9},{9,... | collective-permute-start | bytes 1253384 | tf_op jit(solution)/shard_map/ppermute | solution.py:42
  18.0 20.7 %collective-permute-start.5 = (bf16[2,384,512]{2,1,0:T(8,128)(2,1)}, bf16[2,384,512]{2,1,0:T(8,128)(2,1)}, u32[]{:S(2)}, u32[]{:S(2)}) collective-permute-start(bf16[2,384,512]{2,1,0:T(8,128)(2,1)} %get-tuple-element.59), channel_id=1, source_target_pairs={{0,2},{1,3},{2,0},{3,1},{4,6},{5,7},{6,4},{7,5},{8,10},{9,11},{10,... | collective-permute-start | bytes 2359304 | tf_op jit(solution)/shard_map/ppermute | solution.py:50
  23.1 9.3 %collective-permute-start.3 = (bf16[272,768]{1,0:T(8,128)(2,1)}, bf16[272,768]{1,0:T(8,128)(2,1)}, u32[]{:S(2)}, u32[]{:S(2)}) collective-permute-start(bf16[272,768]{1,0:T(8,128)(2,1)} %collective-permute-done.refs_1_), channel_id=1, source_target_pairs={{0,1},{1,0},{2,3},{3,2},{4,5},{5,4},{6,7},{7,6},{8,9},{9,8},{10,11... | collective-permute-start | bytes 1253384 | tf_op jit(solution)/shard_map/ppermute | solution.py:50
  24.8 30.4 %collective-permute-start.9 = (bf16[256,2048]{1,0:T(8,128)(2,1)}, bf16[256,2048]{1,0:T(8,128)(2,1)S(1)}, u32[]{:S(2)}, u32[]{:S(2)}) collective-permute-start(bf16[256,2048]{1,0:T(8,128)(2,1)} %get-tuple-element.100), channel_id=1, source_target_pairs={{4,12},{12,20},{20,28},{8,0},{16,8},{24,16},{5,13},{13,21},{21,29}... | collective-permute-start | bytes 3145736 | tf_op jit(solution)/shard_map/ppermute | solution.py:639
  26.1 49.1 %collective-permute-start.8 = (bf16[256,2048]{1,0:T(8,128)(2,1)}, bf16[256,2048]{1,0:T(8,128)(2,1)}, u32[]{:S(2)}, u32[]{:S(2)}) collective-permute-start(bf16[256,2048]{1,0:T(8,128)(2,1)} %get-tuple-element.101), channel_id=1, source_target_pairs={{0,4},{4,0},{8,12},{12,8},{16,20},{20,16},{24,28},{28,24},{1,5},{5... | collective-permute-start | bytes 3145736 | tf_op jit(solution)/shard_map/ppermute | solution.py:50
  30.9 24.4 %copy-start.4 = (bf16[1,256,2048]{2,1,0:T(8,128)(2,1)S(1)}, bf16[1,256,2048]{2,1,0:T(8,128)(2,1)}, u32[]{:S(2)}) copy-start(bf16[1,256,2048]{2,1,0:T(8,128)(2,1)} %param.11) | copy-start | bytes 3145732
  30.9 29.8 %collective-permute-start.7 = (bf16[2,384,512]{2,1,0:T(8,128)(2,1)}, bf16[2,384,512]{2,1,0:T(8,128)(2,1)}, u32[]{:S(2)}, u32[]{:S(2)}) collective-permute-start(bf16[2,384,512]{2,1,0:T(8,128)(2,1)} %get-tuple-element.65), channel_id=1, source_target_pairs={{0,2},{1,3},{2,0},{3,1},{4,6},{5,7},{6,4},{7,5},{8,10},{9,11},{10,... | collective-permute-start | bytes 2359304 | tf_op jit(solution)/shard_map/ppermute | solution.py:50
  56.7 23.9 %collective-permute-start.10 = (bf16[256,2048]{1,0:T(8,128)(2,1)}, bf16[256,2048]{1,0:T(8,128)(2,1)S(1)}, u32[]{:S(2)}, u32[]{:S(2)}) collective-permute-start(bf16[256,2048]{1,0:T(8,128)(2,1)} %get-tuple-element.103), channel_id=1, source_target_pairs={{0,4},{4,0},{8,12},{12,8},{16,20},{20,16},{24,28},{28,24},{1,5},{5... | collective-permute-start | bytes 3145736 | tf_op jit(solution)/shard_map/ppermute | solution.py:50
  57.6 25.4 %collective-permute-start.16 = (bf16[256,2048]{1,0:T(8,128)(2,1)}, bf16[256,2048]{1,0:T(8,128)(2,1)S(1)}, u32[]{:S(2)}, u32[]{:S(2)}) collective-permute-start(bf16[256,2048]{1,0:T(8,128)(2,1)} %get-tuple-element.102), channel_id=1, source_target_pairs={{4,12},{12,20},{20,28},{8,0},{16,8},{24,16},{5,13},{13,21},{21,29}... | collective-permute-start | bytes 3145736 | tf_op jit(solution)/shard_map/ppermute | solution.py:639
  59.1 19.6 %collective-permute-start.6 = (bf16[2,384,512]{2,1,0:T(8,128)(2,1)}, bf16[2,384,512]{2,1,0:T(8,128)(2,1)}, u32[]{:S(2)}, u32[]{:S(2)}) collective-permute-start(bf16[2,384,512]{2,1,0:T(8,128)(2,1)} %get-tuple-element.61), channel_id=1, source_target_pairs={{0,2},{1,3},{2,0},{3,1},{4,6},{5,7},{6,4},{7,5},{8,10},{9,11},{10,... | collective-permute-start | bytes 2359304 | tf_op jit(solution)/shard_map/ppermute | solution.py:50
  74.6 19.4 %collective-permute-start.13 = (bf16[2,384,512]{2,1,0:T(8,128)(2,1)}, bf16[2,384,512]{2,1,0:T(8,128)(2,1)}, u32[]{:S(2)}, u32[]{:S(2)}) collective-permute-start(bf16[2,384,512]{2,1,0:T(8,128)(2,1)} %get-tuple-element.78), channel_id=1, source_target_pairs={{0,2},{1,3},{2,0},{3,1},{4,6},{5,7},{6,4},{7,5},{8,10},{9,11},{10,... | collective-permute-start | bytes 2359304 | tf_op jit(solution)/shard_map/ppermute | solution.py:50
  80.7 8.5 %collective-permute-start.11 = (bf16[256,1024]{1,0:T(8,128)(2,1)}, bf16[256,1024]{1,0:T(8,128)(2,1)}, u32[]{:S(2)}, u32[]{:S(2)}) collective-permute-start(bf16[256,1024]{1,0:T(8,128)(2,1)} %get-tuple-element.74), channel_id=1, source_target_pairs={{0,1},{1,0},{2,3},{3,2},{4,5},{5,4},{6,7},{7,6},{8,9},{9,8},{10,11... | collective-permute-start | bytes 1572872 | tf_op jit(solution)/shard_map/ppermute | solution.py:50
  80.7 8.5 %collective-permute-start.12 = (bf16[256,1024]{1,0:T(8,128)(2,1)}, bf16[256,1024]{1,0:T(8,128)(2,1)}, u32[]{:S(2)}, u32[]{:S(2)}) collective-permute-start(bf16[256,1024]{1,0:T(8,128)(2,1)} %get-tuple-element.75), channel_id=1, source_target_pairs={{0,1},{1,0},{2,3},{3,2},{4,5},{5,4},{6,7},{7,6},{8,9},{9,8},{10,11... | collective-permute-start | bytes 1572872 | tf_op jit(solution)/shard_map/ppermute | solution.py:50
  84.1 27.7 %collective-permute-start.17 = (bf16[256,2048]{1,0:T(8,128)(2,1)}, bf16[256,2048]{1,0:T(8,128)(2,1)}, u32[]{:S(2)}, u32[]{:S(2)}) collective-permute-start(bf16[256,2048]{1,0:T(8,128)(2,1)} %broadcast_select_fusion.1), channel_id=1, source_target_pairs={{0,4},{4,0},{8,12},{12,8},{16,20},{20,16},{24,28},{28,24},{1,5},{5... | collective-permute-start | bytes 3145736 | tf_op jit(solution)/shard_map/ppermute | solution.py:50
  86.8 14.4 %collective-permute-start.14 = (bf16[192,1024]{1,0:T(8,128)(2,1)}, bf16[192,1024]{1,0:T(8,128)(2,1)S(1)}, u32[]{:S(2)}, u32[]{:S(2)}) collective-permute-start(bf16[192,1024]{1,0:T(8,128)(2,1)} %get-tuple-element.63), channel_id=1, source_target_pairs={{0,8},{4,12},{8,0},{12,4},{16,24},{20,28},{24,16},{28,20},{1,9},{5... | collective-permute-start | bytes 1179656 | tf_op jit(solution)/shard_map/ppermute | solution.py:50
  96.4 10.3 %collective-permute-start.15 = (bf16[192,1024]{1,0:T(8,128)(2,1)}, bf16[192,1024]{1,0:T(8,128)(2,1)}, u32[]{:S(2)}, u32[]{:S(2)}) collective-permute-start(bf16[192,1024]{1,0:T(8,128)(2,1)} %get-tuple-element.80), channel_id=1, source_target_pairs={{0,8},{4,12},{8,0},{12,4},{16,24},{20,28},{24,16},{28,20},{1,9},{5... | collective-permute-start | bytes 1179656 | tf_op jit(solution)/shard_map/ppermute | solution.py:50
  98.9 33.8 %collective-permute-start.18 = (bf16[256,2048]{1,0:T(8,128)(2,1)S(1)}, bf16[256,2048]{1,0:T(8,128)(2,1)S(1)}, u32[]{:S(2)}, u32[]{:S(2)}) collective-permute-start(bf16[256,2048]{1,0:T(8,128)(2,1)S(1)} %broadcast_select_fusion), channel_id=1, source_target_pairs={{0,4},{4,0},{8,12},{12,8},{16,20},{20,16},{24,28},{28,24},{1,5},{5... | collective-permute-start | bytes 3145736 | tf_op jit(solution)/shard_map/ppermute | solution.py:50
  109.1 18.6 %collective-permute-start.20 = (bf16[96,2048]{1,0:T(8,128)(2,1)}, bf16[96,2048]{1,0:T(8,128)(2,1)S(1)}, u32[]{:S(2)}, u32[]{:S(2)}) collective-permute-start(bf16[96,2048]{1,0:T(8,128)(2,1)} %get-tuple-element.81), channel_id=1, source_target_pairs={{0,16},{4,20},{8,24},{12,28},{16,0},{20,4},{24,8},{28,12},{1,17},{... | collective-permute-start | bytes 1179656 | tf_op jit(solution)/shard_map/ppermute | solution.py:50
  123.8 8.8 %collective-permute-start.19 = (f32[16,2,256]{2,1,0:T(2,128)}, f32[16,2,256]{2,1,0:T(2,128)S(1)}, u32[]{:S(2)}, u32[]{:S(2)}) collective-permute-start(f32[16,2,256]{2,1,0:T(2,128)} %get-tuple-element.89), channel_id=1, source_target_pairs={{4,0},{8,4},{12,8},{16,12},{20,16},{24,20},{28,24},{5,1},{9,5},{13... | collective-permute-start | bytes 98312 | tf_op jit(solution)/shard_map/ppermute | solution.py:42
  130.4 9.5 %collective-permute-start.21 = (bf16[48,2048]{1,0:T(8,128)(2,1)}, bf16[48,2048]{1,0:T(8,128)(2,1)S(1)}, u32[]{:S(2)}, u32[]{:S(2)}) collective-permute-start(bf16[48,2048]{1,0:T(8,128)(2,1)} %get-tuple-element.98), channel_id=1, source_target_pairs={{0,4},{4,0},{8,12},{12,8},{16,20},{20,16},{24,28},{28,24},{1,5},{5... | collective-permute-start | bytes 589832 | tf_op jit(solution)/shard_map/ppermute | solution.py:50
  140.0 1.4 collective-permute-start.22
  (13 other events, 76.1 us)

commit v6 on v5

--- a/solution.py
+++ b/solution.py
@@ -621,7 +621,7 @@
     nb_last = shift(last, "seq", 1)
 
     nb_peer = swap(nb, "fsdp", 1)
-    mine, other, pair = cut(after(info, last, nb_peer), counts, kv_weight, cq, do)
+    mine, other, pair = cut(after(info, last), counts, kv_weight, cq, do)
     near = swap(other, "fsdp", 1)
     weights = [
         [here, near, *[swap(x, "fsdp", piece) for piece in range(2, fsdp, 2)]]
@@ -642,7 +642,7 @@
     one = swap(pick(k, q), "seq", 1)
     far_two = hop(pick(do, v))
 
-    nb_last = after(nb_last, peer)
+    nb_last = after(nb_last, peer, nb_peer)
     peer_last = swap(nb_last, "fsdp", 1)
     nbs = [nb_last, nb, peer_last, nb_peer]
 

time: 143 us -> 142 us (level)
  transfers between devices with their start and end apart: 23 -> 23, of which waited for: 10 -> 9; matrix products, arithmetic and copies ran while one was open for 3% -> 3% of each run, Pallas kernels for 44% -> 47%
where the time goes in v6:
time: 142 us; the launch traced here: 141 us
  Pallas kernels  66.1 us (47%)
  starting transfers between devices  33.4 us (24%)
  waiting for transfers between devices  32.5 us (23%)
  other arithmetic  5.75 us (4%)
  local copies, waits for them, and re-layouts  2.78 us (2%)
    pallas_call x2, Pallas kernels, cross(): pl.pallas_call(functools.partial(cross_kernel, group, turns, len(weights)...  30.5 us
    ppermute x19, waiting for transfers between devices, swap(): lax.ppermute(value, axis, [(i, i ^ bit) for i in range(lax.axis_size(axis...  26.5 us
    ppermute x19, starting transfers between devices, swap(): lax.ppermute(value, axis, [(i, i ^ bit) for i in range(lax.axis_size(axis...  24.2 us
    pallas_call x1, Pallas kernels, self_part(): pl.pallas_call(functools.partial(self_kernel, heads), grid_spec=pltpu.Pre...  12 us
    pallas_call x4, Pallas kernels, halve(): pl.pallas_call(functools.partial(halve_kernel, spans, axis, bit), in_spec...  9.07 us
    ppermute x2, starting transfers between devices, shift(): lax.ppermute(value, axis, [(i, i + steps) for i in range(first, last)])  6.47 us
    pallas_call x1, Pallas kernels, next_part(): pl.pallas_call(functools.partial(next_kernel, heads), grid=(width // (hea...  6.14 us
    select_n x4, other arithmetic, pick(): return jnp.where(after(even, nb_last, *others), when_even, when_odd)  4.26 us
  transfers between devices with their start and end apart: 23, of which 9 were waited for; matrix products, arithmetic and copies ran while one was open for 3% of the time, Pallas kernels for 47%

profile of v6, /device:TPU:0, one launch (start us, length us, event | category | flops | bytes accessed | tf_op | source)
XLA Modules:
  0.0 141.5 jit_solution(11553386827286199842)
XLA Ops:
  3.6 3.9 %shard_map.137 = (bf16[2,192,512]{2,1,0:T(8,128)(2,1)}, bf16[2,192,512]{2,1,0:T(8,128)(2,1)}, bf16[4,192,512]{2,1,0:T(8,128)(2,1)}, bf16[2,272,1024]{2,1,0:T(8,128)(2,1)}) custom-call(s32[2]{0:T(128)} %pad_add_fusion.info_ref, s32[4]{0:T(128)} %bitcast.39, bf16[192,4096]{1,0:T(8,128)(2,1)} %refs_3_.1, bf16[192,4096]{1,0:T(8,128)(2,1)} %refs_3_.1, ...), custom_call_target="tpu_custom_call" | custom-call | flops 3000000000 | bytes 1000 | tf_op jit(solution)/shard_map/pallas_call | solution.py:112
  8.0 5.2 %collective-permute-start = (bf16[272,768]{1,0:T(8,128)(2,1)}, bf16[272,768]{1,0:T(8,128)(2,1)}, u32[]{:S(2)}, u32[]{:S(2)}) collective-permute-start(bf16[272,768]{1,0:T(8,128)(2,1)} %shard_map.136), channel_id=1, source_target_pairs={{0,4},{4,8},{8,12},{12,16},{16,20},{20,24},{24,28},{1,5},{5,9},{9,... | collective-permute-start | bytes 1253384 | tf_op jit(solution)/shard_map/ppermute | solution.py:42
  14.1 2.7 %shard_map.138 = (bf16[2,384,512]{2,1,0:T(8,128)(2,1)}, bf16[2,384,512]{2,1,0:T(8,128)(2,1)}) custom-call(bf16[2,192,512]{2,1,0:T(8,128)(2,1)} %get-tuple-element.56.refs_0_.refs_5_, bf16[2,192,512]{2,1,0:T(8,128)(2,1)} %get-tuple-element.58.refs_1_.refs_5_, bf16[4,192,512]{2,1,0:T(8,128)(2,1)} %copy-done.9), custom_call_target="tpu_custom_call" | custom-call | flops 2000000000 | bytes 1000 | tf_op jit(solution)/shard_map/pallas_call | solution.py:143
  18.3 4.0 %collective-permute-done.refs_1_ = bf16[272,768]{1,0:T(8,128)(2,1)} collective-permute-done((bf16[272,768]{1,0:T(8,128)(2,1)}, bf16[272,768]{1,0:T(8,128)(2,1)}, u32[]{:S(2)}, u32[]{:S(2)}) %collective-permute-start) | collective-permute-done | bytes 417824 | tf_op jit(solution)/shard_map/ppermute | solution.py:42
  25.3 4.8 %collective-permute-start.8 = (bf16[256,2048]{1,0:T(8,128)(2,1)}, bf16[256,2048]{1,0:T(8,128)(2,1)}, u32[]{:S(2)}, u32[]{:S(2)}) collective-permute-start(bf16[256,2048]{1,0:T(8,128)(2,1)} %get-tuple-element.101), channel_id=1, source_target_pairs={{0,4},{4,0},{8,12},{12,8},{16,20},{20,16},{24,28},{28,24},{1,5},{5... | collective-permute-start | bytes 3145736 | tf_op jit(solution)/shard_map/ppermute | solution.py:50
  31.6 5.9 %collective-permute-done.5.refs_7_ = bf16[2,384,512]{2,1,0:T(8,128)(2,1)} collective-permute-done((bf16[2,384,512]{2,1,0:T(8,128)(2,1)}, bf16[2,384,512]{2,1,0:T(8,128)(2,1)}, u32[]{:S(2)}, u32[]{:S(2)}) %collective-permute-start.5) | collective-permute-done | bytes 786464 | tf_op jit(solution)/shard_map/ppermute | solution.py:50
  37.5 16.5 %shard_map.139 = (bf16[256,1024]{1,0:T(8,128)(2,1)}, bf16[256,1024]{1,0:T(8,128)(2,1)}, bf16[256,1024]{1,0:T(8,128)(2,1)}, bf16[256,1024]{1,0:T(8,128)(2,1)}, bf...) custom-call(s32[2]{0:T(128)} %pad_add_fusion.info_ref, s32[4]{0:T(128)} %bitcast.40, ...), custom_call_target="tpu_custom_call" | custom-call | flops 8999999488 | bytes 1000 | tf_op jit(solution)/shard_map/pallas_call | solution.py:328
  59.6 14.0 %shard_map.141 = (bf16[256,1024]{1,0:T(8,128)(2,1)}, bf16[256,1024]{1,0:T(8,128)(2,1)}, bf16[256,1024]{1,0:T(8,128)(2,1)}, bf16[256,1024]{1,0:T(8,128)(2,1)}, bf...) custom-call(s32[2]{0:T(128)} %pad_add_fusion.info_ref, ...), custom_call_target="tpu_custom_call", output_to_operand_aliasing={{0}: (13, {}), {1}: (14, {}), {2}: (15, {}), {3}: (16, {})} | custom-call | flops 8999999488 | bytes 1000 | tf_op jit(solution)/shard_map/pallas_call | solution.py:328
  74.2 3.9 %collective-permute-done.6.refs_1_ = bf16[2,384,512]{2,1,0:T(8,128)(2,1)} collective-permute-done((bf16[2,384,512]{2,1,0:T(8,128)(2,1)}, bf16[2,384,512]{2,1,0:T(8,128)(2,1)}, u32[]{:S(2)}, u32[]{:S(2)}) %collective-permute-start.6) | collective-permute-done | bytes 786464 | tf_op jit(solution)/shard_map/ppermute | solution.py:50
  78.1 1.8 %collective-permute-done.10.two_ref = bf16[256,2048]{1,0:T(8,128)(2,1)S(1)} collective-permute-done((bf16[256,2048]{1,0:T(8,128)(2,1)}, bf16[256,2048]{1,0:T(8,128)(2,1)S(1)}, u32[]{:S(2)}, u32[]{:S(2)}) %collective-permute-start.10) | collective-permute-done | bytes 1048608 | tf_op jit(solution)/shard_map/ppermute | solution.py:50
  80.4 2.0 %collective-permute-done.16 = bf16[256,2048]{1,0:T(8,128)(2,1)S(1)} collective-permute-done((bf16[256,2048]{1,0:T(8,128)(2,1)}, bf16[256,2048]{1,0:T(8,128)(2,1)S(1)}, u32[]{:S(2)}, u32[]{:S(2)}) %collective-permute-start.16) | collective-permute-done | bytes 1048608 | tf_op jit(solution)/shard_map/ppermute | solution.py:639
  83.7 2.4 %shard_map.140 = (bf16[192,1024]{1,0:T(8,128)(2,1)}, bf16[192,1024]{1,0:T(8,128)(2,1)}) custom-call(s32[2]{0:T(128)} %pad_add_fusion.info_ref, bf16[2,384,512]{2,1,0:T(8,128)(2,1)} %get-tuple-element.60.refs_0_, bf16[2,384,512]{2,1,0:T(8,128)(2,1)} %collective-permute-done.6.refs_1_), custom_call_target="tpu_custom_call" | custom-call | flops 1000000000 | bytes 1000 | tf_op jit(solution)/shard_map/pallas_call | solution.py:599
  86.1 2.4 %collective-permute-start.14 = (bf16[192,1024]{1,0:T(8,128)(2,1)}, bf16[192,1024]{1,0:T(8,128)(2,1)S(1)}, u32[]{:S(2)}, u32[]{:S(2)}) collective-permute-start(bf16[192,1024]{1,0:T(8,128)(2,1)} %get-tuple-element.63), channel_id=1, source_target_pairs={{0,8},{4,12},{8,0},{12,4},{16,24},{20,28},{24,16},{28,20},{1,9},{5... | collective-permute-start | bytes 1179656 | tf_op jit(solution)/shard_map/ppermute | solution.py:50
  88.5 5.0 %collective-permute-done.13.refs_1_ = bf16[2,384,512]{2,1,0:T(8,128)(2,1)} collective-permute-done((bf16[2,384,512]{2,1,0:T(8,128)(2,1)}, bf16[2,384,512]{2,1,0:T(8,128)(2,1)}, u32[]{:S(2)}, u32[]{:S(2)}) %collective-permute-start.13) | collective-permute-done | bytes 786464 | tf_op jit(solution)/shard_map/ppermute | solution.py:50
  93.4 2.4 %shard_map.142 = (bf16[192,1024]{1,0:T(8,128)(2,1)}, bf16[192,1024]{1,0:T(8,128)(2,1)}) custom-call(s32[2]{0:T(128)} %pad_add_fusion.info_ref, bf16[2,384,512]{2,1,0:T(8,128)(2,1)} %get-tuple-element.77.refs_0_, bf16[2,384,512]{2,1,0:T(8,128)(2,1)} %collective-permute-done.13.refs_1_), custom_call_target="tpu_custom_call" | custom-call | flops 1000000000 | bytes 1000 | tf_op jit(solution)/shard_map/pallas_call | solution.py:599
  95.8 2.4 %collective-permute-start.15 = (bf16[192,1024]{1,0:T(8,128)(2,1)}, bf16[192,1024]{1,0:T(8,128)(2,1)}, u32[]{:S(2)}, u32[]{:S(2)}) collective-permute-start(bf16[192,1024]{1,0:T(8,128)(2,1)} %get-tuple-element.80), channel_id=1, source_target_pairs={{0,8},{4,12},{8,0},{12,4},{16,24},{20,28},{24,16},{28,20},{1,9},{5... | collective-permute-start | bytes 1179656 | tf_op jit(solution)/shard_map/ppermute | solution.py:50
  98.3 2.2 %collective-permute-start.18 = (bf16[256,2048]{1,0:T(8,128)(2,1)S(1)}, bf16[256,2048]{1,0:T(8,128)(2,1)S(1)}, u32[]{:S(2)}, u32[]{:S(2)}) collective-permute-start(bf16[256,2048]{1,0:T(8,128)(2,1)S(1)} %broadcast_select_fusion), channel_id=1, source_target_pairs={{0,4},{4,0},{8,12},{12,8},{16,20},{20,16},{24,28},{28,24},{1,5},{5... | collective-permute-start | bytes 3145736 | tf_op jit(solution)/shard_map/ppermute | solution.py:50
  100.5 5.9 %collective-permute-done.15.refs_3_ = bf16[192,1024]{1,0:T(8,128)(2,1)} collective-permute-done((bf16[192,1024]{1,0:T(8,128)(2,1)}, bf16[192,1024]{1,0:T(8,128)(2,1)}, u32[]{:S(2)}, u32[]{:S(2)}) %collective-permute-start.15) | collective-permute-done | bytes 393248 | tf_op jit(solution)/shard_map/ppermute | solution.py:50
  106.4 2.4 %shard_map.143 = (bf16[96,2048]{1,0:T(8,128)(2,1)}, bf16[96,2048]{1,0:T(8,128)(2,1)}) custom-call(s32[2]{0:T(128)} %pad_add_fusion.info_ref, bf16[192,1024]{1,0:T(8,128)(2,1)} %get-tuple-element.62.refs_0_, bf16[192,1024]{1,0:T(8,128)(2,1)} %get-tuple-element.79.refs_1_, bf16[192,1024]{1,0:T(8,128)(2,1)} %copy-done.10, ...), custom_call_target="tpu_custom_call" | custom-call | flops 1000000000 | bytes 1000 | tf_op jit(solution)/shard_map/pallas_call | solution.py:599
  108.7 2.8 %collective-permute-start.20 = (bf16[96,2048]{1,0:T(8,128)(2,1)}, bf16[96,2048]{1,0:T(8,128)(2,1)S(1)}, u32[]{:S(2)}, u32[]{:S(2)}) collective-permute-start(bf16[96,2048]{1,0:T(8,128)(2,1)} %get-tuple-element.81), channel_id=1, source_target_pairs={{0,16},{4,20},{8,24},{12,28},{16,0},{20,4},{24,8},{28,12},{1,17},{... | collective-permute-start | bytes 1179656 | tf_op jit(solution)/shard_map/ppermute | solution.py:50
  111.5 12.0 %shard_map.144 = (bf16[256,2048]{1,0:T(8,128)(2,1)}, bf16[256,2048]{1,0:T(8,128)(2,1)}, bf16[256,2048]{1,0:T(8,128)(2,1)}, f32[256,2048]{1,0:T(8,128)}, f32[256,2048]{1,0:T(8,128)}, /*index=5*/f32[16,2,256]{2,1,0:T(2,128)}) custom-call(s32[2]{0:T(128)} %pad_add_fusion.info_ref, bf16[256,2048]{1,0:T(8,128)(2,1)} %bitcast.26, bf16[256,2048]{1,0:T(8,128)(2,1)} %bitcast.25, ...), custom_call_target="tpu_custom_call" | custom-call | flops 14000000000 | bytes 1000 | tf_op jit(solution)/shard_map/pallas_call | solution.py:462
  124.8 2.8 %collective-permute-done.20.refs_1_ = bf16[96,2048]{1,0:T(8,128)(2,1)S(1)} collective-permute-done((bf16[96,2048]{1,0:T(8,128)(2,1)}, bf16[96,2048]{1,0:T(8,128)(2,1)S(1)}, u32[]{:S(2)}, u32[]{:S(2)}) %collective-permute-start.20) | collective-permute-done | bytes 393248 | tf_op jit(solution)/shard_map/ppermute | solution.py:50
  128.3 1.9 %shard_map.146 = (bf16[48,2048]{1,0:T(8,128)(2,1)}, bf16[48,2048]{1,0:T(8,128)(2,1)}) custom-call(s32[2]{0:T(128)} %pad_add_fusion.info_ref, bf16[96,2048]{1,0:T(8,128)(2,1)} %get-tuple-element.96.refs_0_, bf16[96,2048]{1,0:T(8,128)(2,1)} %copy-done.11), custom_call_target="tpu_custom_call" | custom-call | flops 1000000000 | bytes 1000 | tf_op jit(solution)/shard_map/pallas_call | solution.py:599
  133.0 6.1 %shard_map.145 = (bf16[256,2048]{1,0:T(8,128)(2,1)}, bf16[256,2048]{1,0:T(8,128)(2,1)}) custom-call(s32[2]{0:T(128)} %pad_add_fusion.info_ref, bf16[256,2048]{1,0:T(8,128)(2,1)} %collective-permute-done.8.one_ref, bf16[256,2048]{1,0:T(8,128)(2,1)} %collective-permute-done.17.three_ref, bf16[256,2048]{1,0:T(8,128)(2,1)} %copy-done.8, ...), custom_call_target="tpu_custom_call" | custom-call | flops 8000000000 | bytes 1000 | tf_op jit(solution)/shard_map/pallas_call | solution.py:533
  (71 shorter events, 25.4 us)
Async XLA Ops:
  0.6 21.7 %collective-permute-start.2 = (bf16[4,256,768]{2,1,0:T(8,128)(2,1)}, bf16[4,256,768]{2,1,0:T(8,128)(2,1)}, u32[]{:S(2)}, u32[]{:S(2)}) collective-permute-start(bf16[4,256,768]{2,1,0:T(8,128)(2,1)} %bitcast.31), channel_id=1, source_target_pairs={{0,1},{1,0},{2,3},{3,2},{4,5},{5,4},{6,7},{7,6},{8,9},{9,8},{10,11... | collective-permute-start | bytes 4718600 | tf_op jit(solution)/shard_map/ppermute | solution.py:50
  7.5 14.8 %collective-permute-start.1 = (bf16[2,272,1024]{2,1,0:T(8,128)(2,1)}, bf16[2,272,1024]{2,1,0:T(8,128)(2,1)S(1)}, u32[]{:S(2)}, u32[]{:S(2)}) collective-permute-start(bf16[2,272,1024]{2,1,0:T(8,128)(2,1)} %get-tuple-element.54), channel_id=1, source_target_pairs={{0,1},{1,0},{2,3},{3,2},{4,5},{5,4},{6,7},{7,6},{8,9},{9,8},{10,11... | collective-permute-start | bytes 3342344 | tf_op jit(solution)/shard_map/ppermute | solution.py:50
  7.6 5.6 %collective-permute-start.4 = (bf16[4,192,512]{2,1,0:T(8,128)(2,1)}, bf16[4,192,512]{2,1,0:T(8,128)(2,1)S(1)}, u32[]{:S(2)}, u32[]{:S(2)}) collective-permute-start(bf16[4,192,512]{2,1,0:T(8,128)(2,1)} %get-tuple-element.57), channel_id=1, source_target_pairs={{0,1},{1,0},{2,3},{3,2},{4,5},{5,4},{6,7},{7,6},{8,9},{9,8},{10,11... | collective-permute-start | bytes 2359304 | tf_op jit(solution)/shard_map/ppermute | solution.py:50
  8.0 14.3 %collective-permute-start = (bf16[272,768]{1,0:T(8,128)(2,1)}, bf16[272,768]{1,0:T(8,128)(2,1)}, u32[]{:S(2)}, u32[]{:S(2)}) collective-permute-start(bf16[272,768]{1,0:T(8,128)(2,1)} %shard_map.136), channel_id=1, source_target_pairs={{0,4},{4,8},{8,12},{12,16},{16,20},{20,24},{24,28},{1,5},{5,9},{9,... | collective-permute-start | bytes 1253384 | tf_op jit(solution)/shard_map/ppermute | solution.py:42
  16.8 20.7 %collective-permute-start.5 = (bf16[2,384,512]{2,1,0:T(8,128)(2,1)}, bf16[2,384,512]{2,1,0:T(8,128)(2,1)}, u32[]{:S(2)}, u32[]{:S(2)}) collective-permute-start(bf16[2,384,512]{2,1,0:T(8,128)(2,1)} %get-tuple-element.59), channel_id=1, source_target_pairs={{0,2},{1,3},{2,0},{3,1},{4,6},{5,7},{6,4},{7,5},{8,10},{9,11},{10,... | collective-permute-start | bytes 2359304 | tf_op jit(solution)/shard_map/ppermute | solution.py:50
  22.3 15.2 %collective-permute-start.3 = (bf16[272,768]{1,0:T(8,128)(2,1)}, bf16[272,768]{1,0:T(8,128)(2,1)}, u32[]{:S(2)}, u32[]{:S(2)}) collective-permute-start(bf16[272,768]{1,0:T(8,128)(2,1)} %collective-permute-done.refs_1_), channel_id=1, source_target_pairs={{0,1},{1,0},{2,3},{3,2},{4,5},{5,4},{6,7},{7,6},{8,9},{9,8},{10,11... | collective-permute-start | bytes 1253384 | tf_op jit(solution)/shard_map/ppermute | solution.py:50
  24.0 30.0 %collective-permute-start.9 = (bf16[256,2048]{1,0:T(8,128)(2,1)}, bf16[256,2048]{1,0:T(8,128)(2,1)S(1)}, u32[]{:S(2)}, u32[]{:S(2)}) collective-permute-start(bf16[256,2048]{1,0:T(8,128)(2,1)} %get-tuple-element.100), channel_id=1, source_target_pairs={{4,12},{12,20},{20,28},{8,0},{16,8},{24,16},{5,13},{13,21},{21,29}... | collective-permute-start | bytes 3145736 | tf_op jit(solution)/shard_map/ppermute | solution.py:639
  25.3 48.9 %collective-permute-start.8 = (bf16[256,2048]{1,0:T(8,128)(2,1)}, bf16[256,2048]{1,0:T(8,128)(2,1)}, u32[]{:S(2)}, u32[]{:S(2)}) collective-permute-start(bf16[256,2048]{1,0:T(8,128)(2,1)} %get-tuple-element.101), channel_id=1, source_target_pairs={{0,4},{4,0},{8,12},{12,8},{16,20},{20,16},{24,28},{28,24},{1,5},{5... | collective-permute-start | bytes 3145736 | tf_op jit(solution)/shard_map/ppermute | solution.py:50
  30.1 23.9 %copy-start.4 = (bf16[1,256,2048]{2,1,0:T(8,128)(2,1)S(1)}, bf16[1,256,2048]{2,1,0:T(8,128)(2,1)}, u32[]{:S(2)}) copy-start(bf16[1,256,2048]{2,1,0:T(8,128)(2,1)} %param.11) | copy-start | bytes 3145732
  30.1 29.5 %collective-permute-start.7 = (bf16[2,384,512]{2,1,0:T(8,128)(2,1)}, bf16[2,384,512]{2,1,0:T(8,128)(2,1)}, u32[]{:S(2)}, u32[]{:S(2)}) collective-permute-start(bf16[2,384,512]{2,1,0:T(8,128)(2,1)} %get-tuple-element.65), channel_id=1, source_target_pairs={{0,2},{1,3},{2,0},{3,1},{4,6},{5,7},{6,4},{7,5},{8,10},{9,11},{10,... | collective-permute-start | bytes 2359304 | tf_op jit(solution)/shard_map/ppermute | solution.py:50
  55.5 24.4 %collective-permute-start.10 = (bf16[256,2048]{1,0:T(8,128)(2,1)}, bf16[256,2048]{1,0:T(8,128)(2,1)S(1)}, u32[]{:S(2)}, u32[]{:S(2)}) collective-permute-start(bf16[256,2048]{1,0:T(8,128)(2,1)} %get-tuple-element.103), channel_id=1, source_target_pairs={{0,4},{4,0},{8,12},{12,8},{16,20},{20,16},{24,28},{28,24},{1,5},{5... | collective-permute-start | bytes 3145736 | tf_op jit(solution)/shard_map/ppermute | solution.py:50
  56.5 25.9 %collective-permute-start.16 = (bf16[256,2048]{1,0:T(8,128)(2,1)}, bf16[256,2048]{1,0:T(8,128)(2,1)S(1)}, u32[]{:S(2)}, u32[]{:S(2)}) collective-permute-start(bf16[256,2048]{1,0:T(8,128)(2,1)} %get-tuple-element.102), channel_id=1, source_target_pairs={{4,12},{12,20},{20,28},{8,0},{16,8},{24,16},{5,13},{13,21},{21,29}... | collective-permute-start | bytes 3145736 | tf_op jit(solution)/shard_map/ppermute | solution.py:639
  58.0 20.1 %collective-permute-start.6 = (bf16[2,384,512]{2,1,0:T(8,128)(2,1)}, bf16[2,384,512]{2,1,0:T(8,128)(2,1)}, u32[]{:S(2)}, u32[]{:S(2)}) collective-permute-start(bf16[2,384,512]{2,1,0:T(8,128)(2,1)} %get-tuple-element.61), channel_id=1, source_target_pairs={{0,2},{1,3},{2,0},{3,1},{4,6},{5,7},{6,4},{7,5},{8,10},{9,11},{10,... | collective-permute-start | bytes 2359304 | tf_op jit(solution)/shard_map/ppermute | solution.py:50
  73.6 19.9 %collective-permute-start.13 = (bf16[2,384,512]{2,1,0:T(8,128)(2,1)}, bf16[2,384,512]{2,1,0:T(8,128)(2,1)}, u32[]{:S(2)}, u32[]{:S(2)}) collective-permute-start(bf16[2,384,512]{2,1,0:T(8,128)(2,1)} %get-tuple-element.78), channel_id=1, source_target_pairs={{0,2},{1,3},{2,0},{3,1},{4,6},{5,7},{6,4},{7,5},{8,10},{9,11},{10,... | collective-permute-start | bytes 2359304 | tf_op jit(solution)/shard_map/ppermute | solution.py:50
  79.9 8.6 %collective-permute-start.11 = (bf16[256,1024]{1,0:T(8,128)(2,1)}, bf16[256,1024]{1,0:T(8,128)(2,1)}, u32[]{:S(2)}, u32[]{:S(2)}) collective-permute-start(bf16[256,1024]{1,0:T(8,128)(2,1)} %get-tuple-element.74), channel_id=1, source_target_pairs={{0,1},{1,0},{2,3},{3,2},{4,5},{5,4},{6,7},{7,6},{8,9},{9,8},{10,11... | collective-permute-start | bytes 1572872 | tf_op jit(solution)/shard_map/ppermute | solution.py:50
  79.9 8.6 %collective-permute-start.12 = (bf16[256,1024]{1,0:T(8,128)(2,1)}, bf16[256,1024]{1,0:T(8,128)(2,1)}, u32[]{:S(2)}, u32[]{:S(2)}) collective-permute-start(bf16[256,1024]{1,0:T(8,128)(2,1)} %get-tuple-element.75), channel_id=1, source_target_pairs={{0,1},{1,0},{2,3},{3,2},{4,5},{5,4},{6,7},{7,6},{8,9},{9,8},{10,11... | collective-permute-start | bytes 1572872 | tf_op jit(solution)/shard_map/ppermute | solution.py:50
  83.5 28.0 %collective-permute-start.17 = (bf16[256,2048]{1,0:T(8,128)(2,1)}, bf16[256,2048]{1,0:T(8,128)(2,1)}, u32[]{:S(2)}, u32[]{:S(2)}) collective-permute-start(bf16[256,2048]{1,0:T(8,128)(2,1)} %broadcast_select_fusion.1), channel_id=1, source_target_pairs={{0,4},{4,0},{8,12},{12,8},{16,20},{20,16},{24,28},{28,24},{1,5},{5... | collective-permute-start | bytes 3145736 | tf_op jit(solution)/shard_map/ppermute | solution.py:50
  86.1 14.4 %collective-permute-start.14 = (bf16[192,1024]{1,0:T(8,128)(2,1)}, bf16[192,1024]{1,0:T(8,128)(2,1)S(1)}, u32[]{:S(2)}, u32[]{:S(2)}) collective-permute-start(bf16[192,1024]{1,0:T(8,128)(2,1)} %get-tuple-element.63), channel_id=1, source_target_pairs={{0,8},{4,12},{8,0},{12,4},{16,24},{20,28},{24,16},{28,20},{1,9},{5... | collective-permute-start | bytes 1179656 | tf_op jit(solution)/shard_map/ppermute | solution.py:50
  95.8 10.5 %collective-permute-start.15 = (bf16[192,1024]{1,0:T(8,128)(2,1)}, bf16[192,1024]{1,0:T(8,128)(2,1)}, u32[]{:S(2)}, u32[]{:S(2)}) collective-permute-start(bf16[192,1024]{1,0:T(8,128)(2,1)} %get-tuple-element.80), channel_id=1, source_target_pairs={{0,8},{4,12},{8,0},{12,4},{16,24},{20,28},{24,16},{28,20},{1,9},{5... | collective-permute-start | bytes 1179656 | tf_op jit(solution)/shard_map/ppermute | solution.py:50
  98.3 33.7 %collective-permute-start.18 = (bf16[256,2048]{1,0:T(8,128)(2,1)S(1)}, bf16[256,2048]{1,0:T(8,128)(2,1)S(1)}, u32[]{:S(2)}, u32[]{:S(2)}) collective-permute-start(bf16[256,2048]{1,0:T(8,128)(2,1)S(1)} %broadcast_select_fusion), channel_id=1, source_target_pairs={{0,4},{4,0},{8,12},{12,8},{16,20},{20,16},{24,28},{28,24},{1,5},{5... | collective-permute-start | bytes 3145736 | tf_op jit(solution)/shard_map/ppermute | solution.py:50
  108.7 18.8 %collective-permute-start.20 = (bf16[96,2048]{1,0:T(8,128)(2,1)}, bf16[96,2048]{1,0:T(8,128)(2,1)S(1)}, u32[]{:S(2)}, u32[]{:S(2)}) collective-permute-start(bf16[96,2048]{1,0:T(8,128)(2,1)} %get-tuple-element.81), channel_id=1, source_target_pairs={{0,16},{4,20},{8,24},{12,28},{16,0},{20,4},{24,8},{28,12},{1,17},{... | collective-permute-start | bytes 1179656 | tf_op jit(solution)/shard_map/ppermute | solution.py:50
  123.5 8.4 %collective-permute-start.19 = (f32[16,2,256]{2,1,0:T(2,128)}, f32[16,2,256]{2,1,0:T(2,128)S(1)}, u32[]{:S(2)}, u32[]{:S(2)}) collective-permute-start(f32[16,2,256]{2,1,0:T(2,128)} %get-tuple-element.89), channel_id=1, source_target_pairs={{4,0},{8,4},{12,8},{16,12},{20,16},{24,20},{28,24},{5,1},{9,5},{13... | collective-permute-start | bytes 98312 | tf_op jit(solution)/shard_map/ppermute | solution.py:42
  130.2 8.9 %collective-permute-start.21 = (bf16[48,2048]{1,0:T(8,128)(2,1)}, bf16[48,2048]{1,0:T(8,128)(2,1)S(1)}, u32[]{:S(2)}, u32[]{:S(2)}) collective-permute-start(bf16[48,2048]{1,0:T(8,128)(2,1)} %get-tuple-element.98), channel_id=1, source_target_pairs={{0,4},{4,0},{8,12},{12,8},{16,20},{20,16},{24,28},{28,24},{1,5},{5... | collective-permute-start | bytes 589832 | tf_op jit(solution)/shard_map/ppermute | solution.py:50
  139.3 1.4 collective-permute-start.22
  (12 other events, 73.3 us)

commit v7 on v6

--- a/solution.py
+++ b/solution.py
@@ -675,11 +675,13 @@
     )
     got.append(swap(halves[1][1], *stages[split_at]))
     four = swap(pick(far_two, do, halves[1][1], third), "seq", 1)
-    keeps = [keep for keep, _ in halves]
-    keep, send = halve(info, keeps, got, stages[split_at + 1])
-    keeps, got = [keep], [swap(send, *stages[split_at + 1])]
+    keeps, sends = zip(
+        halve(after(info, halves[1][1]), [halves[0][0]], [got[0]], stages[split_at + 1]),
+        halve(info, [halves[1][0]], [got[1]], stages[split_at + 1]),
+    )
+    got = [swap(send, *stages[split_at + 1]) for send in sends]
     block_out, query_grad, cross_grad, dk, dv, stats = self_part(
-        after(info, send), q, do, k, v, one, two, three, own, back
+        after(info, *sends), q, do, k, v, one, two, three, own, back
     )
     stats_after = shift(stats, "seq", -1)
     key_grad, value_grad = next_part(info, one, three, four, k, v, stats_after, dk, dv)

time: 142 us -> 142 us (level)
  waiting for transfers between devices: 32.5 us -> 29 us
  Pallas kernels: 66.1 us -> 67.7 us
    ppermute x19 -> x20, waiting for transfers between devices: 26.5 us -> 22.9 us  [swap(): lax.ppermute(value, axis, [(i, i ^ bit) for i in range(lax.axis_size(axis...]
    pallas_call x4 -> x5, Pallas kernels: 9.07 us -> 10.7 us  [halve(): pl.pallas_call(functools.partial(halve_kernel, spans, axis, bit), in_spec...]
    ppermute x19 -> x20, starting transfers between devices: 24.2 us -> 25.5 us  [swap(): lax.ppermute(value, axis, [(i, i ^ bit) for i in range(lax.axis_size(axis...]
    unnamed x26 -> x28, local copies, waits for them, and re-layouts: 2.71 us -> 3.45 us
  transfers between devices with their start and end apart: 23 -> 24, of which waited for: 9 -> 8; matrix products, arithmetic and copies ran while one was open for 3% -> 3% of each run, Pallas kernels for 47% -> 48%
where the time goes in v7:
time: 142 us
  Pallas kernels  67.7 us (48%)
  starting transfers between devices  34.7 us (24%)
  waiting for transfers between devices  29 us (20%)
  other arithmetic  5.7 us (4%)
  local copies, waits for them, and re-layouts  3.52 us (2%)
    pallas_call x2, Pallas kernels, cross(): pl.pallas_call(functools.partial(cross_kernel, group, turns, len(weights)...  30.5 us
    ppermute x20, starting transfers between devices, swap(): lax.ppermute(value, axis, [(i, i ^ bit) for i in range(lax.axis_size(axis...  25.5 us
    ppermute x20, waiting for transfers between devices, swap(): lax.ppermute(value, axis, [(i, i ^ bit) for i in range(lax.axis_size(axis...  22.9 us
    pallas_call x1, Pallas kernels, self_part(): pl.pallas_call(functools.partial(self_kernel, heads), grid_spec=pltpu.Pre...  12 us
    pallas_call x5, Pallas kernels, halve(): pl.pallas_call(functools.partial(halve_kernel, spans, axis, bit), in_spec...  10.7 us
    ppermute x2, starting transfers between devices, shift(): lax.ppermute(value, axis, [(i, i + steps) for i in range(first, last)])  6.48 us
    pallas_call x1, Pallas kernels, next_part(): pl.pallas_call(functools.partial(next_kernel, heads), grid=(width // (hea...  6.14 us
    select_n x4, other arithmetic, pick(): return jnp.where(after(even, nb_last, *others), when_even, when_odd)  4.26 us
  transfers between devices with their start and end apart: 24, of which 8 were waited for; matrix products, arithmetic and copies ran while one was open for 3% of the time, Pallas kernels for 48%

profile of v7, /device:TPU:0, one launch (start us, length us, event | category | flops | bytes accessed | tf_op | source)
XLA Modules:
  0.0 141.5 jit_solution(12017831408860823962)
XLA Ops:
  3.5 3.9 %shard_map.137 = (bf16[2,192,512]{2,1,0:T(8,128)(2,1)}, bf16[2,192,512]{2,1,0:T(8,128)(2,1)}, bf16[4,192,512]{2,1,0:T(8,128)(2,1)}, bf16[2,272,1024]{2,1,0:T(8,128)(2,1)}) custom-call(s32[2]{0:T(128)} %pad_add_fusion.info_ref, s32[4]{0:T(128)} %bitcast.39, bf16[192,4096]{1,0:T(8,128)(2,1)} %refs_3_.1, bf16[192,4096]{1,0:T(8,128)(2,1)} %refs_3_.1, ...), custom_call_target="tpu_custom_call" | custom-call | flops 3000000000 | bytes 1000 | tf_op jit(solution)/shard_map/pallas_call | solution.py:112
  8.0 5.2 %collective-permute-start = (bf16[272,768]{1,0:T(8,128)(2,1)}, bf16[272,768]{1,0:T(8,128)(2,1)}, u32[]{:S(2)}, u32[]{:S(2)}) collective-permute-start(bf16[272,768]{1,0:T(8,128)(2,1)} %shard_map.136), channel_id=1, source_target_pairs={{0,4},{4,8},{8,12},{12,16},{16,20},{20,24},{24,28},{1,5},{5,9},{9,... | collective-permute-start | bytes 1253384 | tf_op jit(solution)/shard_map/ppermute | solution.py:42
  14.1 2.7 %shard_map.138 = (bf16[2,384,512]{2,1,0:T(8,128)(2,1)}, bf16[2,384,512]{2,1,0:T(8,128)(2,1)}) custom-call(bf16[2,192,512]{2,1,0:T(8,128)(2,1)} %get-tuple-element.59.refs_0_.refs_5_, bf16[2,192,512]{2,1,0:T(8,128)(2,1)} %get-tuple-element.61.refs_1_.refs_5_, bf16[4,192,512]{2,1,0:T(8,128)(2,1)} %copy-done.9), custom_call_target="tpu_custom_call" | custom-call | flops 2000000000 | bytes 1000 | tf_op jit(solution)/shard_map/pallas_call | solution.py:143
  18.3 4.0 %collective-permute-done.refs_1_ = bf16[272,768]{1,0:T(8,128)(2,1)} collective-permute-done((bf16[272,768]{1,0:T(8,128)(2,1)}, bf16[272,768]{1,0:T(8,128)(2,1)}, u32[]{:S(2)}, u32[]{:S(2)}) %collective-permute-start) | collective-permute-done | bytes 417824 | tf_op jit(solution)/shard_map/ppermute | solution.py:42
  25.2 4.8 %collective-permute-start.8 = (bf16[256,2048]{1,0:T(8,128)(2,1)}, bf16[256,2048]{1,0:T(8,128)(2,1)}, u32[]{:S(2)}, u32[]{:S(2)}) collective-permute-start(bf16[256,2048]{1,0:T(8,128)(2,1)} %get-tuple-element.107), channel_id=1, source_target_pairs={{0,4},{4,0},{8,12},{12,8},{16,20},{20,16},{24,28},{28,24},{1,5},{5... | collective-permute-start | bytes 3145736 | tf_op jit(solution)/shard_map/ppermute | solution.py:50
  31.6 5.9 %collective-permute-done.5.refs_7_ = bf16[2,384,512]{2,1,0:T(8,128)(2,1)} collective-permute-done((bf16[2,384,512]{2,1,0:T(8,128)(2,1)}, bf16[2,384,512]{2,1,0:T(8,128)(2,1)}, u32[]{:S(2)}, u32[]{:S(2)}) %collective-permute-start.5) | collective-permute-done | bytes 786464 | tf_op jit(solution)/shard_map/ppermute | solution.py:50
  37.5 16.5 %shard_map.139 = (bf16[256,1024]{1,0:T(8,128)(2,1)}, bf16[256,1024]{1,0:T(8,128)(2,1)}, bf16[256,1024]{1,0:T(8,128)(2,1)}, bf16[256,1024]{1,0:T(8,128)(2,1)}, bf...) custom-call(s32[2]{0:T(128)} %pad_add_fusion.info_ref, s32[4]{0:T(128)} %bitcast.40, ...), custom_call_target="tpu_custom_call" | custom-call | flops 8999999488 | bytes 1000 | tf_op jit(solution)/shard_map/pallas_call | solution.py:328
  59.6 14.0 %shard_map.141 = (bf16[256,1024]{1,0:T(8,128)(2,1)}, bf16[256,1024]{1,0:T(8,128)(2,1)}, bf16[256,1024]{1,0:T(8,128)(2,1)}, bf16[256,1024]{1,0:T(8,128)(2,1)}, bf...) custom-call(s32[2]{0:T(128)} %pad_add_fusion.info_ref, ...), custom_call_target="tpu_custom_call", output_to_operand_aliasing={{0}: (13, {}), {1}: (14, {}), {2}: (15, {}), {3}: (16, {})} | custom-call | flops 8999999488 | bytes 1000 | tf_op jit(solution)/shard_map/pallas_call | solution.py:328
  74.1 3.9 %collective-permute-done.6.refs_1_ = bf16[2,384,512]{2,1,0:T(8,128)(2,1)} collective-permute-done((bf16[2,384,512]{2,1,0:T(8,128)(2,1)}, bf16[2,384,512]{2,1,0:T(8,128)(2,1)}, u32[]{:S(2)}, u32[]{:S(2)}) %collective-permute-start.6) | collective-permute-done | bytes 786464 | tf_op jit(solution)/shard_map/ppermute | solution.py:50
  80.3 2.1 %collective-permute-done.16 = bf16[256,2048]{1,0:T(8,128)(2,1)S(1)} collective-permute-done((bf16[256,2048]{1,0:T(8,128)(2,1)}, bf16[256,2048]{1,0:T(8,128)(2,1)S(1)}, u32[]{:S(2)}, u32[]{:S(2)}) %collective-permute-start.16) | collective-permute-done | bytes 1048608 | tf_op jit(solution)/shard_map/ppermute | solution.py:639
  83.7 2.4 %shard_map.140 = (bf16[192,1024]{1,0:T(8,128)(2,1)}, bf16[192,1024]{1,0:T(8,128)(2,1)}) custom-call(s32[2]{0:T(128)} %pad_add_fusion.info_ref, bf16[2,384,512]{2,1,0:T(8,128)(2,1)} %get-tuple-element.63.refs_0_, bf16[2,384,512]{2,1,0:T(8,128)(2,1)} %collective-permute-done.6.refs_1_), custom_call_target="tpu_custom_call" | custom-call | flops 1000000000 | bytes 1000 | tf_op jit(solution)/shard_map/pallas_call | solution.py:599
  86.0 2.4 %collective-permute-start.14 = (bf16[192,1024]{1,0:T(8,128)(2,1)}, bf16[192,1024]{1,0:T(8,128)(2,1)S(1)}, u32[]{:S(2)}, u32[]{:S(2)}) collective-permute-start(bf16[192,1024]{1,0:T(8,128)(2,1)} %get-tuple-element.65), channel_id=1, source_target_pairs={{0,8},{4,12},{8,0},{12,4},{16,24},{20,28},{24,16},{28,20},{1,9},{5... | collective-permute-start | bytes 1179656 | tf_op jit(solution)/shard_map/ppermute | solution.py:50
  88.4 5.0 %collective-permute-done.13.refs_1_ = bf16[2,384,512]{2,1,0:T(8,128)(2,1)} collective-permute-done((bf16[2,384,512]{2,1,0:T(8,128)(2,1)}, bf16[2,384,512]{2,1,0:T(8,128)(2,1)}, u32[]{:S(2)}, u32[]{:S(2)}) %collective-permute-start.13) | collective-permute-done | bytes 786464 | tf_op jit(solution)/shard_map/ppermute | solution.py:50
  93.4 2.4 %shard_map.142 = (bf16[192,1024]{1,0:T(8,128)(2,1)}, bf16[192,1024]{1,0:T(8,128)(2,1)}) custom-call(s32[2]{0:T(128)} %pad_add_fusion.info_ref, bf16[2,384,512]{2,1,0:T(8,128)(2,1)} %get-tuple-element.79.refs_0_, bf16[2,384,512]{2,1,0:T(8,128)(2,1)} %collective-permute-done.13.refs_1_), custom_call_target="tpu_custom_call" | custom-call | flops 1000000000 | bytes 1000 | tf_op jit(solution)/shard_map/pallas_call | solution.py:599
  95.8 2.4 %collective-permute-start.15 = (bf16[192,1024]{1,0:T(8,128)(2,1)}, bf16[192,1024]{1,0:T(8,128)(2,1)}, u32[]{:S(2)}, u32[]{:S(2)}) collective-permute-start(bf16[192,1024]{1,0:T(8,128)(2,1)} %get-tuple-element.81), channel_id=1, source_target_pairs={{0,8},{4,12},{8,0},{12,4},{16,24},{20,28},{24,16},{28,20},{1,9},{5... | collective-permute-start | bytes 1179656 | tf_op jit(solution)/shard_map/ppermute | solution.py:50
  98.3 2.2 %collective-permute-start.18 = (bf16[256,2048]{1,0:T(8,128)(2,1)S(1)}, bf16[256,2048]{1,0:T(8,128)(2,1)S(1)}, u32[]{:S(2)}, u32[]{:S(2)}) collective-permute-start(bf16[256,2048]{1,0:T(8,128)(2,1)S(1)} %broadcast_select_fusion), channel_id=1, source_target_pairs={{0,4},{4,0},{8,12},{12,8},{16,20},{20,16},{24,28},{28,24},{1,5},{5... | collective-permute-start | bytes 3145736 | tf_op jit(solution)/shard_map/ppermute | solution.py:50
  101.2 1.9 %shard_map.143 = (bf16[96,1024]{1,0:T(8,128)(2,1)}, bf16[96,1024]{1,0:T(8,128)(2,1)}) custom-call(s32[2]{0:T(128)} %pad_add_fusion.info_ref, bf16[192,1024]{1,0:T(8,128)(2,1)} %get-tuple-element.83.refs_0_, bf16[192,1024]{1,0:T(8,128)(2,1)} %copy-done.10), custom_call_target="tpu_custom_call" | custom-call | flops 1000000000 | bytes 1000 | tf_op jit(solution)/shard_map/pallas_call | solution.py:599
  103.7 5.1 %collective-permute-done.15.refs_1_ = bf16[192,1024]{1,0:T(8,128)(2,1)} collective-permute-done((bf16[192,1024]{1,0:T(8,128)(2,1)}, bf16[192,1024]{1,0:T(8,128)(2,1)}, u32[]{:S(2)}, u32[]{:S(2)}) %collective-permute-start.15) | collective-permute-done | bytes 393248 | tf_op jit(solution)/shard_map/ppermute | solution.py:50
  108.8 1.9 %shard_map.144 = (bf16[96,1024]{1,0:T(8,128)(2,1)}, bf16[96,1024]{1,0:T(8,128)(2,1)}) custom-call(s32[2]{0:T(128)} %pad_add_fusion.info_ref, bf16[192,1024]{1,0:T(8,128)(2,1)} %get-tuple-element.85.refs_0_, bf16[192,1024]{1,0:T(8,128)(2,1)} %collective-permute-done.15.refs_1_), custom_call_target="tpu_custom_call" | custom-call | flops 1000000000 | bytes 1000 | tf_op jit(solution)/shard_map/pallas_call | solution.py:599
  110.7 2.5 %collective-permute-start.21 = (bf16[96,1024]{1,0:T(8,128)(2,1)}, bf16[96,1024]{1,0:T(8,128)(2,1)S(1)}, u32[]{:S(2)}, u32[]{:S(2)}) collective-permute-start(bf16[96,1024]{1,0:T(8,128)(2,1)} %get-tuple-element.86), channel_id=1, source_target_pairs={{0,16},{4,20},{8,24},{12,28},{16,0},{20,4},{24,8},{28,12},{1,17},{... | collective-permute-start | bytes 589832 | tf_op jit(solution)/shard_map/ppermute | solution.py:50
  113.2 12.0 %shard_map.145 = (bf16[256,2048]{1,0:T(8,128)(2,1)}, bf16[256,2048]{1,0:T(8,128)(2,1)}, bf16[256,2048]{1,0:T(8,128)(2,1)}, f32[256,2048]{1,0:T(8,128)}, f32[256,2048]{1,0:T(8,128)}, /*index=5*/f32[16,2,256]{2,1,0:T(2,128)}) custom-call(s32[2]{0:T(128)} %pad_add_fusion.info_ref, bf16[256,2048]{1,0:T(8,128)(2,1)} %bitcast.26, bf16[256,2048]{1,0:T(8,128)(2,1)} %bitcast.25, ...), custom_call_target="tpu_custom_call" | custom-call | flops 14000000000 | bytes 1000 | tf_op jit(solution)/shard_map/pallas_call | solution.py:462
  127.3 2.0 %shard_map.147 = (bf16[48,2048]{1,0:T(8,128)(2,1)}, bf16[48,2048]{1,0:T(8,128)(2,1)}) custom-call(s32[2]{0:T(128)} %pad_add_fusion.info_ref, bf16[96,1024]{1,0:T(8,128)(2,1)} %get-tuple-element.101.refs_0_, bf16[96,1024]{1,0:T(8,128)(2,1)} %get-tuple-element.102.refs_1_, bf16[96,1024]{1,0:T(8,128)(2,1)} %copy-done.11, bf16[96,1024]{1,0:T(8,128)(2,1)} %copy-done.12), custom_call_target="tpu_custom_call" | custom-call | flops 1000000000 | bytes 1000 | tf_op jit(solution)/shard_map/pallas_call | solution.py:599
  129.3 2.6 %collective-permute-start.22 = (bf16[48,2048]{1,0:T(8,128)(2,1)}, bf16[48,2048]{1,0:T(8,128)(2,1)S(1)}, u32[]{:S(2)}, u32[]{:S(2)}) collective-permute-start(bf16[48,2048]{1,0:T(8,128)(2,1)} %get-tuple-element.104), channel_id=1, source_target_pairs={{0,4},{4,0},{8,12},{12,8},{16,20},{20,16},{24,28},{28,24},{1,5},{5... | collective-permute-start | bytes 589832 | tf_op jit(solution)/shard_map/ppermute | solution.py:50
  133.1 6.1 %shard_map.146 = (bf16[256,2048]{1,0:T(8,128)(2,1)}, bf16[256,2048]{1,0:T(8,128)(2,1)}) custom-call(s32[2]{0:T(128)} %pad_add_fusion.info_ref, bf16[256,2048]{1,0:T(8,128)(2,1)} %collective-permute-done.8.one_ref, bf16[256,2048]{1,0:T(8,128)(2,1)} %collective-permute-done.17.three_ref, bf16[256,2048]{1,0:T(8,128)(2,1)} %copy-done.8, ...), custom_call_target="tpu_custom_call" | custom-call | flops 8000000000 | bytes 1000 | tf_op jit(solution)/shard_map/pallas_call | solution.py:533
  (76 shorter events, 26.7 us)
Async XLA Ops:
  0.6 21.6 %collective-permute-start.2 = (bf16[4,256,768]{2,1,0:T(8,128)(2,1)}, bf16[4,256,768]{2,1,0:T(8,128)(2,1)}, u32[]{:S(2)}, u32[]{:S(2)}) collective-permute-start(bf16[4,256,768]{2,1,0:T(8,128)(2,1)} %bitcast.31), channel_id=1, source_target_pairs={{0,1},{1,0},{2,3},{3,2},{4,5},{5,4},{6,7},{7,6},{8,9},{9,8},{10,11... | collective-permute-start | bytes 4718600 | tf_op jit(solution)/shard_map/ppermute | solution.py:50
  7.5 14.8 %collective-permute-start.1 = (bf16[2,272,1024]{2,1,0:T(8,128)(2,1)}, bf16[2,272,1024]{2,1,0:T(8,128)(2,1)S(1)}, u32[]{:S(2)}, u32[]{:S(2)}) collective-permute-start(bf16[2,272,1024]{2,1,0:T(8,128)(2,1)} %get-tuple-element.57), channel_id=1, source_target_pairs={{0,1},{1,0},{2,3},{3,2},{4,5},{5,4},{6,7},{7,6},{8,9},{9,8},{10,11... | collective-permute-start | bytes 3342344 | tf_op jit(solution)/shard_map/ppermute | solution.py:50
  7.5 5.6 %collective-permute-start.4 = (bf16[4,192,512]{2,1,0:T(8,128)(2,1)}, bf16[4,192,512]{2,1,0:T(8,128)(2,1)S(1)}, u32[]{:S(2)}, u32[]{:S(2)}) collective-permute-start(bf16[4,192,512]{2,1,0:T(8,128)(2,1)} %get-tuple-element.60), channel_id=1, source_target_pairs={{0,1},{1,0},{2,3},{3,2},{4,5},{5,4},{6,7},{7,6},{8,9},{9,8},{10,11... | collective-permute-start | bytes 2359304 | tf_op jit(solution)/shard_map/ppermute | solution.py:50
  8.0 14.3 %collective-permute-start = (bf16[272,768]{1,0:T(8,128)(2,1)}, bf16[272,768]{1,0:T(8,128)(2,1)}, u32[]{:S(2)}, u32[]{:S(2)}) collective-permute-start(bf16[272,768]{1,0:T(8,128)(2,1)} %shard_map.136), channel_id=1, source_target_pairs={{0,4},{4,8},{8,12},{12,16},{16,20},{20,24},{24,28},{1,5},{5,9},{9,... | collective-permute-start | bytes 1253384 | tf_op jit(solution)/shard_map/ppermute | solution.py:42
  16.8 20.7 %collective-permute-start.5 = (bf16[2,384,512]{2,1,0:T(8,128)(2,1)}, bf16[2,384,512]{2,1,0:T(8,128)(2,1)}, u32[]{:S(2)}, u32[]{:S(2)}) collective-permute-start(bf16[2,384,512]{2,1,0:T(8,128)(2,1)} %get-tuple-element.62), channel_id=1, source_target_pairs={{0,2},{1,3},{2,0},{3,1},{4,6},{5,7},{6,4},{7,5},{8,10},{9,11},{10,... | collective-permute-start | bytes 2359304 | tf_op jit(solution)/shard_map/ppermute | solution.py:50
  22.3 15.2 %collective-permute-start.3 = (bf16[272,768]{1,0:T(8,128)(2,1)}, bf16[272,768]{1,0:T(8,128)(2,1)}, u32[]{:S(2)}, u32[]{:S(2)}) collective-permute-start(bf16[272,768]{1,0:T(8,128)(2,1)} %collective-permute-done.refs_1_), channel_id=1, source_target_pairs={{0,1},{1,0},{2,3},{3,2},{4,5},{5,4},{6,7},{7,6},{8,9},{9,8},{10,11... | collective-permute-start | bytes 1253384 | tf_op jit(solution)/shard_map/ppermute | solution.py:50
  24.0 30.0 %collective-permute-start.9 = (bf16[256,2048]{1,0:T(8,128)(2,1)}, bf16[256,2048]{1,0:T(8,128)(2,1)S(1)}, u32[]{:S(2)}, u32[]{:S(2)}) collective-permute-start(bf16[256,2048]{1,0:T(8,128)(2,1)} %get-tuple-element.106), channel_id=1, source_target_pairs={{4,12},{12,20},{20,28},{8,0},{16,8},{24,16},{5,13},{13,21},{21,29}... | collective-permute-start | bytes 3145736 | tf_op jit(solution)/shard_map/ppermute | solution.py:639
  25.2 48.9 %collective-permute-start.8 = (bf16[256,2048]{1,0:T(8,128)(2,1)}, bf16[256,2048]{1,0:T(8,128)(2,1)}, u32[]{:S(2)}, u32[]{:S(2)}) collective-permute-start(bf16[256,2048]{1,0:T(8,128)(2,1)} %get-tuple-element.107), channel_id=1, source_target_pairs={{0,4},{4,0},{8,12},{12,8},{16,20},{20,16},{24,28},{28,24},{1,5},{5... | collective-permute-start | bytes 3145736 | tf_op jit(solution)/shard_map/ppermute | solution.py:50
  30.1 29.5 %collective-permute-start.7 = (bf16[2,384,512]{2,1,0:T(8,128)(2,1)}, bf16[2,384,512]{2,1,0:T(8,128)(2,1)}, u32[]{:S(2)}, u32[]{:S(2)}) collective-permute-start(bf16[2,384,512]{2,1,0:T(8,128)(2,1)} %get-tuple-element.67), channel_id=1, source_target_pairs={{0,2},{1,3},{2,0},{3,1},{4,6},{5,7},{6,4},{7,5},{8,10},{9,11},{10,... | collective-permute-start | bytes 2359304 | tf_op jit(solution)/shard_map/ppermute | solution.py:50
  55.5 24.3 %collective-permute-start.10 = (bf16[256,2048]{1,0:T(8,128)(2,1)}, bf16[256,2048]{1,0:T(8,128)(2,1)S(1)}, u32[]{:S(2)}, u32[]{:S(2)}) collective-permute-start(bf16[256,2048]{1,0:T(8,128)(2,1)} %get-tuple-element.109), channel_id=1, source_target_pairs={{0,4},{4,0},{8,12},{12,8},{16,20},{20,16},{24,28},{28,24},{1,5},{5... | collective-permute-start | bytes 3145736 | tf_op jit(solution)/shard_map/ppermute | solution.py:50
  56.5 25.9 %collective-permute-start.16 = (bf16[256,2048]{1,0:T(8,128)(2,1)}, bf16[256,2048]{1,0:T(8,128)(2,1)S(1)}, u32[]{:S(2)}, u32[]{:S(2)}) collective-permute-start(bf16[256,2048]{1,0:T(8,128)(2,1)} %get-tuple-element.108), channel_id=1, source_target_pairs={{4,12},{12,20},{20,28},{8,0},{16,8},{24,16},{5,13},{13,21},{21,29}... | collective-permute-start | bytes 3145736 | tf_op jit(solution)/shard_map/ppermute | solution.py:639
  58.0 20.1 %collective-permute-start.6 = (bf16[2,384,512]{2,1,0:T(8,128)(2,1)}, bf16[2,384,512]{2,1,0:T(8,128)(2,1)}, u32[]{:S(2)}, u32[]{:S(2)}) collective-permute-start(bf16[2,384,512]{2,1,0:T(8,128)(2,1)} %get-tuple-element.64), channel_id=1, source_target_pairs={{0,2},{1,3},{2,0},{3,1},{4,6},{5,7},{6,4},{7,5},{8,10},{9,11},{10,... | collective-permute-start | bytes 2359304 | tf_op jit(solution)/shard_map/ppermute | solution.py:50
  73.5 19.9 %collective-permute-start.13 = (bf16[2,384,512]{2,1,0:T(8,128)(2,1)}, bf16[2,384,512]{2,1,0:T(8,128)(2,1)}, u32[]{:S(2)}, u32[]{:S(2)}) collective-permute-start(bf16[2,384,512]{2,1,0:T(8,128)(2,1)} %get-tuple-element.80), channel_id=1, source_target_pairs={{0,2},{1,3},{2,0},{3,1},{4,6},{5,7},{6,4},{7,5},{8,10},{9,11},{10,... | collective-permute-start | bytes 2359304 | tf_op jit(solution)/shard_map/ppermute | solution.py:50
  79.8 8.6 %collective-permute-start.11 = (bf16[256,1024]{1,0:T(8,128)(2,1)}, bf16[256,1024]{1,0:T(8,128)(2,1)}, u32[]{:S(2)}, u32[]{:S(2)}) collective-permute-start(bf16[256,1024]{1,0:T(8,128)(2,1)} %get-tuple-element.76), channel_id=1, source_target_pairs={{0,1},{1,0},{2,3},{3,2},{4,5},{5,4},{6,7},{7,6},{8,9},{9,8},{10,11... | collective-permute-start | bytes 1572872 | tf_op jit(solution)/shard_map/ppermute | solution.py:50
  79.8 8.6 %collective-permute-start.12 = (bf16[256,1024]{1,0:T(8,128)(2,1)}, bf16[256,1024]{1,0:T(8,128)(2,1)}, u32[]{:S(2)}, u32[]{:S(2)}) collective-permute-start(bf16[256,1024]{1,0:T(8,128)(2,1)} %get-tuple-element.77), channel_id=1, source_target_pairs={{0,1},{1,0},{2,3},{3,2},{4,5},{5,4},{6,7},{7,6},{8,9},{9,8},{10,11... | collective-permute-start | bytes 1572872 | tf_op jit(solution)/shard_map/ppermute | solution.py:50
  83.5 29.7 %collective-permute-start.17 = (bf16[256,2048]{1,0:T(8,128)(2,1)}, bf16[256,2048]{1,0:T(8,128)(2,1)}, u32[]{:S(2)}, u32[]{:S(2)}) collective-permute-start(bf16[256,2048]{1,0:T(8,128)(2,1)} %broadcast_select_fusion.1), channel_id=1, source_target_pairs={{0,4},{4,0},{8,12},{12,8},{16,20},{20,16},{24,28},{28,24},{1,5},{5... | collective-permute-start | bytes 3145736 | tf_op jit(solution)/shard_map/ppermute | solution.py:50
  86.0 14.4 %collective-permute-start.14 = (bf16[192,1024]{1,0:T(8,128)(2,1)}, bf16[192,1024]{1,0:T(8,128)(2,1)S(1)}, u32[]{:S(2)}, u32[]{:S(2)}) collective-permute-start(bf16[192,1024]{1,0:T(8,128)(2,1)} %get-tuple-element.65), channel_id=1, source_target_pairs={{0,8},{4,12},{8,0},{12,4},{16,24},{20,28},{24,16},{28,20},{1,9},{5... | collective-permute-start | bytes 1179656 | tf_op jit(solution)/shard_map/ppermute | solution.py:50
  95.8 12.9 %collective-permute-start.15 = (bf16[192,1024]{1,0:T(8,128)(2,1)}, bf16[192,1024]{1,0:T(8,128)(2,1)}, u32[]{:S(2)}, u32[]{:S(2)}) collective-permute-start(bf16[192,1024]{1,0:T(8,128)(2,1)} %get-tuple-element.81), channel_id=1, source_target_pairs={{0,8},{4,12},{8,0},{12,4},{16,24},{20,28},{24,16},{28,20},{1,9},{5... | collective-permute-start | bytes 1179656 | tf_op jit(solution)/shard_map/ppermute | solution.py:50
  98.3 33.7 %collective-permute-start.18 = (bf16[256,2048]{1,0:T(8,128)(2,1)S(1)}, bf16[256,2048]{1,0:T(8,128)(2,1)S(1)}, u32[]{:S(2)}, u32[]{:S(2)}) collective-permute-start(bf16[256,2048]{1,0:T(8,128)(2,1)S(1)} %broadcast_select_fusion), channel_id=1, source_target_pairs={{0,4},{4,0},{8,12},{12,8},{16,20},{20,16},{24,28},{28,24},{1,5},{5... | collective-permute-start | bytes 3145736 | tf_op jit(solution)/shard_map/ppermute | solution.py:50
  103.1 23.4 %collective-permute-start.20 = (bf16[96,1024]{1,0:T(8,128)(2,1)}, bf16[96,1024]{1,0:T(8,128)(2,1)S(1)}, u32[]{:S(2)}, u32[]{:S(2)}) collective-permute-start(bf16[96,1024]{1,0:T(8,128)(2,1)} %get-tuple-element.84), channel_id=1, source_target_pairs={{0,16},{4,20},{8,24},{12,28},{16,0},{20,4},{24,8},{28,12},{1,17},{... | collective-permute-start | bytes 589832 | tf_op jit(solution)/shard_map/ppermute | solution.py:50
  110.7 15.9 %collective-permute-start.21 = (bf16[96,1024]{1,0:T(8,128)(2,1)}, bf16[96,1024]{1,0:T(8,128)(2,1)S(1)}, u32[]{:S(2)}, u32[]{:S(2)}) collective-permute-start(bf16[96,1024]{1,0:T(8,128)(2,1)} %get-tuple-element.86), channel_id=1, source_target_pairs={{0,16},{4,20},{8,24},{12,28},{16,0},{20,4},{24,8},{28,12},{1,17},{... | collective-permute-start | bytes 589832 | tf_op jit(solution)/shard_map/ppermute | solution.py:50
  125.2 6.7 %collective-permute-start.19 = (f32[16,2,256]{2,1,0:T(2,128)}, f32[16,2,256]{2,1,0:T(2,128)S(1)}, u32[]{:S(2)}, u32[]{:S(2)}) collective-permute-start(f32[16,2,256]{2,1,0:T(2,128)} %get-tuple-element.94), channel_id=1, source_target_pairs={{4,0},{8,4},{12,8},{16,12},{20,16},{24,20},{28,24},{5,1},{9,5},{13... | collective-permute-start | bytes 98312 | tf_op jit(solution)/shard_map/ppermute | solution.py:42
  129.3 9.9 %collective-permute-start.22 = (bf16[48,2048]{1,0:T(8,128)(2,1)}, bf16[48,2048]{1,0:T(8,128)(2,1)S(1)}, u32[]{:S(2)}, u32[]{:S(2)}) collective-permute-start(bf16[48,2048]{1,0:T(8,128)(2,1)} %get-tuple-element.104), channel_id=1, source_target_pairs={{0,4},{4,0},{8,12},{12,8},{16,20},{20,16},{24,28},{28,24},{1,5},{5... | collective-permute-start | bytes 589832 | tf_op jit(solution)/shard_map/ppermute | solution.py:50
  139.3 1.4 collective-permute-start.23
  (14 other events, 92.8 us)
